TPU v7x, 32 devices: a whole 2x2x4 slice. The times are simulated.
32 devices in a mesh: section: 16 (over z, y, core), tensor: 2 (over x).
Axes of the slice: x: 2, y: 2, z: 4, core: 2. Of those that a mesh axis runs over, the one named last changes fastest.
Arguments:
- queries: bfloat16 [2048, 3072], P('section', 'tensor'), may hold values from -6 to 6
- keys: bfloat16 [2048, 3072], P('section', 'tensor'), may hold values from -6 to 6
- values: bfloat16 [2048, 3072], P('section', 'tensor'), may hold values from -6 to 6
- latents: float32 [1024, 128], P('section'), may hold values from -6 to 6
- out_weight: bfloat16 [3072, 3072], P('tensor'), may hold values from -1 to 1
- gain: float32 [3072], P('tensor'), may hold values from 0.1 to 1.9
- head_weight: bfloat16 [3072, 64], P('tensor'), may hold values from -0.109375 to 0.109375
- levels: int32 [8], replicated, may hold values from 0 to 7, each once
- timesteps: int32 [9], replicated, may hold values from 0 to 1000, as said below
- order: int32 [8], replicated, may hold values from 0 to 7, each once
Outputs:
- velocity: float32 [1024, 128], P('section')
- advanced: float32 [1024, 128], P('section')
Inputs may be any that keep to these rules, and one draw needn't show every extreme that they name: timesteps fall strictly from 1000 at index 0 to 0 at index 8.
All inputs are finite; a program needn't handle non-finite values.
Results may differ from a plain program's by a relative error of at most 0.004.
Values may be sent and summed in bfloat16 or wider, within the bound.
No kernel may reach another device: no remote copies, remote signals or barrier semaphores. Data moves between devices by JAX's collectives and lax.ppermute only.
A program may use at most 128 MiB of HBM per device.

v0:
```python
import math

import jax
import jax.numpy as jnp
from jax import lax
from jax.sharding import PartitionSpec as P

D = 3072
HD = 128
GROUPS = 8


def passed_along(value, axis, steps):
    count = lax.axis_size(axis)
    pairs = [(source, (source + steps) % count) for source in range(count)]
    return lax.ppermute(value, axis, pairs)


def local(queries, keys, values, latents, out_weight, gain, head_weight, levels, timesteps, order):
    tok_rows = queries.shape[0]
    tok_width = queries.shape[1]
    heads_here = tok_width // HD
    group_span = lax.axis_size("section") // GROUPS
    group_rows = tok_rows * group_span
    own_group = lax.axis_index("section") // group_span
    group_ids = jnp.arange(GROUPS, dtype=jnp.int32)
    own_order = jnp.sum(jnp.where(group_ids == own_group, order, 0))
    query_heads = queries.reshape(tok_rows, heads_here, HD)
    factor = 1.0 / math.sqrt(HD)
    key_piece = lax.all_gather(keys, "section", axis=0, tiled=True)
    value_piece = lax.all_gather(values, "section", axis=0, tiled=True)
    key_count = key_piece.shape[0]
    key_heads = key_piece.reshape(key_count, heads_here, HD)
    value_heads = value_piece.reshape(key_count, heads_here, HD)
    scores = (
        jnp.einsum("qhd,khd->hqk", query_heads, key_heads, preferred_element_type=jnp.float32)
        * factor
    )
    key_group = jnp.arange(key_count, dtype=jnp.int32) // group_rows
    key_order = jnp.sum(
        jnp.where(key_group[:, None] == group_ids[None, :], order[None, :], 0), axis=1
    )
    visible = (key_order <= own_order)[None, None, :]
    masked = jnp.where(visible, scores, -1e30)
    running = jnp.full((heads_here, tok_rows), -1e30, jnp.float32)
    newest = jnp.maximum(running, jnp.max(masked, axis=2))
    weights = jnp.where(visible, jnp.exp(masked - newest[:, :, None]), 0.0)
    prob_total = jnp.sum(weights, axis=2)
    summed = jnp.einsum(
        "hqk,khd->hqd",
        weights.astype(jnp.bfloat16),
        value_heads,
        preferred_element_type=jnp.float32,
    )
    running, prob_total, summed = (newest, prob_total, summed)
    attended = (
        (summed / prob_total[:, :, None])
        .transpose(1, 0, 2)
        .reshape(tok_rows, tok_width)
        .astype(jnp.bfloat16)
    )
    projected = jnp.dot(attended, out_weight, preferred_element_type=jnp.float32)
    share_cols = gain.shape[0]
    summed_all = lax.psum(projected, "tensor")
    squares = jnp.sum(summed_all * summed_all, axis=1)
    col_share = lax.dynamic_slice_in_dim(
        summed_all, lax.axis_index("tensor") * share_cols, share_cols, 1
    )
    scaled = (col_share * gain[None, :]).astype(jnp.bfloat16)
    head_part = jnp.dot(scaled, head_weight, preferred_element_type=jnp.float32)
    head_raw = lax.psum(head_part, "tensor")
    velocity = head_raw * lax.rsqrt(squares / D + 1e-06)[:, None]
    packed = velocity.reshape(tok_rows // 2, 2 * head_weight.shape[1])
    group_level = jnp.sum(jnp.where(group_ids == own_group, levels, 0))
    step_ids = jnp.arange(timesteps.shape[0], dtype=jnp.int32)
    time_now = jnp.sum(jnp.where(step_ids == group_level, timesteps, 0))
    time_next = jnp.sum(jnp.where(step_ids == group_level + 1, timesteps, 0))
    sigma_step = (time_next - time_now).astype(jnp.float32) / 1000.0
    moved_rows = latents + sigma_step * packed
    advanced = passed_along(moved_rows, "section", group_span)
    return (packed, advanced)


def solution(mesh):
    return jax.shard_map(
        local,
        mesh=mesh,
        in_specs=(
            P("section", "tensor"),
            P("section", "tensor"),
            P("section", "tensor"),
            P("section", None),
            P("tensor", None),
            P("tensor"),
            P("tensor", None),
            P(),
            P(),
            P(),
        ),
        out_specs=(P("section", None), P("section", None)),
        check_vma=False,
    )
```

profile of v0, /device:TPU:0, one launch (start us, length us, event | category | flops | bytes accessed | tf_op | source)
XLA Modules:
  0.0 240.3 jit_solution(15629801854913674679)
XLA Ops:
  7.2 0.0 copy-start
  7.2 0.0 all-gather.3.cloned.1.call-start
  7.2 2.0 copy.21
  9.2 0.0 all-gather.3.cloned.1.call-update
  9.2 0.0 all-gather.5.cloned.1.call-start
  9.3 0.7 all-gather.5.cloned.1.call-update
  10.0 0.0 all-reduce.2.cloned.1.call-start
  10.0 1.2 copy.20
  11.3 1.3 fusion.20
  12.6 0.7 select_reduce_fusion
  13.3 0.7 broadcast_compare_fusion
  14.0 64.6 %all-gather.3.cloned.1.call-done = bf16[2048,1536]{0,1:T(8,128)(2,1)} async-done(((bf16[128,1536]{0,1:T(8,128)(2,1)}), bf16[2048,1536]{0,1:T(8,128)(2,1)}) %all-gather.3.cloned.1.call-update) | async-done | bytes 6291472 | tf_op jit(solution)/shard_map/all_gather | solution.py:30
  78.6 4.6 %fusion = (f32[12,128]{1,0:T(8,128)S(1)}, f32[12,128,2048]{2,1,0:T(8,128)S(1)}) fusion(pred[2048]{0:T(1024)(128)(4,1)S(1)} %broadcast_compare_fusion, bf16[128,12,128]{0,2,1:T(8,128)(2,1)S(1)} %bitcast.19, bf16[2048,12,128]{0,2,1:T(8,128)(2,1)} %bitcast.17), kind=kOutput, calls=%fused_computation.2 | convolution fusion | flops 814742016 | bytes 19275776 | tf_op jit(solution)/shard_map/qhd,khd->hqk/dot_general | solution.py:36
  83.2 0.0 copy-start.1
  83.2 4.6 %copy-done.1 = f32[12,128,2048]{2,1,0:T(8,128)} copy-done((f32[12,128,2048]{2,1,0:T(8,128)}, f32[12,128,2048]{2,1,0:T(8,128)S(1)}, u32[]{:S(2)}) %copy-start.1) | copy-done | bytes 12582936
  87.8 3.3 %fusion.1 = f32[12,128]{1,0:T(8,128)S(1)} fusion(f32[12,128,2048]{2,1,0:T(8,128)S(1)} %get-tuple-element.5, f32[12,128]{1,0:T(8,128)S(1)} %broadcast_maximum_fusion, pred[2048]{0:T(1024)(128)(4,1)S(1)} %broadcast_compare_fusion), kind=kLoop, calls=%fused_computation.3 | loop fusion | flops 15727104 | bytes 12597248 | tf_op jit(solution)/shard_map/reduce_sum | solution.py:48
  91.1 49.8 %all-gather.5.cloned.1.call-done = bf16[2048,1536]{1,0:T(8,128)(2,1)} async-done(((bf16[128,1536]{1,0:T(8,128)(2,1)}), bf16[2048,1536]{1,0:T(8,128)(2,1)}) %all-gather.5.cloned.1.call-update) | async-done | bytes 6291472 | tf_op jit(solution)/shard_map/all_gather | solution.py:31
  140.9 8.7 %copy.24 = bf16[2048,1536]{0,1:T(8,128)(2,1)} copy(bf16[2048,1536]{1,0:T(8,128)(2,1)} %all-gather.5.cloned.1.call-done) | data formatting | bytes 12582912 | tf_op jit(solution)/shard_map/all_gather | solution.py:31
  149.6 9.9 %fusion.12 = bf16[128,12,128]{0,2,1:T(8,128)(2,1)S(1)} fusion(bf16[2048,12,128]{0,2,1:T(8,128)(2,1)} %bitcast.18, f32[12,128,2048]{2,1,0:T(8,128)} %copy-done.1, f32[12,128]{1,0:T(8,128)S(1)} %broadcast_maximum_fusion, pred[2048]{0:T(1024)(128)(4,1)S(1)} %broadcast_compare_fusion, f32[128,12]{0,1:T(8,128)S(1)} %bitcast.21), kind=kOutput, calls=%fused_computation.10 | convolution fusion | flops 821428224 | bytes 19281920 | tf_op jit(solution)/shard_map/hqk,khd->hqd/dot_general | solution.py:49
  159.5 0.0 copy-start.6
  159.5 0.0 copy-start.5
  159.5 0.0 copy-start.4
  159.5 0.0 copy-start.3
  159.6 6.3 %fusion.28 = f32[128,3072]{1,0:T(8,128)} fusion(bf16[128,1536]{0,1:T(8,128)(2,1)S(1)} %bitcast.20, bf16[1536,3072]{1,0:T(8,128)(2,1)} %param.14), kind=kOutput, calls=%fused_computation.40 | convolution fusion | flops 1207959552 | bytes 11403264 | tf_op jit(solution)/shard_map/dot_general | solution.py:62
  165.8 0.0 all-reduce.2.cloned.1.call-update
  165.9 0.0 copy-done.6
  165.9 0.6 fusion.21
  167.2 0.0 copy-done.5
  167.2 1.3 fusion.23
  169.6 46.5 %all-reduce.2.cloned.1.call-done = f32[128,3072]{1,0:T(8,128)} async-done(((f32[128,3072]{1,0:T(8,128)}), f32[128,3072]{1,0:T(8,128)}) %all-reduce.2.cloned.1.call-update) | async-done | bytes 1572880 | tf_op jit(solution)/shard_map/psum | solution.py:64
  216.1 0.0 copy-done
  216.1 0.0 copy-done.4
  216.1 1.4 fusion.15
  217.5 7.2 %psum.15 = f32[128,64]{0,1:T(8,128)S(1)} all-reduce(f32[128,64]{0,1:T(8,128)S(1)} %fusion.15), channel_id=1, replica_groups=mesh['section'=16,'tensor'=2] {'tensor'}, use_global_device_ids=true, to_apply=%region_5.6 | all-reduce | flops 8192 | bytes 65536 | tf_op jit(solution)/shard_map/psum | solution.py:71
  224.7 1.6 multiply_reduce_fusion
  226.3 0.1 copy.25
  226.4 0.1 reshape.48
  226.5 0.0 copy-done.3
  226.5 0.0 copy-start.2
  226.5 1.8 collective-permute-start
  228.3 4.9 %collective-permute-done = f32[64,128]{1,0:T(8,128)S(1)} collective-permute-done((f32[64,128]{1,0:T(8,128)S(1)}, f32[64,128]{1,0:T(8,128)S(1)}, u32[]{:S(2)}, u32[]{:S(2)}) %collective-permute-start) | collective-permute-done | bytes 32800 | tf_op jit(solution)/shard_map/ppermute | solution.py:16
  233.2 0.6 copy.30
  233.8 0.0 copy-done.2
  (5 shorter events, 0.0 us)
Async XLA Ops:
  7.2 208.9 %copy-start = (bf16[1536,64]{0,1:T(8,128)(2,1)S(1)}, bf16[1536,64]{0,1:T(8,128)(2,1)}, u32[]{:S(2)}) copy-start(bf16[1536,64]{0,1:T(8,128)(2,1)} %param.16) | copy-start | bytes 589828
  7.2 71.4 %all-gather.3.cloned.1.call-start = ((), (), s32[]{:S(2)}) async-start(), calls=%async_computation | async-start | bytes 6684672 | tf_op jit(solution)/shard_map/all_gather | solution.py:30
  9.2 131.7 %all-gather.5.cloned.1.call-start = ((), (), s32[]{:S(2)}) async-start(), calls=%async_computation.1 | async-start | bytes 6684672 | tf_op jit(solution)/shard_map/all_gather | solution.py:31
  10.0 206.1 %all-reduce.2.cloned.1.call-start = ((), (), s32[]{:S(2)}) async-start(), calls=%async_computation.2 | async-start | bytes 3145728 | tf_op jit(solution)/shard_map/psum | solution.py:64
  83.2 4.6 %copy-start.1 = (f32[12,128,2048]{2,1,0:T(8,128)}, f32[12,128,2048]{2,1,0:T(8,128)S(1)}, u32[]{:S(2)}) copy-start(f32[12,128,2048]{2,1,0:T(8,128)S(1)} %get-tuple-element.5) | copy-start | bytes 37748740
  159.5 6.4 %copy-start.6 = (s32[8]{0:T(128)S(1)}, s32[8]{0:T(128)}, u32[]{:S(2)}) copy-start(s32[8]{0:T(128)} %param.17) | copy-start | bytes 100
  159.5 7.6 %copy-start.5 = (s32[9]{0:T(128)S(1)}, s32[9]{0:T(128)}, u32[]{:S(2)}) copy-start(s32[9]{0:T(128)} %param.18) | copy-start | bytes 112
  159.5 56.6 %copy-start.4 = (f32[1536]{0:T(1024)S(1)}, f32[1536]{0:T(1024)}, u32[]{:S(2)}) copy-start(f32[1536]{0:T(1024)} %param.15) | copy-start | bytes 18436
  159.5 66.9 %copy-start.3 = (f32[64,128]{1,0:T(8,128)S(1)}, f32[64,128]{1,0:T(8,128)}, u32[]{:S(2)}) copy-start(f32[64,128]{1,0:T(8,128)} %param.13) | copy-start | bytes 98308
  226.5 7.3 %copy-start.2 = (f32[64,128]{1,0:T(8,128)}, f32[64,128]{1,0:T(8,128)S(1)}, u32[]{:S(2)}) copy-start(f32[64,128]{1,0:T(8,128)S(1)} %reshape.48) | copy-start | bytes 98308
  226.5 6.7 %collective-permute-start = (f32[64,128]{1,0:T(8,128)S(1)}, f32[64,128]{1,0:T(8,128)S(1)}, u32[]{:S(2)}, u32[]{:S(2)}) collective-permute-start(f32[64,128]{1,0:T(8,128)S(1)} %multiply_add_fusion), channel_id=1, source_target_pairs={{0,4},{2,6},{4,8},{6,10},{8,12},{10,14},{12,16},{14,18},{16,20},{1... | collective-permute-start | bytes 98312 | tf_op jit(solution)/shard_map/ppermute | solution.py:16
Sparse Core Ops, SparseCore 0:
  10.2 68.3 all-gather.2
  80.8 60.0 all-gather.4
  166.0 50.0 all-reduce.1
where the time goes:
time: 241 us; the launch traced here: 240 us
  waiting for transfers between devices  167 us (69%)
  matrix products  22.2 us (9%)
  local copies, waits for them, and re-layouts  17.3 us (7%)
  between operations  15.8 us (7%)
  other arithmetic  9.51 us (4%)
  blocking collectives  7.18 us (3%)
    all_gather x1, waiting for transfers between devices, local(): key_piece = lax.all_gather(keys, 'section', axis=0, tiled=True)  64.6 us
    all_gather x1, waiting for transfers between devices, local(): value_piece = lax.all_gather(values, 'section', axis=0, tiled=True)  49.8 us
    psum x1, waiting for transfers between devices, local(): summed_all = lax.psum(projected, 'tensor')  46.5 us
    dot_general x1, matrix products, local(): jnp.einsum('hqk,khd->hqd', weights.astype(jnp.bfloat16), value_heads, pre...  9.9 us
    all_gather x1, local copies, waits for them, and re-layouts, local(): value_piece = lax.all_gather(values, 'section', axis=0, tiled=True)  8.7 us
    unnamed x17, local copies, waits for them, and re-layouts  8.4 us
    psum x1, blocking collectives, local(): head_raw = lax.psum(head_part, 'tensor')  7.18 us
    dot_general x1, matrix products, local(): jnp.dot(attended, out_weight, preferred_element_type=jnp.float32)  6.28 us
  transfers between devices with their start and end apart: 4, of which 4 were waited for; matrix products, arithmetic and copies ran while one was open for 6% of the time, Pallas kernels for 0%

commit v1 on v0

v1 whole, which is shorter than its diff:
```python
import functools
import math

import jax
import jax.numpy as jnp
from jax import lax
from jax.experimental import pallas as pl
from jax.experimental.pallas import tpu as pltpu
from jax.sharding import PartitionSpec as P

HD = 128
GROUPS = 8
MAX_HEAD_SPLIT = 4
NEG = -1e30
VMEM = pl.BlockSpec(memory_space=pltpu.VMEM)
SMEM = pl.BlockSpec(memory_space=pltpu.SMEM)


def params(mib):
    return pltpu.CompilerParams(vmem_limit_bytes=mib * 1024 * 1024)


def struct(shape, dtype):
    return jax.ShapeDtypeStruct(shape, dtype)


class Plan:
    def __init__(self, queries):
        self.sections = lax.axis_size("section")
        self.tensors = lax.axis_size("tensor")
        self.rows, self.width = queries.shape
        self.heads = self.width // HD
        self.split = math.gcd(self.heads, MAX_HEAD_SPLIT)
        self.members = self.sections // self.split
        self.cols = self.width // self.split
        self.span = self.sections // GROUPS
        self.share = self.rows // self.tensors

    def part(self):
        return lax.axis_index("section") // self.members

    def to_part(self, value, step):
        pairs = [(s, s ^ (step * self.members)) for s in range(self.sections)]
        return lax.ppermute(value, "section", pairs)

    def to_member(self, value, step):
        return lax.ppermute(value, "section", [(s, s ^ step) for s in range(self.sections)])

    def to_tensor(self, value, step):
        return lax.ppermute(value, "tensor", [(t, t ^ step) for t in range(self.tensors)])

    def to_next_group(self, value, step):
        pairs = [
            (s * self.tensors + t, ((s + self.span) % self.sections) * self.tensors + (t ^ step))
            for s in range(self.sections)
            for t in range(self.tensors)
        ]
        return lax.ppermute(value, ("section", "tensor"), pairs)

    def gather_members(self, piece):
        pieces = {0: piece}
        step = self.members // 2
        while step:
            pieces.update({i ^ step: self.to_member(v, step) for i, v in list(pieces.items())})
            step //= 2
        return [pieces[i] for i in range(self.members)]


def pack_kernel(plan, arrays, *refs):
    sources, targets = refs[:arrays], refs[arrays:]
    part = plan.part()
    for step, target in enumerate(targets):
        here = pl.ds(pl.multiple_of((part ^ step) * plan.cols, 128), plan.cols)
        for i, source in enumerate(sources):
            target[pl.ds(i * plan.rows, plan.rows), :] = source[:, here]


def pack(plan, *arrays):
    return pl.pallas_call(
        functools.partial(pack_kernel, plan, len(arrays)),
        out_shape=[struct((len(arrays) * plan.rows, plan.cols), jnp.bfloat16)] * plan.split,
        in_specs=[VMEM] * len(arrays),
        out_specs=[VMEM] * plan.split,
        compiler_params=params(32),
    )(*arrays)


def attend_kernel(plan, steps, order_ref, *refs):
    rows = plan.rows
    queries, refs = refs[: len(steps)], refs[len(steps) :]
    count = plan.split * plan.members
    pieces, refs = refs[:count], refs[count:]
    outs, scores = refs[: len(steps)], refs[len(steps)]
    me = lax.axis_index("section")
    factor = 1.0 / math.sqrt(HD)
    many = len(steps) * rows
    width = 2 * rows if plan.span % 2 == 0 and plan.members % 2 == 0 else rows
    per = width // rows
    blocks = [pieces[i : i + per] for i in range(0, count, per)]

    def order_of(step, member):
        return order_ref[(me ^ (step * plan.members + member)) // plan.span]

    own = [order_of(step, 0) for step in steps]
    for h in range(plan.cols // HD):
        lanes = pl.ds(h * HD, HD)
        q = jnp.concatenate([ref[:, lanes] for ref in queries], axis=0)
        top = None
        for j, block in enumerate(blocks):
            k = jnp.concatenate([ref[pl.ds(0, rows), lanes] for ref in block], axis=0)
            s = lax.dot_general(q, k, (((1,), (1,)), ((), ())), preferred_element_type=jnp.float32)
            first = j * per
            key_order = order_of(first // plan.members, first % plan.members)
            s = jnp.concatenate(
                [
                    s[i * rows : (i + 1) * rows] * factor + jnp.where(key_order <= o, 0.0, NEG)
                    for i, o in enumerate(own)
                ],
                axis=0,
            )
            scores[:, pl.ds(j * width, width)] = s
            top = s if top is None else jnp.maximum(top, s)
        top = jnp.max(top, axis=1, keepdims=True)
        total = jnp.zeros((many, width), jnp.float32)
        summed = jnp.zeros((many, HD), jnp.float32)
        for j, block in enumerate(blocks):
            v = jnp.concatenate([ref[pl.ds(rows, rows), lanes] for ref in block], axis=0)
            w = jnp.exp(scores[:, pl.ds(j * width, width)] - top)
            total += w
            summed += jnp.dot(w.astype(jnp.bfloat16), v, preferred_element_type=jnp.float32)
        out = (summed / jnp.sum(total, axis=1, keepdims=True)).astype(jnp.bfloat16)
        for i, ref in enumerate(outs):
            ref[:, lanes] = out[i * rows : (i + 1) * rows]


def attend(plan, steps, order, queries, pieces):
    return pl.pallas_call(
        functools.partial(attend_kernel, plan, steps),
        out_shape=[struct((plan.rows, plan.cols), jnp.bfloat16)] * len(steps),
        in_specs=[SMEM] + [VMEM] * (len(steps) + len(pieces)),
        out_specs=[VMEM] * len(steps),
        scratch_shapes=[pltpu.VMEM((len(steps) * plan.rows, len(pieces) * plan.rows), jnp.float32)],
        compiler_params=params(48),
        cost_estimate=pl.CostEstimate(
            flops=4 * len(steps) * plan.rows * len(pieces) * plan.rows * plan.cols,
            bytes_accessed=4 * len(pieces) * plan.rows * plan.cols,
            transcendentals=len(steps) * plan.rows * len(pieces) * plan.rows * plan.cols // HD,
        ),
    )(order, *queries, *pieces)


def project_kernel(plan, *refs):
    parts, weight = refs[: plan.split], refs[plan.split]
    outs = refs[plan.split + 1 :]
    part, tensor = plan.part(), lax.axis_index("tensor")
    total = None
    for step, ref in enumerate(parts):
        here = pl.ds(pl.multiple_of((part ^ step) * plan.cols, 128), plan.cols)
        term = jnp.dot(ref[...], weight[here, :], preferred_element_type=jnp.float32)
        total = term if total is None else total + term
    full = refs[-1]
    full[...] = total
    for step, out in enumerate(outs[:-1]):
        here = pl.ds(pl.multiple_of((tensor ^ step) * plan.share, 8), plan.share)
        out[...] = full[here, :].astype(out.dtype)


def project(plan, parts, weight):
    width = weight.shape[1]
    tile = 512
    shapes = [struct((plan.share, width), jnp.float32)]
    shapes += [struct((plan.share, width), jnp.bfloat16)] * (plan.tensors - 1)
    return pl.pallas_call(
        functools.partial(project_kernel, plan),
        grid=(width // tile,),
        out_shape=shapes,
        in_specs=[pl.BlockSpec((plan.rows, plan.cols), lambda i: (0, 0))] * plan.split
        + [pl.BlockSpec((weight.shape[0], tile), lambda i: (0, i))],
        out_specs=[pl.BlockSpec((plan.share, tile), lambda i: (0, i))] * plan.tensors,
        scratch_shapes=[pltpu.VMEM((plan.rows, tile), jnp.float32)],
        compiler_params=params(32),
    )(*parts, weight)


def head_kernel(plan, levels, timesteps, *refs):
    sums, refs = refs[: plan.tensors], refs[plan.tensors :]
    gains, refs = refs[: plan.tensors], refs[plan.tensors :]
    heads, refs = refs[: plan.tensors], refs[plan.tensors :]
    latents, velocity_ref, moved_ref, full, rows = refs
    tensor = lax.axis_index("tensor")
    total = sums[0][...]
    for ref in sums[1:]:
        total = total + ref[...].astype(jnp.float32)
    full[...] = total
    squares = jnp.sum(total * total, axis=1, keepdims=True)
    raw = None
    for step in range(plan.tensors):
        share = gains[step].shape[1]
        here = pl.ds(pl.multiple_of((tensor ^ step) * share, 128), share)
        scaled = (full[:, here] * gains[step][...]).astype(jnp.bfloat16)
        term = jnp.dot(scaled, heads[step][...], preferred_element_type=jnp.float32)
        raw = term if raw is None else raw + term
    rows[...] = raw * lax.rsqrt(squares / total.shape[1] + 1e-6)
    half = plan.share // 2
    velocity = jnp.concatenate(
        [rows[pl.ds(0, half, 2), :], rows[pl.ds(1, half, 2), :]], axis=1
    )
    level = levels[lax.axis_index("section") // plan.span]
    change = (timesteps[level + 1] - timesteps[level]).astype(jnp.float32)
    delta = jnp.full(velocity.shape, change, jnp.float32) / 1000.0
    velocity_ref[...] = velocity
    here = pl.ds(pl.multiple_of(tensor * half, 8), half)
    moved_ref[...] = latents[here, :] + delta * velocity


def head(plan, levels, timesteps, sums, gains, heads, latents):
    half = struct((plan.share // 2, latents.shape[1]), jnp.float32)
    return pl.pallas_call(
        functools.partial(head_kernel, plan),
        out_shape=[half, half],
        in_specs=[SMEM, SMEM] + [VMEM] * (3 * plan.tensors + 1),
        out_specs=[VMEM, VMEM],
        scratch_shapes=[
            pltpu.VMEM(sums[0].shape, jnp.float32),
            pltpu.VMEM((plan.share, heads[0].shape[1]), jnp.float32),
        ],
        compiler_params=params(32),
    )(levels, timesteps, *sums, *gains, *heads, latents)


def place_kernel(plan, *refs):
    velocities, moved = refs[: plan.tensors], refs[plan.tensors : 2 * plan.tensors]
    tensor = lax.axis_index("tensor")
    for parts, out in ((velocities, refs[-2]), (moved, refs[-1])):
        for step, ref in enumerate(parts):
            rows = ref.shape[0]
            out[pl.ds(pl.multiple_of((tensor ^ step) * rows, 8), rows), :] = ref[...]


def place(plan, velocities, moved):
    shape = struct((plan.rows // 2, velocities[0].shape[1]), jnp.float32)
    return pl.pallas_call(
        functools.partial(place_kernel, plan),
        out_shape=[shape, shape],
        in_specs=[VMEM] * (2 * plan.tensors),
        out_specs=[VMEM, VMEM],
    )(*velocities, *moved)


def local(queries, keys, values, latents, out_weight, gain, head_weight, levels, timesteps, order):
    plan = Plan(queries)
    split, tensors = plan.split, plan.tensors

    sent = pack(plan, keys, values)
    key_values = [sent[0]] + [plan.to_part(sent[i], i) for i in range(1, split)]
    sent = pack(plan, queries)
    asked = [sent[0]] + [plan.to_part(sent[i], i) for i in range(1, split)]
    gains = [gain[None, :]]
    heads = [head_weight]
    gains += [plan.to_tensor(gains[0], i) for i in range(1, tensors)]
    heads += [plan.to_tensor(heads[0], i) for i in range(1, tensors)]
    pieces = [p for piece in key_values for p in plan.gather_members(piece)]

    far = list(range(split // 2, split))
    near = list(range(split // 2))
    attended = [None] * split
    for steps in (far, near):
        if steps:
            outs = attend(plan, steps, order, [asked[i] for i in steps], pieces)
            for i, out in zip(steps, outs):
                attended[i] = plan.to_part(out, i) if i else out

    sums = project(plan, attended, out_weight)
    sums = [sums[0]] + [plan.to_tensor(sums[i], i) for i in range(1, tensors)]
    velocity, moved = head(plan, levels, timesteps, sums, gains, heads, latents)
    velocities = [velocity] + [plan.to_tensor(velocity, i) for i in range(1, tensors)]
    advanced = [plan.to_next_group(moved, i) for i in range(tensors)]
    return tuple(place(plan, velocities, advanced))


def solution(mesh):
    return jax.shard_map(
        local,
        mesh=mesh,
        in_specs=(
            P("section", "tensor"),
            P("section", "tensor"),
            P("section", "tensor"),
            P("section", None),
            P("tensor", None),
            P("tensor"),
            P("tensor", None),
            P(),
            P(),
            P(),
        ),
        out_specs=(P("section", None), P("section", None)),
        check_vma=False,
    )
```

time: 241 us -> 102 us (0.42)
  waiting for transfers between devices: 167 us -> 48.8 us
  starting transfers between devices: 1.88 us -> 29.8 us
  matrix products: 22.2 us -> 0 us
  between operations: 15.8 us -> 0.79 us
  Pallas kernels: 0 us -> 13 us
  other arithmetic: 9.51 us -> 0 us
  local copies, waits for them, and re-layouts: 17.3 us -> 8.81 us
  blocking collectives: 7.18 us -> 0 us
    all_gather x2 -> x0, waiting for transfers between devices: 114 us -> none  [the longest x1 64.6 us: local(): key_piece = lax.all_gather(keys, 'section', axis=0, tiled=True)]
    psum x1 -> x0, waiting for transfers between devices: 46.5 us -> none  [local(): summed_all = lax.psum(projected, 'tensor')]
    ppermute x1 -> x27, waiting for transfers between devices: 4.9 us -> 48.8 us  [the longest x9 18.2 us: to_part(): return lax.ppermute(value, 'section', pairs)]
    ppermute x1 -> x27, starting transfers between devices: 1.77 us -> 29.8 us  [the longest x9 15.4 us: to_part(): return lax.ppermute(value, 'section', pairs)]
    dot_general x4 -> x0, matrix products: 22.2 us -> none  [the longest x1 9.9 us: local(): jnp.einsum('hqk,khd->hqd', weights.astype(jnp.bfloat16), value_heads, pre...]
    pallas_call x0 -> x7, Pallas kernels: none -> 13 us  [the longest x2 6.85 us: attend(): pl.pallas_call(functools.partial(attend_kernel, plan, steps), out_shape=[...]
    reduce_sum x6 -> x0, other arithmetic: 8.83 us -> none  [the longest x1 3.28 us: local(): prob_total = jnp.sum(weights, axis=2)]
    all_gather x1 -> x0, local copies, waits for them, and re-layouts: 8.7 us -> none  [local(): value_piece = lax.all_gather(values, 'section', axis=0, tiled=True)]
  transfers between devices with their start and end apart: 4 -> 27, of which waited for: 4 -> 10; matrix products, arithmetic and copies ran while one was open for 6% -> 0% of each run, Pallas kernels for 0% -> 7%
where the time goes in v1:
time: 102 us; the launch traced here: 101 us
  waiting for transfers between devices  48.8 us (48%)
  starting transfers between devices  29.8 us (29%)
  Pallas kernels  13 us (13%)
  local copies, waits for them, and re-layouts  8.81 us (9%)
    ppermute x9, waiting for transfers between devices, to_part(): return lax.ppermute(value, 'section', pairs)  18.2 us
    ppermute x9, starting transfers between devices, to_part(): return lax.ppermute(value, 'section', pairs)  15.4 us
    ppermute x4, waiting for transfers between devices, to_tensor(): lax.ppermute(value, 'tensor', [(t, t ^ step) for t in range(self.tensors)])  14.9 us
    ppermute x12, waiting for transfers between devices, to_member(): lax.ppermute(value, 'section', [(s, s ^ step) for s in range(self.section...  9.42 us
    unnamed x31, local copies, waits for them, and re-layouts  8.81 us
    pallas_call x2, Pallas kernels, attend(): pl.pallas_call(functools.partial(attend_kernel, plan, steps), out_shape=[...  6.85 us
    ppermute x12, starting transfers between devices, to_member(): lax.ppermute(value, 'section', [(s, s ^ step) for s in range(self.section...  6.58 us
    ppermute x2, waiting for transfers between devices, to_next_group(): return lax.ppermute(value, ('section', 'tensor'), pairs)  6.24 us
  transfers between devices with their start and end apart: 27, of which 10 were waited for; matrix products, arithmetic and copies ran while one was open for 0% of the time, Pallas kernels for 7%

profile of v1, /device:TPU:0, one launch (start us, length us, event | category | flops | bytes accessed | tf_op | source)
XLA Modules:
  0.0 101.2 jit_solution(5069267851040868068)
XLA Ops:
  0.6 1.0 copy-done.1
  1.6 0.1 shard_map.113
  1.7 4.1 %collective-permute-start.17 = (bf16[128,384]{1,0:T(8,128)(2,1)S(1)}, bf16[128,384]{1,0:T(8,128)(2,1)S(1)}, u32[]{:S(2)}, u32[]{:S(2)}) collective-permute-start(bf16[128,384]{1,0:T(8,128)(2,1)S(1)} %get-tuple-element.26), channel_id=1, source_target_pairs={{0,16},{2,18},{4,20},{6,22},{8,24},{10,26},{12,28},{14,30},{16,0},... | collective-permute-start | bytes 294920 | tf_op jit(solution)/shard_map/ppermute | solution.py:44
  5.8 1.3 %collective-permute-start.18 = (bf16[128,384]{1,0:T(8,128)(2,1)S(1)}, bf16[128,384]{1,0:T(8,128)(2,1)S(1)}, u32[]{:S(2)}, u32[]{:S(2)}) collective-permute-start(bf16[128,384]{1,0:T(8,128)(2,1)S(1)} %get-tuple-element.27), channel_id=1, source_target_pairs={{0,24},{2,26},{4,28},{6,30},{8,16},{10,18},{12,20},{14,22},{16,8},... | collective-permute-start | bytes 294920 | tf_op jit(solution)/shard_map/ppermute | solution.py:44
  7.2 1.0 copy-done.2
  8.2 1.0 copy-done.3
  9.2 0.1 shard_map.114
  9.2 1.8 %collective-permute-start.8 = (bf16[256,384]{1,0:T(8,128)(2,1)S(1)}, bf16[256,384]{1,0:T(8,128)(2,1)S(1)}, u32[]{:S(2)}, u32[]{:S(2)}) collective-permute-start(bf16[256,384]{1,0:T(8,128)(2,1)S(1)} %get-tuple-element.22), channel_id=1, source_target_pairs={{0,16},{2,18},{4,20},{6,22},{8,24},{10,26},{12,28},{14,30},{16,0},... | collective-permute-start | bytes 589832 | tf_op jit(solution)/shard_map/ppermute | solution.py:44
  11.0 0.9 collective-permute-start.12
  11.9 0.9 collective-permute-start.4
  12.8 9.3 %collective-permute-done.17.refs_0_ = bf16[128,384]{1,0:T(8,128)(2,1)S(1)} collective-permute-done((bf16[128,384]{1,0:T(8,128)(2,1)S(1)}, bf16[128,384]{1,0:T(8,128)(2,1)S(1)}, u32[]{:S(2)}, u32[]{:S(2)}) %collective-permute-start.17) | collective-permute-done | bytes 98336 | tf_op jit(solution)/shard_map/ppermute | solution.py:44
  22.1 1.7 %collective-permute-start.2 = (bf16[256,384]{1,0:T(8,128)(2,1)S(1)}, bf16[256,384]{1,0:T(8,128)(2,1)S(1)}, u32[]{:S(2)}, u32[]{:S(2)}) collective-permute-start(bf16[256,384]{1,0:T(8,128)(2,1)S(1)} %get-tuple-element.20.refs_2_), channel_id=1, source_target_pairs={{0,4},{2,6},{4,0},{6,2},{8,12},{10,14},{12,8},{14,10},{16,20},{18,... | collective-permute-start | bytes 589832 | tf_op jit(solution)/shard_map/ppermute | solution.py:47
  23.9 0.0 collective-permute-done.18.refs_1_
  23.9 0.0 collective-permute-start.1
  23.9 4.6 %collective-permute-done.8.refs_10_ = bf16[256,384]{1,0:T(8,128)(2,1)S(1)} collective-permute-done((bf16[256,384]{1,0:T(8,128)(2,1)S(1)}, bf16[256,384]{1,0:T(8,128)(2,1)S(1)}, u32[]{:S(2)}, u32[]{:S(2)}) %collective-permute-start.8) | collective-permute-done | bytes 196640 | tf_op jit(solution)/shard_map/ppermute | solution.py:44
  28.4 1.7 %collective-permute-start.10 = (bf16[256,384]{1,0:T(8,128)(2,1)S(1)}, bf16[256,384]{1,0:T(8,128)(2,1)S(1)}, u32[]{:S(2)}, u32[]{:S(2)}) collective-permute-start(bf16[256,384]{1,0:T(8,128)(2,1)S(1)} %collective-permute-done.8.refs_10_), channel_id=1, source_target_pairs={{0,4},{2,6},{4,0},{6,2},{8,12},{10,14},{12,8},{14,10},{16,20},{18,... | collective-permute-start | bytes 589832 | tf_op jit(solution)/shard_map/ppermute | solution.py:47
  30.2 0.0 collective-permute-done.12.refs_14_
  30.2 0.3 collective-permute-start.14
  30.5 0.0 collective-permute-done.4.refs_6_
  30.5 1.7 %collective-permute-start.6 = (bf16[256,384]{1,0:T(8,128)(2,1)S(1)}, bf16[256,384]{1,0:T(8,128)(2,1)S(1)}, u32[]{:S(2)}, u32[]{:S(2)}) collective-permute-start(bf16[256,384]{1,0:T(8,128)(2,1)S(1)} %collective-permute-done.4.refs_6_), channel_id=1, source_target_pairs={{0,4},{2,6},{4,0},{6,2},{8,12},{10,14},{12,8},{14,10},{16,20},{18,... | collective-permute-start | bytes 589832 | tf_op jit(solution)/shard_map/ppermute | solution.py:47
  32.2 0.0 collective-permute-done.2.refs_4_
  32.2 0.0 collective-permute-start.3
  32.2 0.0 collective-permute-done.1.refs_3_
  32.2 0.5 collective-permute-start.13
  32.7 3.6 %collective-permute-done.10.refs_12_ = bf16[256,384]{1,0:T(8,128)(2,1)S(1)} collective-permute-done((bf16[256,384]{1,0:T(8,128)(2,1)S(1)}, bf16[256,384]{1,0:T(8,128)(2,1)S(1)}, u32[]{:S(2)}, u32[]{:S(2)}) %collective-permute-start.10) | collective-permute-done | bytes 196640 | tf_op jit(solution)/shard_map/ppermute | solution.py:47
  36.3 0.0 collective-permute-start.5
  36.3 3.7 %collective-permute-done.14.refs_16_ = bf16[256,384]{1,0:T(8,128)(2,1)S(1)} collective-permute-done((bf16[256,384]{1,0:T(8,128)(2,1)S(1)}, bf16[256,384]{1,0:T(8,128)(2,1)S(1)}, u32[]{:S(2)}, u32[]{:S(2)}) %collective-permute-start.14) | collective-permute-done | bytes 196640 | tf_op jit(solution)/shard_map/ppermute | solution.py:47
  40.0 0.0 collective-permute-start.9
  40.0 2.1 %collective-permute-done.6.refs_8_ = bf16[256,384]{1,0:T(8,128)(2,1)S(1)} collective-permute-done((bf16[256,384]{1,0:T(8,128)(2,1)S(1)}, bf16[256,384]{1,0:T(8,128)(2,1)S(1)}, u32[]{:S(2)}, u32[]{:S(2)}) %collective-permute-start.6) | collective-permute-done | bytes 196640 | tf_op jit(solution)/shard_map/ppermute | solution.py:47
  42.1 0.0 collective-permute-start.11
  42.1 0.5 collective-permute-start.15
  42.6 0.1 collective-permute-start.7
  42.7 0.0 collective-permute-done.5.refs_7_
  42.7 1.5 %collective-permute-start = (bf16[128,384]{1,0:T(8,128)(2,1)S(1)}, bf16[128,384]{1,0:T(8,128)(2,1)S(1)}, u32[]{:S(2)}, u32[]{:S(2)}) collective-permute-start(bf16[128,384]{1,0:T(8,128)(2,1)S(1)} %get-tuple-element.19), channel_id=1, source_target_pairs={{0,8},{2,10},{4,12},{6,14},{8,0},{10,2},{12,4},{14,6},{16,24},{18,... | collective-permute-start | bytes 294920 | tf_op jit(solution)/shard_map/ppermute | solution.py:44
  44.2 0.0 collective-permute-done.11.refs_13_
  44.2 0.0 collective-permute-done.15.refs_17_
  44.2 0.0 copy-start.6
  44.2 0.6 copy-done.6
  44.9 3.4 %shard_map.116 = (bf16[128,384]{1,0:T(8,128)(2,1)S(1)}, bf16[128,384]{1,0:T(8,128)(2,1)S(1)}) custom-call(s32[8]{0:T(128)S(1)} %copy-done.6, bf16[128,384]{1,0:T(8,128)(2,1)S(1)} %collective-permute-done.17.refs_0_, bf16[128,384]{1,0:T(8,128)(2,1)S(1)} %collective-permute-done.18.refs_1_, bf16[256,384]{1,0:T(8,128)(2,1)S(1)} %get-tuple-element.20.refs_2_, ...), custom_call_target="tpu_custom_call" | custom-call | flops 805306368 | bytes 3145728 | tf_op jit(solution)/shard_map/pallas_call | solution.py:137
  48.3 3.4 %collective-permute-start.19 = (bf16[128,384]{1,0:T(8,128)(2,1)S(1)}, bf16[128,384]{1,0:T(8,128)(2,1)S(1)}, u32[]{:S(2)}, u32[]{:S(2)}) collective-permute-start(bf16[128,384]{1,0:T(8,128)(2,1)S(1)} %get-tuple-element.28), channel_id=1, source_target_pairs={{0,16},{2,18},{4,20},{6,22},{8,24},{10,26},{12,28},{14,30},{16,0},... | collective-permute-start | bytes 294920 | tf_op jit(solution)/shard_map/ppermute | solution.py:44
  51.7 0.9 collective-permute-start.20
  52.6 0.0 collective-permute-done.refs_1_
  52.6 0.7 copy-done.7
  53.3 3.4 %shard_map.115 = (bf16[128,384]{1,0:T(8,128)(2,1)S(1)}, bf16[128,384]{1,0:T(8,128)(2,1)S(1)}) custom-call(s32[8]{0:T(128)S(1)} %copy-done.7, bf16[128,384]{1,0:T(8,128)(2,1)S(1)} %get-tuple-element.18.refs_0_, bf16[128,384]{1,0:T(8,128)(2,1)S(1)} %collective-permute-done.refs_1_, bf16[256,384]{1,0:T(8,128)(2,1)S(1)} %get-tuple-element.20.refs_2_, ...), custom_call_target="tpu_custom_call" | custom-call | flops 805306368 | bytes 3145728 | tf_op jit(solution)/shard_map/pallas_call | solution.py:137
  56.7 0.6 collective-permute-start.16
  57.3 2.2 %collective-permute-done.19.refs_2_ = bf16[128,384]{1,0:T(8,128)(2,1)S(1)} collective-permute-done((bf16[128,384]{1,0:T(8,128)(2,1)S(1)}, bf16[128,384]{1,0:T(8,128)(2,1)S(1)}, u32[]{:S(2)}, u32[]{:S(2)}) %collective-permute-start.19) | collective-permute-done | bytes 98336 | tf_op jit(solution)/shard_map/ppermute | solution.py:44
  59.5 2.0 %collective-permute-done.16.refs_1_ = bf16[128,384]{1,0:T(8,128)(2,1)S(1)} collective-permute-done((bf16[128,384]{1,0:T(8,128)(2,1)S(1)}, bf16[128,384]{1,0:T(8,128)(2,1)S(1)}, u32[]{:S(2)}, u32[]{:S(2)}) %collective-permute-start.16) | collective-permute-done | bytes 98336 | tf_op jit(solution)/shard_map/ppermute | solution.py:44
  61.5 3.7 %copy-done = bf16[1536,3072]{1,0:T(8,128)(2,1)S(1)} copy-done((bf16[1536,3072]{1,0:T(8,128)(2,1)S(1)}, bf16[1536,3072]{1,0:T(8,128)(2,1)}, u32[]{:S(2)}) %copy-start) | copy-done | bytes 9437208
  65.2 3.7 %shard_map.117 = (f32[64,3072]{1,0:T(8,128)S(1)}, bf16[64,3072]{1,0:T(8,128)(2,1)S(1)}) custom-call(bf16[128,384]{1,0:T(8,128)(2,1)S(1)} %get-tuple-element.24.refs_0_, bf16[128,384]{1,0:T(8,128)(2,1)S(1)} %collective-permute-done.16.refs_1_, bf16[128,384]{1,0:T(8,128)(2,1)S(1)} %collective-permute-done.19.refs_2_, ...), custom_call_target="tpu_custom_call" | custom-call | tf_op jit(solution)/shard_map/pallas_call | solution.py:173
  68.9 1.5 %collective-permute-start.21 = (bf16[64,3072]{1,0:T(8,128)(2,1)S(1)}, bf16[64,3072]{1,0:T(8,128)(2,1)S(1)}, u32[]{:S(2)}, u32[]{:S(2)}) collective-permute-start(bf16[64,3072]{1,0:T(8,128)(2,1)S(1)} %get-tuple-element.31), channel_id=1, source_target_pairs={{0,1},{1,0},{2,3},{3,2},{4,5},{5,4},{6,7},{7,6},{8,9},{9,8},{10,11... | collective-permute-start | bytes 1179656 | tf_op jit(solution)/shard_map/ppermute | solution.py:50
  70.4 0.2 copy.13.refs_4_
  70.7 0.6 collective-permute-start.23
  71.3 1.5 %collective-permute-start.22 = (f32[1,1536]{1,0:T(1,128)S(1)}, f32[1,1536]{1,0:T(1,128)S(1)}, u32[]{:S(2)}, u32[]{:S(2)}) collective-permute-start(f32[1,1536]{1,0:T(1,128)S(1)} %broadcast_in_dim.3.refs_2_), channel_id=1, source_target_pairs={{0,1},{1,0},{2,3},{3,2},{4,5},{5,4},{6,7},{7,6},{8,9},{9,8},{10,11... | collective-permute-start | bytes 18440 | tf_op jit(solution)/shard_map/ppermute | solution.py:50
  72.8 14.9 %collective-permute-done.22.refs_3_ = f32[1,1536]{1,0:T(1,128)S(1)} collective-permute-done((f32[1,1536]{1,0:T(1,128)S(1)}, f32[1,1536]{1,0:T(1,128)S(1)}, u32[]{:S(2)}, u32[]{:S(2)}) %collective-permute-start.22) | collective-permute-done | bytes 6176 | tf_op jit(solution)/shard_map/ppermute | solution.py:50
  87.7 0.0 collective-permute-done.23.refs_5_
  87.7 0.0 collective-permute-done.21.refs_1_
  87.8 1.0 shard_map.118
  88.8 1.5 %collective-permute-start.24 = (f32[32,128]{1,0:T(8,128)S(1)}, f32[32,128]{1,0:T(8,128)S(1)}, u32[]{:S(2)}, u32[]{:S(2)}) collective-permute-start(f32[32,128]{1,0:T(8,128)S(1)} %get-tuple-element.32.refs_0_), channel_id=1, source_target_pairs={{0,1},{1,0},{2,3},{3,2},{4,5},{5,4},{6,7},{7,6},{8,9},{9,8},{10,11... | collective-permute-start | bytes 49160 | tf_op jit(solution)/shard_map/ppermute | solution.py:50
  90.3 1.5 %collective-permute-start.25 = (f32[32,128]{1,0:T(8,128)S(1)}, f32[32,128]{1,0:T(8,128)S(1)}, u32[]{:S(2)}, u32[]{:S(2)}) collective-permute-start(f32[32,128]{1,0:T(8,128)S(1)} %get-tuple-element.33), channel_id=1, source_target_pairs={{0,4},{1,5},{2,6},{3,7},{4,8},{5,9},{6,10},{7,11},{8,12},{9,13},{1... | collective-permute-start | bytes 49160 | tf_op jit(solution)/shard_map/ppermute | solution.py:58
  91.8 1.1 %collective-permute-start.26 = (f32[32,128]{1,0:T(8,128)S(1)}, f32[32,128]{1,0:T(8,128)S(1)}, u32[]{:S(2)}, u32[]{:S(2)}) collective-permute-start(f32[32,128]{1,0:T(8,128)S(1)} %get-tuple-element.33), channel_id=1, source_target_pairs={{0,5},{1,4},{2,7},{3,6},{4,9},{5,8},{6,11},{7,10},{8,13},{9,12},{1... | collective-permute-start | bytes 49160 | tf_op jit(solution)/shard_map/ppermute | solution.py:58
  92.9 3.8 %collective-permute-done.25.refs_2_ = f32[32,128]{1,0:T(8,128)S(1)} collective-permute-done((f32[32,128]{1,0:T(8,128)S(1)}, f32[32,128]{1,0:T(8,128)S(1)}, u32[]{:S(2)}, u32[]{:S(2)}) %collective-permute-start.25) | collective-permute-done | bytes 16416 | tf_op jit(solution)/shard_map/ppermute | solution.py:58
  96.7 2.4 %collective-permute-done.26.refs_3_ = f32[32,128]{1,0:T(8,128)S(1)} collective-permute-done((f32[32,128]{1,0:T(8,128)S(1)}, f32[32,128]{1,0:T(8,128)S(1)}, u32[]{:S(2)}, u32[]{:S(2)}) %collective-permute-start.26) | collective-permute-done | bytes 16416 | tf_op jit(solution)/shard_map/ppermute | solution.py:58
  99.2 0.6 copy-done.13
  99.8 1.4 %shard_map.119 = (f32[64,128]{1,0:T(8,128)}, f32[64,128]{1,0:T(8,128)}) custom-call(f32[32,128]{1,0:T(8,128)} %copy-done.5, f32[32,128]{1,0:T(8,128)} %copy-done.11, f32[32,128]{1,0:T(8,128)} %copy-done.12, f32[32,128]{1,0:T(8,128)} %copy-done.13), custom_call_target="tpu_custom_call" | custom-call | tf_op jit(solution)/shard_map/pallas_call | solution.py:242
  (29 shorter events, 0.1 us)
Async XLA Ops:
  0.6 1.0 copy-start.1
  1.6 68.8 %copy-start.10 = (bf16[1536,64]{0,1:T(8,128)(2,1)S(1)}, bf16[1536,64]{0,1:T(8,128)(2,1)}, u32[]{:S(2)}) copy-start(bf16[1536,64]{0,1:T(8,128)(2,1)} %param.16) | copy-start | bytes 589828
  1.6 69.7 %copy-start.14 = (f32[1536]{0:T(1024)S(1)}, f32[1536]{0:T(1024)}, u32[]{:S(2)}) copy-start(f32[1536]{0:T(1024)} %param.15) | copy-start | bytes 18436
  1.6 86.1 %copy-start.4 = (f32[64,128]{1,0:T(8,128)S(1)}, f32[64,128]{1,0:T(8,128)}, u32[]{:S(2)}) copy-start(f32[64,128]{1,0:T(8,128)} %refs_6_.1) | copy-start | bytes 98308
  1.6 86.1 %copy-start.8 = (s32[8]{0:T(128)S(1)}, s32[8]{0:T(128)}, u32[]{:S(2)}) copy-start(s32[8]{0:T(128)} %levels.1) | copy-start | bytes 100
  1.6 86.1 %copy-start.9 = (s32[9]{0:T(128)S(1)}, s32[9]{0:T(128)}, u32[]{:S(2)}) copy-start(s32[9]{0:T(128)} %timesteps.1) | copy-start | bytes 112
  1.7 20.4 %collective-permute-start.17 = (bf16[128,384]{1,0:T(8,128)(2,1)S(1)}, bf16[128,384]{1,0:T(8,128)(2,1)S(1)}, u32[]{:S(2)}, u32[]{:S(2)}) collective-permute-start(bf16[128,384]{1,0:T(8,128)(2,1)S(1)} %get-tuple-element.26), channel_id=1, source_target_pairs={{0,16},{2,18},{4,20},{6,22},{8,24},{10,26},{12,28},{14,30},{16,0},... | collective-permute-start | bytes 294920 | tf_op jit(solution)/shard_map/ppermute | solution.py:44
  5.8 18.0 %collective-permute-start.18 = (bf16[128,384]{1,0:T(8,128)(2,1)S(1)}, bf16[128,384]{1,0:T(8,128)(2,1)S(1)}, u32[]{:S(2)}, u32[]{:S(2)}) collective-permute-start(bf16[128,384]{1,0:T(8,128)(2,1)S(1)} %get-tuple-element.27), channel_id=1, source_target_pairs={{0,24},{2,26},{4,28},{6,30},{8,16},{10,18},{12,20},{14,22},{16,8},... | collective-permute-start | bytes 294920 | tf_op jit(solution)/shard_map/ppermute | solution.py:44
  7.2 1.0 copy-start.2
  8.2 1.0 copy-start.3
  9.2 19.2 %collective-permute-start.8 = (bf16[256,384]{1,0:T(8,128)(2,1)S(1)}, bf16[256,384]{1,0:T(8,128)(2,1)S(1)}, u32[]{:S(2)}, u32[]{:S(2)}) collective-permute-start(bf16[256,384]{1,0:T(8,128)(2,1)S(1)} %get-tuple-element.22), channel_id=1, source_target_pairs={{0,16},{2,18},{4,20},{6,22},{8,24},{10,26},{12,28},{14,30},{16,0},... | collective-permute-start | bytes 589832 | tf_op jit(solution)/shard_map/ppermute | solution.py:44
  11.0 19.2 %collective-permute-start.12 = (bf16[256,384]{1,0:T(8,128)(2,1)S(1)}, bf16[256,384]{1,0:T(8,128)(2,1)S(1)}, u32[]{:S(2)}, u32[]{:S(2)}) collective-permute-start(bf16[256,384]{1,0:T(8,128)(2,1)S(1)} %get-tuple-element.23), channel_id=1, source_target_pairs={{0,24},{2,26},{4,28},{6,30},{8,16},{10,18},{12,20},{14,22},{16,8},... | collective-permute-start | bytes 589832 | tf_op jit(solution)/shard_map/ppermute | solution.py:44
  11.9 18.6 %collective-permute-start.4 = (bf16[256,384]{1,0:T(8,128)(2,1)S(1)}, bf16[256,384]{1,0:T(8,128)(2,1)S(1)}, u32[]{:S(2)}, u32[]{:S(2)}) collective-permute-start(bf16[256,384]{1,0:T(8,128)(2,1)S(1)} %get-tuple-element.21), channel_id=1, source_target_pairs={{0,8},{2,10},{4,12},{6,14},{8,0},{10,2},{12,4},{14,6},{16,24},{18,... | collective-permute-start | bytes 589832 | tf_op jit(solution)/shard_map/ppermute | solution.py:44
  22.1 10.1 %collective-permute-start.2 = (bf16[256,384]{1,0:T(8,128)(2,1)S(1)}, bf16[256,384]{1,0:T(8,128)(2,1)S(1)}, u32[]{:S(2)}, u32[]{:S(2)}) collective-permute-start(bf16[256,384]{1,0:T(8,128)(2,1)S(1)} %get-tuple-element.20.refs_2_), channel_id=1, source_target_pairs={{0,4},{2,6},{4,0},{6,2},{8,12},{10,14},{12,8},{14,10},{16,20},{18,... | collective-permute-start | bytes 589832 | tf_op jit(solution)/shard_map/ppermute | solution.py:47
  23.9 8.4 %collective-permute-start.1 = (bf16[256,384]{1,0:T(8,128)(2,1)S(1)}, bf16[256,384]{1,0:T(8,128)(2,1)S(1)}, u32[]{:S(2)}, u32[]{:S(2)}) collective-permute-start(bf16[256,384]{1,0:T(8,128)(2,1)S(1)} %get-tuple-element.20.refs_2_), channel_id=1, source_target_pairs={{0,2},{2,0},{4,6},{6,4},{8,10},{10,8},{12,14},{14,12},{16,18},{18,... | collective-permute-start | bytes 589832 | tf_op jit(solution)/shard_map/ppermute | solution.py:47
  28.4 7.8 %collective-permute-start.10 = (bf16[256,384]{1,0:T(8,128)(2,1)S(1)}, bf16[256,384]{1,0:T(8,128)(2,1)S(1)}, u32[]{:S(2)}, u32[]{:S(2)}) collective-permute-start(bf16[256,384]{1,0:T(8,128)(2,1)S(1)} %collective-permute-done.8.refs_10_), channel_id=1, source_target_pairs={{0,4},{2,6},{4,0},{6,2},{8,12},{10,14},{12,8},{14,10},{16,20},{18,... | collective-permute-start | bytes 589832 | tf_op jit(solution)/shard_map/ppermute | solution.py:47
  30.2 9.8 %collective-permute-start.14 = (bf16[256,384]{1,0:T(8,128)(2,1)S(1)}, bf16[256,384]{1,0:T(8,128)(2,1)S(1)}, u32[]{:S(2)}, u32[]{:S(2)}) collective-permute-start(bf16[256,384]{1,0:T(8,128)(2,1)S(1)} %collective-permute-done.12.refs_14_), channel_id=1, source_target_pairs={{0,4},{2,6},{4,0},{6,2},{8,12},{10,14},{12,8},{14,10},{16,20},{18,... | collective-permute-start | bytes 589832 | tf_op jit(solution)/shard_map/ppermute | solution.py:47
  30.5 11.7 %collective-permute-start.6 = (bf16[256,384]{1,0:T(8,128)(2,1)S(1)}, bf16[256,384]{1,0:T(8,128)(2,1)S(1)}, u32[]{:S(2)}, u32[]{:S(2)}) collective-permute-start(bf16[256,384]{1,0:T(8,128)(2,1)S(1)} %collective-permute-done.4.refs_6_), channel_id=1, source_target_pairs={{0,4},{2,6},{4,0},{6,2},{8,12},{10,14},{12,8},{14,10},{16,20},{18,... | collective-permute-start | bytes 589832 | tf_op jit(solution)/shard_map/ppermute | solution.py:47
  32.2 9.9 %collective-permute-start.3 = (bf16[256,384]{1,0:T(8,128)(2,1)S(1)}, bf16[256,384]{1,0:T(8,128)(2,1)S(1)}, u32[]{:S(2)}, u32[]{:S(2)}) collective-permute-start(bf16[256,384]{1,0:T(8,128)(2,1)S(1)} %collective-permute-done.2.refs_4_), channel_id=1, source_target_pairs={{0,2},{2,0},{4,6},{6,4},{8,10},{10,8},{12,14},{14,12},{16,18},{18,... | collective-permute-start | bytes 589832 | tf_op jit(solution)/shard_map/ppermute | solution.py:47
  32.2 10.4 %collective-permute-start.13 = (bf16[256,384]{1,0:T(8,128)(2,1)S(1)}, bf16[256,384]{1,0:T(8,128)(2,1)S(1)}, u32[]{:S(2)}, u32[]{:S(2)}) collective-permute-start(bf16[256,384]{1,0:T(8,128)(2,1)S(1)} %collective-permute-done.12.refs_14_), channel_id=1, source_target_pairs={{0,2},{2,0},{4,6},{6,4},{8,10},{10,8},{12,14},{14,12},{16,18},{18,... | collective-permute-start | bytes 589832 | tf_op jit(solution)/shard_map/ppermute | solution.py:47
  36.3 6.4 %collective-permute-start.5 = (bf16[256,384]{1,0:T(8,128)(2,1)S(1)}, bf16[256,384]{1,0:T(8,128)(2,1)S(1)}, u32[]{:S(2)}, u32[]{:S(2)}) collective-permute-start(bf16[256,384]{1,0:T(8,128)(2,1)S(1)} %collective-permute-done.4.refs_6_), channel_id=1, source_target_pairs={{0,2},{2,0},{4,6},{6,4},{8,10},{10,8},{12,14},{14,12},{16,18},{18,... | collective-permute-start | bytes 589832 | tf_op jit(solution)/shard_map/ppermute | solution.py:47
  40.0 4.2 %collective-permute-start.9 = (bf16[256,384]{1,0:T(8,128)(2,1)S(1)}, bf16[256,384]{1,0:T(8,128)(2,1)S(1)}, u32[]{:S(2)}, u32[]{:S(2)}) collective-permute-start(bf16[256,384]{1,0:T(8,128)(2,1)S(1)} %collective-permute-done.8.refs_10_), channel_id=1, source_target_pairs={{0,2},{2,0},{4,6},{6,4},{8,10},{10,8},{12,14},{14,12},{16,18},{18,... | collective-permute-start | bytes 589832 | tf_op jit(solution)/shard_map/ppermute | solution.py:47
  42.1 2.1 %collective-permute-start.11 = (bf16[256,384]{1,0:T(8,128)(2,1)S(1)}, bf16[256,384]{1,0:T(8,128)(2,1)S(1)}, u32[]{:S(2)}, u32[]{:S(2)}) collective-permute-start(bf16[256,384]{1,0:T(8,128)(2,1)S(1)} %collective-permute-done.10.refs_12_), channel_id=1, source_target_pairs={{0,2},{2,0},{4,6},{6,4},{8,10},{10,8},{12,14},{14,12},{16,18},{18,... | collective-permute-start | bytes 589832 | tf_op jit(solution)/shard_map/ppermute | solution.py:47
  42.1 2.1 %collective-permute-start.15 = (bf16[256,384]{1,0:T(8,128)(2,1)S(1)}, bf16[256,384]{1,0:T(8,128)(2,1)S(1)}, u32[]{:S(2)}, u32[]{:S(2)}) collective-permute-start(bf16[256,384]{1,0:T(8,128)(2,1)S(1)} %collective-permute-done.14.refs_16_), channel_id=1, source_target_pairs={{0,2},{2,0},{4,6},{6,4},{8,10},{10,8},{12,14},{14,12},{16,18},{18,... | collective-permute-start | bytes 589832 | tf_op jit(solution)/shard_map/ppermute | solution.py:47
  42.6 1.5 %collective-permute-start.7 = (bf16[256,384]{1,0:T(8,128)(2,1)S(1)}, bf16[256,384]{1,0:T(8,128)(2,1)S(1)}, u32[]{:S(2)}, u32[]{:S(2)}) collective-permute-start(bf16[256,384]{1,0:T(8,128)(2,1)S(1)} %collective-permute-done.6.refs_8_), channel_id=1, source_target_pairs={{0,2},{2,0},{4,6},{6,4},{8,10},{10,8},{12,14},{14,12},{16,18},{18,... | collective-permute-start | bytes 589832 | tf_op jit(solution)/shard_map/ppermute | solution.py:47
  42.7 9.9 %collective-permute-start = (bf16[128,384]{1,0:T(8,128)(2,1)S(1)}, bf16[128,384]{1,0:T(8,128)(2,1)S(1)}, u32[]{:S(2)}, u32[]{:S(2)}) collective-permute-start(bf16[128,384]{1,0:T(8,128)(2,1)S(1)} %get-tuple-element.19), channel_id=1, source_target_pairs={{0,8},{2,10},{4,12},{6,14},{8,0},{10,2},{12,4},{14,6},{16,24},{18,... | collective-permute-start | bytes 294920 | tf_op jit(solution)/shard_map/ppermute | solution.py:44
  44.2 0.7 copy-start.6
  48.3 11.2 %collective-permute-start.19 = (bf16[128,384]{1,0:T(8,128)(2,1)S(1)}, bf16[128,384]{1,0:T(8,128)(2,1)S(1)}, u32[]{:S(2)}, u32[]{:S(2)}) collective-permute-start(bf16[128,384]{1,0:T(8,128)(2,1)S(1)} %get-tuple-element.28), channel_id=1, source_target_pairs={{0,16},{2,18},{4,20},{6,22},{8,24},{10,26},{12,28},{14,30},{16,0},... | collective-permute-start | bytes 294920 | tf_op jit(solution)/shard_map/ppermute | solution.py:44
  51.7 7.8 %collective-permute-start.20 = (bf16[128,384]{1,0:T(8,128)(2,1)S(1)}, bf16[128,384]{1,0:T(8,128)(2,1)S(1)}, u32[]{:S(2)}, u32[]{:S(2)}) collective-permute-start(bf16[128,384]{1,0:T(8,128)(2,1)S(1)} %get-tuple-element.29), channel_id=1, source_target_pairs={{0,24},{2,26},{4,28},{6,30},{8,16},{10,18},{12,20},{14,22},{16,8},... | collective-permute-start | bytes 294920 | tf_op jit(solution)/shard_map/ppermute | solution.py:44
  52.6 0.7 copy-start.7
  56.7 4.8 %collective-permute-start.16 = (bf16[128,384]{1,0:T(8,128)(2,1)S(1)}, bf16[128,384]{1,0:T(8,128)(2,1)S(1)}, u32[]{:S(2)}, u32[]{:S(2)}) collective-permute-start(bf16[128,384]{1,0:T(8,128)(2,1)S(1)} %get-tuple-element.25), channel_id=1, source_target_pairs={{0,8},{2,10},{4,12},{6,14},{8,0},{10,2},{12,4},{14,6},{16,24},{18,... | collective-permute-start | bytes 294920 | tf_op jit(solution)/shard_map/ppermute | solution.py:44
  61.5 3.7 %copy-start = (bf16[1536,3072]{1,0:T(8,128)(2,1)S(1)}, bf16[1536,3072]{1,0:T(8,128)(2,1)}, u32[]{:S(2)}) copy-start(bf16[1536,3072]{1,0:T(8,128)(2,1)} %refs_4_.2) | copy-start | bytes 28311556
  68.9 18.8 %collective-permute-start.21 = (bf16[64,3072]{1,0:T(8,128)(2,1)S(1)}, bf16[64,3072]{1,0:T(8,128)(2,1)S(1)}, u32[]{:S(2)}, u32[]{:S(2)}) collective-permute-start(bf16[64,3072]{1,0:T(8,128)(2,1)S(1)} %get-tuple-element.31), channel_id=1, source_target_pairs={{0,1},{1,0},{2,3},{3,2},{4,5},{5,4},{6,7},{7,6},{8,9},{9,8},{10,11... | collective-permute-start | bytes 1179656 | tf_op jit(solution)/shard_map/ppermute | solution.py:50
  70.7 17.1 %collective-permute-start.23 = (bf16[1536,64]{1,0:T(8,128)(2,1)S(1)}, bf16[1536,64]{1,0:T(8,128)(2,1)S(1)}, u32[]{:S(2)}, u32[]{:S(2)}) collective-permute-start(bf16[1536,64]{1,0:T(8,128)(2,1)S(1)} %copy.13.refs_4_), channel_id=1, source_target_pairs={{0,1},{1,0},{2,3},{3,2},{4,5},{5,4},{6,7},{7,6},{8,9},{9,8},{10,11... | collective-permute-start | bytes 589832 | tf_op jit(solution)/shard_map/ppermute | solution.py:50
  71.3 16.4 %collective-permute-start.22 = (f32[1,1536]{1,0:T(1,128)S(1)}, f32[1,1536]{1,0:T(1,128)S(1)}, u32[]{:S(2)}, u32[]{:S(2)}) collective-permute-start(f32[1,1536]{1,0:T(1,128)S(1)} %broadcast_in_dim.3.refs_2_), channel_id=1, source_target_pairs={{0,1},{1,0},{2,3},{3,2},{4,5},{5,4},{6,7},{7,6},{8,9},{9,8},{10,11... | collective-permute-start | bytes 18440 | tf_op jit(solution)/shard_map/ppermute | solution.py:50
  88.8 10.4 %copy-start.5 = (f32[32,128]{1,0:T(8,128)}, f32[32,128]{1,0:T(8,128)S(1)}, u32[]{:S(2)}) copy-start(f32[32,128]{1,0:T(8,128)S(1)} %get-tuple-element.32.refs_0_) | copy-start | bytes 49156
  88.8 4.2 %collective-permute-start.24 = (f32[32,128]{1,0:T(8,128)S(1)}, f32[32,128]{1,0:T(8,128)S(1)}, u32[]{:S(2)}, u32[]{:S(2)}) collective-permute-start(f32[32,128]{1,0:T(8,128)S(1)} %get-tuple-element.32.refs_0_), channel_id=1, source_target_pairs={{0,1},{1,0},{2,3},{3,2},{4,5},{5,4},{6,7},{7,6},{8,9},{9,8},{10,11... | collective-permute-start | bytes 49160 | tf_op jit(solution)/shard_map/ppermute | solution.py:50
  90.3 6.4 %collective-permute-start.25 = (f32[32,128]{1,0:T(8,128)S(1)}, f32[32,128]{1,0:T(8,128)S(1)}, u32[]{:S(2)}, u32[]{:S(2)}) collective-permute-start(f32[32,128]{1,0:T(8,128)S(1)} %get-tuple-element.33), channel_id=1, source_target_pairs={{0,4},{1,5},{2,6},{3,7},{4,8},{5,9},{6,10},{7,11},{8,12},{9,13},{1... | collective-permute-start | bytes 49160 | tf_op jit(solution)/shard_map/ppermute | solution.py:58
  91.8 7.3 %collective-permute-start.26 = (f32[32,128]{1,0:T(8,128)S(1)}, f32[32,128]{1,0:T(8,128)S(1)}, u32[]{:S(2)}, u32[]{:S(2)}) collective-permute-start(f32[32,128]{1,0:T(8,128)S(1)} %get-tuple-element.33), channel_id=1, source_target_pairs={{0,5},{1,4},{2,7},{3,6},{4,9},{5,8},{6,11},{7,10},{8,13},{9,12},{1... | collective-permute-start | bytes 49160 | tf_op jit(solution)/shard_map/ppermute | solution.py:58
  92.9 6.2 %copy-start.11 = (f32[32,128]{1,0:T(8,128)}, f32[32,128]{1,0:T(8,128)S(1)}, u32[]{:S(2)}) copy-start(f32[32,128]{1,0:T(8,128)S(1)} %collective-permute-done.24.refs_1_) | copy-start | bytes 49156
  96.7 2.4 %copy-start.12 = (f32[32,128]{1,0:T(8,128)}, f32[32,128]{1,0:T(8,128)S(1)}, u32[]{:S(2)}) copy-start(f32[32,128]{1,0:T(8,128)S(1)} %collective-permute-done.25.refs_2_) | copy-start | bytes 49156
  99.2 0.6 copy-start.13

commit v2 on v1

v2 whole, which is shorter than its diff:
```python
import functools
import math

import jax
import jax.numpy as jnp
from jax import lax
from jax.experimental import pallas as pl
from jax.experimental.pallas import tpu as pltpu
from jax.sharding import PartitionSpec as P

HD = 128
GROUPS = 8
MAX_HEAD_SPLIT = 4
NEG = -1e30
VMEM = pl.BlockSpec(memory_space=pltpu.VMEM)
ANY = pl.BlockSpec(memory_space=pl.ANY)
SMEM = pl.BlockSpec(memory_space=pltpu.SMEM)


def params(mib):
    return pltpu.CompilerParams(vmem_limit_bytes=mib * 1024 * 1024)


def struct(shape, dtype):
    return jax.ShapeDtypeStruct(shape, dtype)


class Plan:
    def __init__(self, queries):
        self.sections = lax.axis_size("section")
        self.tensors = lax.axis_size("tensor")
        self.rows, self.width = queries.shape
        self.heads = self.width // HD
        self.split = math.gcd(self.heads, MAX_HEAD_SPLIT)
        self.members = self.sections // self.split
        self.cols = self.width // self.split
        self.span = self.sections // GROUPS
        self.share = self.rows // self.tensors
        self.per = 2 if self.span % 2 == 0 and self.members % 2 == 0 else 1
        self.blocks = self.sections // self.per

    def part(self):
        return lax.axis_index("section") // self.members

    def to_part(self, value, step):
        pairs = [(s, s ^ (step * self.members)) for s in range(self.sections)]
        return lax.ppermute(value, "section", pairs)

    def to_member(self, value, step):
        return lax.ppermute(value, "section", [(s, s ^ step) for s in range(self.sections)])

    def to_tensor(self, value, step):
        return lax.ppermute(value, "tensor", [(t, t ^ step) for t in range(self.tensors)])

    def to_next_group(self, value, step):
        pairs = [
            (s * self.tensors + t, ((s + self.span) % self.sections) * self.tensors + (t ^ step))
            for s in range(self.sections)
            for t in range(self.tensors)
        ]
        return lax.ppermute(value, ("section", "tensor"), pairs)

    def gather_members(self, piece):
        pieces = {0: piece}
        step = self.members // 2
        while step:
            pieces.update({i ^ step: self.to_member(v, step) for i, v in list(pieces.items())})
            step //= 2
        return [pieces[i] for i in range(self.members)]


def pack(plan, step, *arrays):
    at = (plan.part() ^ step) * plan.cols
    return jnp.concatenate([lax.dynamic_slice_in_dim(a, at, plan.cols, 1) for a in arrays], axis=0)


def held(values, after):
    def kernel(*refs):
        pass

    return pl.pallas_call(
        kernel,
        out_shape=[struct(v.shape, v.dtype) for v in values],
        in_specs=[ANY] * (len(values) + len(after)),
        out_specs=[ANY] * len(values),
        input_output_aliases={i: i for i in range(len(values))},
        compiler_params=params(1),
    )(*values, *after)


def ready_kernel(plan, waits, order, gain, head_weight, *refs):
    shared, bias = refs[waits:]
    count = head_weight.shape[0]
    shared[pl.ds(0, count), :] = head_weight[...]
    rest, rows = gain[...], []
    for _ in range(3):
        rows.append(rest.astype(jnp.bfloat16))
        rest = rest - rows[-1].astype(jnp.float32)
    rows = [jnp.broadcast_to(row, (16, gain.shape[1])) for row in rows]
    shared[pl.ds(count, 48), :] = jnp.concatenate(rows, axis=0)
    me = lax.axis_index("section")

    def order_of(step, member):
        return order[(me ^ (step * plan.members + member)) // plan.span]

    for i in range(plan.split):
        for j in range(plan.blocks):
            first = j * plan.per
            seen = order_of(first // plan.members, first % plan.members) <= order_of(i, 0)
            bias[pl.ds(i * plan.blocks + j, 1), :] = jnp.full((1, HD), jnp.where(seen, 0.0, NEG))


def ready(plan, order, gain, head_weight, after):
    return pl.pallas_call(
        functools.partial(ready_kernel, plan, len(after)),
        out_shape=[
            struct((head_weight.shape[0] + 48, head_weight.shape[1]), jnp.bfloat16),
            struct((plan.split * plan.blocks, HD), jnp.float32),
        ],
        in_specs=[SMEM, VMEM, VMEM] + [ANY] * len(after),
        out_specs=[VMEM, VMEM],
        compiler_params=params(4),
    )(order, gain, head_weight, *after)


def attend_kernel(plan, steps, waits, bias, *refs):
    rows = plan.rows
    refs = refs[waits:]
    queries, refs = refs[: len(steps)], refs[len(steps) :]
    pieces, refs = refs[: plan.sections], refs[plan.sections :]
    outs, scores = refs[: len(steps)], refs[len(steps)]
    factor = math.log2(math.e) / math.sqrt(HD)
    many = len(steps) * rows
    width = plan.per * rows

    def hidden(j):
        at = [step * plan.blocks + j for step in steps]
        return jnp.concatenate([jnp.broadcast_to(bias[pl.ds(i, 1), :], (rows, HD)) for i in at], axis=0)

    def block(j, which, lanes):
        parts = pieces[j * plan.per : (j + 1) * plan.per]
        return jnp.concatenate([ref[pl.ds(which * rows, rows), lanes] for ref in parts], axis=0)

    for h in range(plan.cols // HD):
        lanes = pl.ds(h * HD, HD)
        q = [ref[pl.ds(ref.shape[0] - rows, rows), lanes] for ref in queries]
        q = jnp.concatenate(q, axis=0)
        top = None
        for j in range(plan.blocks):
            s = lax.dot_general(q, block(j, 0, lanes), (((1,), (1,)), ((), ())), preferred_element_type=jnp.float32)
            scores[:, pl.ds(j * width, width)] = s
            s = functools.reduce(jnp.maximum, [s[:, i : i + HD] for i in range(0, width, HD)])
            s = s + hidden(j)
            top = s if top is None else jnp.maximum(top, s)
        top = jnp.broadcast_to(jnp.max(top, axis=1, keepdims=True), top.shape)
        total = jnp.zeros((many, HD), jnp.float32)
        summed = jnp.zeros((many, HD), jnp.float32)
        for j in range(plan.blocks):
            base = top - hidden(j)
            w = [scores[:, pl.ds(j * width + i, HD)] for i in range(0, width, HD)]
            w = [jnp.exp2((s - base) * factor) for s in w]
            total += functools.reduce(jnp.add, w)
            w = jnp.concatenate(w, axis=1).astype(jnp.bfloat16)
            summed += jnp.dot(w, block(j, 1, lanes), preferred_element_type=jnp.float32)
        out = (summed / jnp.sum(total, axis=1, keepdims=True)).astype(jnp.bfloat16)
        for i, ref in enumerate(outs):
            ref[:, lanes] = out[i * rows : (i + 1) * rows]


def attend(plan, steps, bias, queries, pieces, after=()):
    keys = plan.sections * plan.rows
    return pl.pallas_call(
        functools.partial(attend_kernel, plan, steps, len(after)),
        out_shape=[struct((plan.rows, plan.cols), jnp.bfloat16)] * len(steps),
        in_specs=[VMEM] + [ANY] * len(after) + [VMEM] * (len(steps) + len(pieces)),
        out_specs=[VMEM] * len(steps),
        scratch_shapes=[pltpu.VMEM((len(steps) * plan.rows, keys), jnp.float32)],
        compiler_params=params(12),
        cost_estimate=pl.CostEstimate(
            flops=4 * len(steps) * plan.rows * keys * plan.cols,
            bytes_accessed=4 * keys * plan.cols,
            transcendentals=len(steps) * plan.rows * keys * plan.cols // HD,
        ),
    )(bias, *after, *queries, *pieces)


def project_kernel(plan, steps, begun, *refs):
    parts, weight, refs = refs[: len(steps)], refs[len(steps)], refs[len(steps) + 1 :]
    outs = refs[1:] if begun else refs
    part, tensor = plan.part(), lax.axis_index("tensor")
    tile = 512
    for at in range(0, weight.shape[1], tile):
        cols = pl.ds(at, tile)
        total = refs[0][:, cols] if begun else None
        for step, ref in zip(steps, parts):
            here = pl.ds(pl.multiple_of((part ^ step) * plan.cols, 128), plan.cols)
            term = jnp.dot(ref[...], weight[here, cols], preferred_element_type=jnp.float32)
            total = term if total is None else total + term
        if not begun:
            outs[0][:, cols] = total
        else:
            full = outs[-1]
            full[...] = total
            for step, out in enumerate(outs[:-1]):
                here = pl.ds(pl.multiple_of((tensor ^ step) * plan.share, 8), plan.share)
                out[:, cols] = full[here, :].astype(out.dtype)


def project(plan, steps, parts, weight, begun=None):
    width = weight.shape[1]
    if begun is None:
        shapes, scratch, extra = struct((plan.rows, width), jnp.float32), [], ()
    else:
        shapes = [struct((plan.share, width), jnp.float32)]
        shapes += [struct((plan.share, width), jnp.bfloat16)] * (plan.tensors - 1)
        scratch, extra = [pltpu.VMEM((plan.rows, 512), jnp.float32)], (begun,)
    return pl.pallas_call(
        functools.partial(project_kernel, plan, steps, begun is not None),
        out_shape=shapes,
        in_specs=[VMEM] * (len(parts) + 1 + len(extra)),
        out_specs=VMEM if begun is None else [VMEM] * plan.tensors,
        scratch_shapes=scratch,
        compiler_params=params(16),
        cost_estimate=pl.CostEstimate(flops=1, bytes_accessed=1, transcendentals=0),
    )(*parts, weight, *extra)


def head_kernel(plan, levels, timesteps, *refs):
    sums, refs = refs[: plan.tensors], refs[plan.tensors :]
    shared, refs = refs[: plan.tensors], refs[plan.tensors :]
    latents, velocity_ref, moved_ref, full, rows = refs
    tensor = lax.axis_index("tensor")
    total = sums[0][...]
    for ref in sums[1:]:
        total = total + ref[...].astype(jnp.float32)
    full[...] = total
    squares = jnp.sum(total * total, axis=1, keepdims=True)
    count = rows.shape[1]
    raw = None
    for step, ref in enumerate(shared):
        share = ref.shape[1]
        here = pl.ds(pl.multiple_of((tensor ^ step) * share, 128), share)
        gain = sum(ref[pl.ds(count + 16 * i, 16), :].astype(jnp.float32)[:1] for i in range(3))
        scaled = (full[:, here] * gain).astype(jnp.bfloat16)
        term = lax.dot_general(
            scaled,
            ref[pl.ds(0, count), :],
            (((1,), (1,)), ((), ())),
            preferred_element_type=jnp.float32,
        )
        raw = term if raw is None else raw + term
    rows[...] = raw * lax.rsqrt(squares / total.shape[1] + 1e-6)
    half = plan.share // 2
    velocity = jnp.concatenate(
        [rows[pl.ds(0, half, 2), :], rows[pl.ds(1, half, 2), :]], axis=1
    )
    level = levels[lax.axis_index("section") // plan.span]
    change = (timesteps[level + 1] - timesteps[level]).astype(jnp.float32)
    delta = jnp.full(velocity.shape, change, jnp.float32) / 1000.0
    velocity_ref[...] = velocity
    here = pl.ds(pl.multiple_of(tensor * half, 8), half)
    moved_ref[...] = latents[here, :] + delta * velocity


def head(plan, levels, timesteps, sums, shared, latents):
    half = struct((plan.share // 2, latents.shape[1]), jnp.float32)
    return pl.pallas_call(
        functools.partial(head_kernel, plan),
        out_shape=[half, half],
        in_specs=[SMEM, SMEM] + [VMEM] * (2 * plan.tensors + 1),
        out_specs=[VMEM, VMEM],
        scratch_shapes=[
            pltpu.VMEM(sums[0].shape, jnp.float32),
            pltpu.VMEM((plan.share, latents.shape[1] // 2), jnp.float32),
        ],
        compiler_params=params(12),
    )(levels, timesteps, *sums, *shared, latents)


def place_kernel(plan, *refs):
    velocities, moved = refs[: plan.tensors], refs[plan.tensors : 2 * plan.tensors]
    tensor = lax.axis_index("tensor")
    for parts, out in ((velocities, refs[-2]), (moved, refs[-1])):
        for step, ref in enumerate(parts):
            rows = ref.shape[0]
            out[pl.ds(pl.multiple_of((tensor ^ step) * rows, 8), rows), :] = ref[...]


def place(plan, velocities, moved):
    shape = struct((plan.rows // 2, velocities[0].shape[1]), jnp.float32)
    return pl.pallas_call(
        functools.partial(place_kernel, plan),
        out_shape=[shape, shape],
        in_specs=[VMEM] * (2 * plan.tensors),
        out_specs=[VMEM, VMEM],
        compiler_params=params(2),
    )(*velocities, *moved)


def local(queries, keys, values, latents, out_weight, gain, head_weight, levels, timesteps, order):
    plan = Plan(queries)
    split, tensors = plan.split, plan.tensors

    far, near = list(range(1, split)), [0]
    own, asked = pack(plan, 0, keys, values), [pack(plan, 0, queries)]
    if split == 4 and plan.members == 4:
        two = plan.to_part(pack(plan, 2, keys, values, queries), 2)
        one = plan.to_part(pack(plan, 1, keys, values, queries), 1)
        shared, bias = ready(plan, order, gain[None, :], head_weight.T, [one])
        own = plan.gather_members(own)
        ones = plan.gather_members(one[: 2 * plan.rows])
        three = pack(plan, 3, keys, values, queries)
        gate = [two, own[2]]
        three = plan.to_part(held([three], gate)[0] if gate else three, 3)
        asked += [one, two, three]
        twos = plan.gather_members(*held([two[: 2 * plan.rows]], [bias]))
        threes = plan.gather_members(*held([three[: 2 * plan.rows]], [ones[2], twos[2]]))
        pieces = own + ones + twos + threes
    else:
        shared, bias = ready(plan, order, gain[None, :], head_weight.T, [])
        sent = [own] + [plan.to_part(pack(plan, i, keys, values), i) for i in far]
        asked += [plan.to_part(pack(plan, i, queries), i) for i in far]
        pieces = [p for v in sent for p in plan.gather_members(v)]
    shared = [shared] + [plan.to_tensor(shared, i) for i in range(1, tensors)]

    attended = [None] * split
    done = []
    if far:
        done = attend(plan, far, bias, [asked[i] for i in far], pieces)
        attended[1:] = [plan.to_part(v, i) for i, v in zip(far, done)]
    (attended[0],) = attend(plan, near, bias, asked[:1], pieces, done[:1])
    sums = project(plan, near, attended[:1], out_weight)
    if far:
        attended[1:2] = held(attended[1:2], shared[1:])
    sums = project(plan, far, attended[1:], out_weight, sums)
    sums = [sums[0]] + [plan.to_tensor(sums[i], i) for i in range(1, tensors)]
    velocity, moved = head(plan, levels, timesteps, sums, shared, latents)
    advanced = [plan.to_next_group(moved, i) for i in range(tensors)]
    velocities = [velocity] + [plan.to_tensor(velocity, i) for i in range(1, tensors)]
    return place(plan, advanced, velocities)[::-1]


def solution(mesh):
    return jax.shard_map(
        local,
        mesh=mesh,
        in_specs=(
            P("section", "tensor"),
            P("section", "tensor"),
            P("section", "tensor"),
            P("section", None),
            P("tensor", None),
            P("tensor"),
            P("tensor", None),
            P(),
            P(),
            P(),
        ),
        out_specs=(P("section", None), P("section", None)),
        check_vma=False,
    )
```

time: 102 us -> 81.2 us (0.80)
  waiting for transfers between devices: 48.8 us -> 37.9 us
  local copies, waits for them, and re-layouts: 8.81 us -> 5.15 us
  starting transfers between devices: 29.8 us -> 26.6 us
  Pallas kernels: 13 us -> 10.2 us
    unnamed x31 -> x12, local copies, waits for them, and re-layouts: 8.81 us -> 1.6 us
    ppermute x4 -> x3, waiting for transfers between devices: 14.9 us -> 7.95 us  [to_tensor(): lax.ppermute(value, 'tensor', [(t, t ^ step) for t in range(self.tensors)])]
    ppermute x9 -> x6, waiting for transfers between devices: 18.2 us -> 12.7 us  [to_part(): return lax.ppermute(value, 'section', pairs)]
    ppermute x12, waiting for transfers between devices: 9.42 us -> 14.2 us  [to_member(): lax.ppermute(value, 'section', [(s, s ^ step) for s in range(self.section...]
    ppermute x2, waiting for transfers between devices: 6.24 us -> 3.03 us  [to_next_group(): return lax.ppermute(value, ('section', 'tensor'), pairs)]
    dynamic_slice x0 -> x2, local copies, waits for them, and re-layouts: none -> 2.79 us  [pack(): lax.dynamic_slice_in_dim(a, at, plan.cols, 1)]
    ppermute x9 -> x6, starting transfers between devices: 15.4 us -> 12.7 us  [to_part(): return lax.ppermute(value, 'section', pairs)]
    ppermute x2, starting transfers between devices: 2.62 us -> 4.88 us  [to_next_group(): return lax.ppermute(value, ('section', 'tensor'), pairs)]
  transfers between devices with their start and end apart: 27 -> 23, of which waited for: 10 -> 10; matrix products, arithmetic and copies ran while one was open for 0% -> 1% of each run, Pallas kernels for 7% -> 9%
where the time goes in v2:
time: 81.2 us; the launch traced here: 80.9 us
  waiting for transfers between devices  37.9 us (47%)
  starting transfers between devices  26.6 us (33%)
  Pallas kernels  10.2 us (13%)
  local copies, waits for them, and re-layouts  5.15 us (6%)
  between operations  0.87 us (1%)
    ppermute x12, waiting for transfers between devices, to_member(): lax.ppermute(value, 'section', [(s, s ^ step) for s in range(self.section...  14.2 us
    ppermute x6, waiting for transfers between devices, to_part(): return lax.ppermute(value, 'section', pairs)  12.7 us
    ppermute x6, starting transfers between devices, to_part(): return lax.ppermute(value, 'section', pairs)  12.7 us
    ppermute x3, waiting for transfers between devices, to_tensor(): lax.ppermute(value, 'tensor', [(t, t ^ step) for t in range(self.tensors)])  7.95 us
    pallas_call x2, Pallas kernels, attend(): pl.pallas_call(functools.partial(attend_kernel, plan, steps, len(after)),...  5.74 us
    ppermute x12, starting transfers between devices, to_member(): lax.ppermute(value, 'section', [(s, s ^ step) for s in range(self.section...  5.28 us
    ppermute x2, starting transfers between devices, to_next_group(): return lax.ppermute(value, ('section', 'tensor'), pairs)  4.88 us
    ppermute x3, starting transfers between devices, to_tensor(): lax.ppermute(value, 'tensor', [(t, t ^ step) for t in range(self.tensors)])  3.8 us
  transfers between devices with their start and end apart: 23, of which 10 were waited for; matrix products, arithmetic and copies ran while one was open for 1% of the time, Pallas kernels for 9%

profile of v2, /device:TPU:0, one launch (start us, length us, event | category | flops | bytes accessed | tf_op | source)
XLA Modules:
  0.0 80.9 jit_solution(14071263583049066209)
XLA Ops:
  0.7 0.0 copy-start
  0.7 1.2 %constant_dynamic-slice_fusion = (bf16[128,384]{1,0:T(8,128)(2,1)S(1)}, bf16[128,384]{1,0:T(8,128)(2,1)S(1)}, bf16[128,384]{1,0:T(8,128)(2,1)S(1)}, bf16[128,384]{1,0:T(8,128)(2,1)S(1)}) fusion(bf16[128,1536]{1,0:T(8,128)(2,1)} %param.10, s32[]{:T(128)S(6)} %select_n.33, s32[]{:T(128)S(6)} %select_n.31, s32[]{:T(128)S(6)} %select_n.30, s32[]{:T(128)S(6)} %select_n.32), kind=kLoop, calls=%fused_computation.4 | loop fusion | bytes 786448 | tf_op jit(solution)/shard_map/dynamic_slice | solution.py:74
  1.9 1.5 %constant_dynamic-slice_fusion.1 = (bf16[128,384]{1,0:T(8,128)(2,1)S(1)}, bf16[128,384]{1,0:T(8,128)(2,1)S(1)}, bf16[128,384]{1,0:T(8,128)(2,1)S(1)}, bf16[128,3...) fusion(bf16[128,1536]{1,0:T(8,128)(2,1)} %param.12, ...), kind=kLoop, calls=%fused_computation.5 | loop fusion | bytes 1572880 | tf_op jit(solution)/shard_map/dynamic_slice | solution.py:74
  3.5 3.1 %collective-permute-start = (bf16[384,384]{1,0:T(8,128)(2,1)S(1)}, bf16[384,384]{1,0:T(8,128)(2,1)S(1)}, u32[]{:S(2)}, u32[]{:S(2)}) collective-permute-start(bf16[384,384]{1,0:T(8,128)(2,1)S(1)} %pad_maximum_fusion), channel_id=1, source_target_pairs={{0,8},{2,10},{4,12},{6,14},{8,0},{10,2},{12,4},{14,6},{16,24},{18,... | collective-permute-start | bytes 884744 | tf_op jit(solution)/shard_map/ppermute | solution.py:47
  6.6 2.7 %collective-permute-start.1 = (bf16[384,384]{1,0:T(8,128)(2,1)S(1)}, bf16[384,384]{1,0:T(8,128)(2,1)S(1)}, u32[]{:S(2)}, u32[]{:S(2)}) collective-permute-start(bf16[384,384]{1,0:T(8,128)(2,1)S(1)} %pad_maximum_fusion.1), channel_id=1, source_target_pairs={{0,16},{2,18},{4,20},{6,22},{8,24},{10,26},{12,28},{14,30},{16,0},... | collective-permute-start | bytes 884744 | tf_op jit(solution)/shard_map/ppermute | solution.py:47
  9.3 1.6 %collective-permute-start.2 = (bf16[256,384]{1,0:T(8,128)(2,1)S(1)}, bf16[256,384]{1,0:T(8,128)(2,1)S(1)}, u32[]{:S(2)}, u32[]{:S(2)}) collective-permute-start(bf16[256,384]{1,0:T(8,128)(2,1)S(1)} %pad_maximum_fusion.3.refs_3_.refs_2_), channel_id=1, source_target_pairs={{0,4},{2,6},{4,0},{6,2},{8,12},{10,14},{12,8},{14,10},{16,20},{18,... | collective-permute-start | bytes 589832 | tf_op jit(solution)/shard_map/ppermute | solution.py:50
  10.9 4.5 %collective-permute-done.2.refs_2_.refs_5_.refs_4_ = bf16[256,384]{1,0:T(8,128)(2,1)S(1)} collective-permute-done((bf16[256,384]{1,0:T(8,128)(2,1)S(1)}, bf16[256,384]{1,0:T(8,128)(2,1)S(1)}, u32[]{:S(2)}, u32[]{:S(2)}) %collective-permute-start.2) | collective-permute-done | bytes 196640 | tf_op jit(solution)/shard_map/ppermute | solution.py:50
  15.5 7.0 %collective-permute-done.1.refs_1_ = bf16[384,384]{1,0:T(8,128)(2,1)S(1)} collective-permute-done((bf16[384,384]{1,0:T(8,128)(2,1)S(1)}, bf16[384,384]{1,0:T(8,128)(2,1)S(1)}, u32[]{:S(2)}, u32[]{:S(2)}) %collective-permute-start.1) | collective-permute-done | bytes 294944 | tf_op jit(solution)/shard_map/ppermute | solution.py:47
  22.4 2.5 %collective-permute-start.3 = (bf16[384,384]{1,0:T(8,128)(2,1)S(1)}, bf16[384,384]{1,0:T(8,128)(2,1)S(1)}, u32[]{:S(2)}, u32[]{:S(2)}) collective-permute-start(bf16[384,384]{1,0:T(8,128)(2,1)S(1)} %shard_map.114), channel_id=1, source_target_pairs={{0,24},{2,26},{4,28},{6,30},{8,16},{10,18},{12,20},{14,22},{16,8},... | collective-permute-start | bytes 884744 | tf_op jit(solution)/shard_map/ppermute | solution.py:47
  24.9 0.7 broadcast_in_dim.3.gain
  25.6 0.0 collective-permute-done.refs_0_
  25.6 1.6 %collective-permute-start.7 = (bf16[256,384]{1,0:T(8,128)(2,1)S(1)}, bf16[256,384]{1,0:T(8,128)(2,1)S(1)}, u32[]{:S(2)}, u32[]{:S(2)}) collective-permute-start(bf16[256,384]{1,0:T(8,128)(2,1)S(1)} %slice.12.refs_7_.refs_6_), channel_id=1, source_target_pairs={{0,4},{2,6},{4,0},{6,2},{8,12},{10,14},{12,8},{14,10},{16,20},{18,... | collective-permute-start | bytes 589832 | tf_op jit(solution)/shard_map/ppermute | solution.py:50
  27.2 0.0 copy-start.1
  27.3 0.9 %copy-done.1 = bf16[1536,64]{0,1:T(8,128)(2,1)S(1)} copy-done((bf16[1536,64]{0,1:T(8,128)(2,1)S(1)}, bf16[1536,64]{0,1:T(8,128)(2,1)}, u32[]{:S(2)}) %copy-start.1) | copy-done | bytes 196632
  28.2 0.7 copy-done.3
  28.8 0.6 shard_map.113
  29.5 0.6 collective-permute-start.10
  30.1 0.0 collective-permute-start.4
  30.1 0.5 collective-permute-start.5
  30.6 0.5 collective-permute-done.3.refs_2_
  31.1 0.0 collective-permute-start.6
  31.1 0.5 collective-permute-done.7.refs_1_.refs_9_.refs_8_
  31.6 4.6 %collective-permute-done.10.refs_2_.refs_13_.refs_12_ = bf16[256,384]{1,0:T(8,128)(2,1)S(1)} collective-permute-done((bf16[256,384]{1,0:T(8,128)(2,1)S(1)}, bf16[256,384]{1,0:T(8,128)(2,1)S(1)}, u32[]{:S(2)}, u32[]{:S(2)}) %collective-permute-start.10) | collective-permute-done | bytes 196640 | tf_op jit(solution)/shard_map/ppermute | solution.py:50
  36.1 0.0 collective-permute-start.13
  36.1 0.0 collective-permute-start.9
  36.1 0.0 collective-permute-done.4.refs_4_.refs_3_
  36.1 0.5 collective-permute-start.8
  36.7 0.0 collective-permute-done.5.refs_6_.refs_5_
  36.7 0.1 collective-permute-start.11
  36.7 0.0 collective-permute-done.6.refs_8_.refs_7_
  36.7 0.4 collective-permute-start.12
  37.2 4.6 %collective-permute-done.13.refs_17_.refs_16_ = bf16[256,384]{1,0:T(8,128)(2,1)S(1)} collective-permute-done((bf16[256,384]{1,0:T(8,128)(2,1)S(1)}, bf16[256,384]{1,0:T(8,128)(2,1)S(1)}, u32[]{:S(2)}, u32[]{:S(2)}) %collective-permute-start.13) | collective-permute-done | bytes 196640 | tf_op jit(solution)/shard_map/ppermute | solution.py:50
  41.8 0.0 collective-permute-start.14
  41.8 0.0 collective-permute-done.9.refs_12_.refs_11_
  41.8 1.5 %collective-permute-start.16 = (bf16[112,1536]{1,0:T(8,128)(2,1)S(1)}, bf16[112,1536]{1,0:T(8,128)(2,1)S(1)}, u32[]{:S(2)}, u32[]{:S(2)}) collective-permute-start(bf16[112,1536]{1,0:T(8,128)(2,1)S(1)} %get-tuple-element.15.refs_2_), channel_id=1, source_target_pairs={{0,1},{1,0},{2,3},{3,2},{4,5},{5,4},{6,7},{7,6},{8,9},{9,8},{10,11... | collective-permute-start | bytes 1032200 | tf_op jit(solution)/shard_map/ppermute | solution.py:53
  43.3 0.0 collective-permute-done.8.refs_10_.refs_9_
  43.3 0.0 collective-permute-done.11.refs_14_.refs_13_
  43.3 0.0 collective-permute-done.12.refs_16_.refs_15_
  43.3 0.0 collective-permute-done.14.refs_18_.refs_17_
  43.3 4.0 %shard_map.117 = (bf16[128,384]{1,0:T(8,128)(2,1)S(1)}, bf16[128,384]{1,0:T(8,128)(2,1)S(1)}, bf16[128,384]{1,0:T(8,128)(2,1)S(1)}) custom-call(f32[32,128]{1,0:T(8,128)S(1)} %get-tuple-element.13.refs_1_.bias, bf16[384,384]{1,0:T(8,128)(2,1)S(1)} %collective-permute-done.refs_0_, bf16[384,384]{1,0:T(8,128)(2,1)S(1)} %collective-permute-done.1.refs_1_, ...), custom_call_target="tpu_custom_call" | custom-call | flops 1207959552 | bytes 3145728 | tf_op jit(solution)/shard_map/pallas_call | solution.py:172
  47.4 1.5 %collective-permute-start.15 = (bf16[128,384]{1,0:T(8,128)(2,1)S(1)}, bf16[128,384]{1,0:T(8,128)(2,1)S(1)}, u32[]{:S(2)}, u32[]{:S(2)}) collective-permute-start(bf16[128,384]{1,0:T(8,128)(2,1)S(1)} %get-tuple-element.14.refs_0_), channel_id=1, source_target_pairs={{0,8},{2,10},{4,12},{6,14},{8,0},{10,2},{12,4},{14,6},{16,24},{18,... | collective-permute-start | bytes 294920 | tf_op jit(solution)/shard_map/ppermute | solution.py:47
  48.8 1.1 %collective-permute-start.17 = (bf16[128,384]{1,0:T(8,128)(2,1)S(1)}, bf16[128,384]{1,0:T(8,128)(2,1)S(1)}, u32[]{:S(2)}, u32[]{:S(2)}) collective-permute-start(bf16[128,384]{1,0:T(8,128)(2,1)S(1)} %get-tuple-element.16), channel_id=1, source_target_pairs={{0,16},{2,18},{4,20},{6,22},{8,24},{10,26},{12,28},{14,30},{16,0},... | collective-permute-start | bytes 294920 | tf_op jit(solution)/shard_map/ppermute | solution.py:47
  49.9 1.9 %collective-permute-start.18 = (bf16[128,384]{1,0:T(8,128)(2,1)S(1)}, bf16[128,384]{1,0:T(8,128)(2,1)S(1)}, u32[]{:S(2)}, u32[]{:S(2)}) collective-permute-start(bf16[128,384]{1,0:T(8,128)(2,1)S(1)} %get-tuple-element.17), channel_id=1, source_target_pairs={{0,24},{2,26},{4,28},{6,30},{8,16},{10,18},{12,20},{14,22},{16,8},... | collective-permute-start | bytes 294920 | tf_op jit(solution)/shard_map/ppermute | solution.py:47
  51.8 1.7 %shard_map.119.refs_0_ = bf16[128,384]{1,0:T(8,128)(2,1)S(1)} custom-call(f32[32,128]{1,0:T(8,128)S(1)} %get-tuple-element.13.refs_1_.bias, bf16[128,384]{1,0:T(8,128)(2,1)S(1)} %get-tuple-element.14.refs_0_, bf16[128,384]{1,0:T(8,128)(2,1)S(1)} %get-tuple-element.24.refs_1_, bf16[256,384]{1,0:T(8,128)(2,1)S(1)} %pad_maximum_fusion.3.refs_3_.refs_2_, ...), custom_call_target="tpu_custom_call" | custom-call | flops 402653184 | bytes 3145728 | tf_op jit(solution)/shard_map/pallas_call | solution.py:172
  53.5 0.0 copy-done
  53.5 0.0 copy-start.2
  53.5 0.0 copy-start.4
  53.6 0.0 copy-start.5
  53.6 0.6 shard_map.120.refs_4_
  54.2 0.0 collective-permute-done.16.refs_1_.refs_3_
  54.2 0.0 collective-permute-done.15.refs_0_
  54.2 5.3 %collective-permute-done.17.refs_1_ = bf16[128,384]{1,0:T(8,128)(2,1)S(1)} collective-permute-done((bf16[128,384]{1,0:T(8,128)(2,1)S(1)}, bf16[128,384]{1,0:T(8,128)(2,1)S(1)}, u32[]{:S(2)}, u32[]{:S(2)}) %collective-permute-start.17) | collective-permute-done | bytes 98336 | tf_op jit(solution)/shard_map/ppermute | solution.py:47
  59.4 0.0 collective-permute-done.18.refs_2_
  59.5 1.7 %shard_map.121 = (f32[64,3072]{1,0:T(8,128)S(1)}, bf16[64,3072]{1,0:T(8,128)(2,1)S(1)}) custom-call(bf16[128,384]{1,0:T(8,128)(2,1)S(1)} %shard_map.118.refs_0_, bf16[128,384]{1,0:T(8,128)(2,1)S(1)} %collective-permute-done.17.refs_1_, bf16[128,384]{1,0:T(8,128)(2,1)S(1)} %collective-permute-done.18.refs_2_, bf16[1536,3072]{1,0:T(8,128)(2,1)S(1)} %copy-done, ...), custom_call_target="tpu_custom_call" | custom-call | flops 1 | bytes 1 | tf_op jit(solution)/shard_map/pallas_call | solution.py:217
  61.1 1.6 %collective-permute-start.19 = (bf16[64,3072]{1,0:T(8,128)(2,1)S(1)}, bf16[64,3072]{1,0:T(8,128)(2,1)S(1)}, u32[]{:S(2)}, u32[]{:S(2)}) collective-permute-start(bf16[64,3072]{1,0:T(8,128)(2,1)S(1)} %get-tuple-element.19), channel_id=1, source_target_pairs={{0,1},{1,0},{2,3},{3,2},{4,5},{5,4},{6,7},{7,6},{8,9},{9,8},{10,11... | collective-permute-start | bytes 1179656 | tf_op jit(solution)/shard_map/ppermute | solution.py:53
  62.7 7.9 %collective-permute-done.19.refs_1_ = bf16[64,3072]{1,0:T(8,128)(2,1)S(1)} collective-permute-done((bf16[64,3072]{1,0:T(8,128)(2,1)S(1)}, bf16[64,3072]{1,0:T(8,128)(2,1)S(1)}, u32[]{:S(2)}, u32[]{:S(2)}) %collective-permute-start.19) | collective-permute-done | bytes 393248 | tf_op jit(solution)/shard_map/ppermute | solution.py:53
  70.7 1.0 %shard_map.122 = (f32[32,128]{1,0:T(8,128)S(1)}, f32[32,128]{1,0:T(8,128)S(1)}) custom-call(s32[8]{0:T(128)S(1)} %copy-done.4, s32[9]{0:T(128)S(1)} %copy-done.5, f32[64,3072]{1,0:T(8,128)S(1)} %get-tuple-element.18.refs_0_, bf16[64,3072]{1,0:T(8,128)(2,1)S(1)} %collective-permute-done.19.refs_1_, bf16[112,1536]{1,0:T(8,128)(2,1)S(1)} %get-tuple-element.15.refs_2_, ...), custom_call_target="tpu_custom_call" | custom-call | tf_op jit(solution)/shard_map/pallas_call | solution.py:267
  71.6 2.2 %collective-permute-start.21 = (f32[32,128]{1,0:T(8,128)S(1)}, f32[32,128]{1,0:T(8,128)S(1)}, u32[]{:S(2)}, u32[]{:S(2)}) collective-permute-start(f32[32,128]{1,0:T(8,128)S(1)} %get-tuple-element.20), channel_id=1, source_target_pairs={{0,5},{1,4},{2,7},{3,6},{4,9},{5,8},{6,11},{7,10},{8,13},{9,12},{1... | collective-permute-start | bytes 49160 | tf_op jit(solution)/shard_map/ppermute | solution.py:61
  73.9 2.6 %collective-permute-start.20 = (f32[32,128]{1,0:T(8,128)S(1)}, f32[32,128]{1,0:T(8,128)S(1)}, u32[]{:S(2)}, u32[]{:S(2)}) collective-permute-start(f32[32,128]{1,0:T(8,128)S(1)} %get-tuple-element.20), channel_id=1, source_target_pairs={{0,4},{1,5},{2,6},{3,7},{4,8},{5,9},{6,10},{7,11},{8,12},{9,13},{1... | collective-permute-start | bytes 49160 | tf_op jit(solution)/shard_map/ppermute | solution.py:61
  76.5 0.7 collective-permute-start.22
  77.3 1.8 %collective-permute-done.21.refs_1_ = f32[32,128]{1,0:T(8,128)S(1)} collective-permute-done((f32[32,128]{1,0:T(8,128)S(1)}, f32[32,128]{1,0:T(8,128)S(1)}, u32[]{:S(2)}, u32[]{:S(2)}) %collective-permute-start.21) | collective-permute-done | bytes 16416 | tf_op jit(solution)/shard_map/ppermute | solution.py:61
  79.0 1.3 %collective-permute-done.20.refs_0_ = f32[32,128]{1,0:T(8,128)S(1)} collective-permute-done((f32[32,128]{1,0:T(8,128)S(1)}, f32[32,128]{1,0:T(8,128)S(1)}, u32[]{:S(2)}, u32[]{:S(2)}) %collective-permute-start.20) | collective-permute-done | bytes 16416 | tf_op jit(solution)/shard_map/ppermute | solution.py:61
  80.3 0.0 collective-permute-done.22.refs_3_
  80.3 0.6 shard_map.123
  (15 shorter events, 0.2 us)
Async XLA Ops:
  0.7 52.9 %copy-start = (bf16[1536,3072]{1,0:T(8,128)(2,1)S(1)}, bf16[1536,3072]{1,0:T(8,128)(2,1)}, u32[]{:S(2)}) copy-start(bf16[1536,3072]{1,0:T(8,128)(2,1)} %refs_3_.1) | copy-start | bytes 28311556
  3.5 22.1 %collective-permute-start = (bf16[384,384]{1,0:T(8,128)(2,1)S(1)}, bf16[384,384]{1,0:T(8,128)(2,1)S(1)}, u32[]{:S(2)}, u32[]{:S(2)}) collective-permute-start(bf16[384,384]{1,0:T(8,128)(2,1)S(1)} %pad_maximum_fusion), channel_id=1, source_target_pairs={{0,8},{2,10},{4,12},{6,14},{8,0},{10,2},{12,4},{14,6},{16,24},{18,... | collective-permute-start | bytes 884744 | tf_op jit(solution)/shard_map/ppermute | solution.py:47
  6.6 15.8 %collective-permute-start.1 = (bf16[384,384]{1,0:T(8,128)(2,1)S(1)}, bf16[384,384]{1,0:T(8,128)(2,1)S(1)}, u32[]{:S(2)}, u32[]{:S(2)}) collective-permute-start(bf16[384,384]{1,0:T(8,128)(2,1)S(1)} %pad_maximum_fusion.1), channel_id=1, source_target_pairs={{0,16},{2,18},{4,20},{6,22},{8,24},{10,26},{12,28},{14,30},{16,0},... | collective-permute-start | bytes 884744 | tf_op jit(solution)/shard_map/ppermute | solution.py:47
  9.3 6.1 %collective-permute-start.2 = (bf16[256,384]{1,0:T(8,128)(2,1)S(1)}, bf16[256,384]{1,0:T(8,128)(2,1)S(1)}, u32[]{:S(2)}, u32[]{:S(2)}) collective-permute-start(bf16[256,384]{1,0:T(8,128)(2,1)S(1)} %pad_maximum_fusion.3.refs_3_.refs_2_), channel_id=1, source_target_pairs={{0,4},{2,6},{4,0},{6,2},{8,12},{10,14},{12,8},{14,10},{16,20},{18,... | collective-permute-start | bytes 589832 | tf_op jit(solution)/shard_map/ppermute | solution.py:50
  22.4 8.6 %collective-permute-start.3 = (bf16[384,384]{1,0:T(8,128)(2,1)S(1)}, bf16[384,384]{1,0:T(8,128)(2,1)S(1)}, u32[]{:S(2)}, u32[]{:S(2)}) collective-permute-start(bf16[384,384]{1,0:T(8,128)(2,1)S(1)} %shard_map.114), channel_id=1, source_target_pairs={{0,24},{2,26},{4,28},{6,30},{8,16},{10,18},{12,20},{14,22},{16,8},... | collective-permute-start | bytes 884744 | tf_op jit(solution)/shard_map/ppermute | solution.py:47
  25.6 5.9 %collective-permute-start.7 = (bf16[256,384]{1,0:T(8,128)(2,1)S(1)}, bf16[256,384]{1,0:T(8,128)(2,1)S(1)}, u32[]{:S(2)}, u32[]{:S(2)}) collective-permute-start(bf16[256,384]{1,0:T(8,128)(2,1)S(1)} %slice.12.refs_7_.refs_6_), channel_id=1, source_target_pairs={{0,4},{2,6},{4,0},{6,2},{8,12},{10,14},{12,8},{14,10},{16,20},{18,... | collective-permute-start | bytes 589832 | tf_op jit(solution)/shard_map/ppermute | solution.py:50
  27.2 0.9 %copy-start.1 = (bf16[1536,64]{0,1:T(8,128)(2,1)S(1)}, bf16[1536,64]{0,1:T(8,128)(2,1)}, u32[]{:S(2)}) copy-start(bf16[1536,64]{0,1:T(8,128)(2,1)} %param.16) | copy-start | bytes 589828
  28.2 0.7 copy-start.3
  29.5 6.6 %collective-permute-start.10 = (bf16[256,384]{1,0:T(8,128)(2,1)S(1)}, bf16[256,384]{1,0:T(8,128)(2,1)S(1)}, u32[]{:S(2)}, u32[]{:S(2)}) collective-permute-start(bf16[256,384]{1,0:T(8,128)(2,1)S(1)} %shard_map.115.refs_11_.refs_10_), channel_id=1, source_target_pairs={{0,4},{2,6},{4,0},{6,2},{8,12},{10,14},{12,8},{14,10},{16,20},{18,... | collective-permute-start | bytes 589832 | tf_op jit(solution)/shard_map/ppermute | solution.py:50
  30.1 6.1 %collective-permute-start.4 = (bf16[256,384]{1,0:T(8,128)(2,1)S(1)}, bf16[256,384]{1,0:T(8,128)(2,1)S(1)}, u32[]{:S(2)}, u32[]{:S(2)}) collective-permute-start(bf16[256,384]{1,0:T(8,128)(2,1)S(1)} %pad_maximum_fusion.3.refs_3_.refs_2_), channel_id=1, source_target_pairs={{0,2},{2,0},{4,6},{6,4},{8,10},{10,8},{12,14},{14,12},{16,18},{18,... | collective-permute-start | bytes 589832 | tf_op jit(solution)/shard_map/ppermute | solution.py:50
  30.1 6.6 %collective-permute-start.5 = (bf16[256,384]{1,0:T(8,128)(2,1)S(1)}, bf16[256,384]{1,0:T(8,128)(2,1)S(1)}, u32[]{:S(2)}, u32[]{:S(2)}) collective-permute-start(bf16[256,384]{1,0:T(8,128)(2,1)S(1)} %collective-permute-done.2.refs_2_.refs_5_.refs_4_), channel_id=1, source_target_pairs={{0,2},{2,0},{4,6},{6,4},{8,10},{10,8},{12,14},{14,12},{16,18},{18,... | collective-permute-start | bytes 589832 | tf_op jit(solution)/shard_map/ppermute | solution.py:50
  31.1 5.7 %collective-permute-start.6 = (bf16[256,384]{1,0:T(8,128)(2,1)S(1)}, bf16[256,384]{1,0:T(8,128)(2,1)S(1)}, u32[]{:S(2)}, u32[]{:S(2)}) collective-permute-start(bf16[256,384]{1,0:T(8,128)(2,1)S(1)} %slice.12.refs_7_.refs_6_), channel_id=1, source_target_pairs={{0,2},{2,0},{4,6},{6,4},{8,10},{10,8},{12,14},{14,12},{16,18},{18,... | collective-permute-start | bytes 589832 | tf_op jit(solution)/shard_map/ppermute | solution.py:50
  36.1 5.7 %collective-permute-start.13 = (bf16[256,384]{1,0:T(8,128)(2,1)S(1)}, bf16[256,384]{1,0:T(8,128)(2,1)S(1)}, u32[]{:S(2)}, u32[]{:S(2)}) collective-permute-start(bf16[256,384]{1,0:T(8,128)(2,1)S(1)} %shard_map.116.refs_15_.refs_14_), channel_id=1, source_target_pairs={{0,4},{2,6},{4,0},{6,2},{8,12},{10,14},{12,8},{14,10},{16,20},{18,... | collective-permute-start | bytes 589832 | tf_op jit(solution)/shard_map/ppermute | solution.py:50
  36.1 5.7 %collective-permute-start.9 = (bf16[256,384]{1,0:T(8,128)(2,1)S(1)}, bf16[256,384]{1,0:T(8,128)(2,1)S(1)}, u32[]{:S(2)}, u32[]{:S(2)}) collective-permute-start(bf16[256,384]{1,0:T(8,128)(2,1)S(1)} %shard_map.115.refs_11_.refs_10_), channel_id=1, source_target_pairs={{0,2},{2,0},{4,6},{6,4},{8,10},{10,8},{12,14},{14,12},{16,18},{18,... | collective-permute-start | bytes 589832 | tf_op jit(solution)/shard_map/ppermute | solution.py:50
  36.1 7.2 %collective-permute-start.8 = (bf16[256,384]{1,0:T(8,128)(2,1)S(1)}, bf16[256,384]{1,0:T(8,128)(2,1)S(1)}, u32[]{:S(2)}, u32[]{:S(2)}) collective-permute-start(bf16[256,384]{1,0:T(8,128)(2,1)S(1)} %collective-permute-done.7.refs_1_.refs_9_.refs_8_), channel_id=1, source_target_pairs={{0,2},{2,0},{4,6},{6,4},{8,10},{10,8},{12,14},{14,12},{16,18},{18,... | collective-permute-start | bytes 589832 | tf_op jit(solution)/shard_map/ppermute | solution.py:50
  36.7 6.7 %collective-permute-start.11 = (bf16[256,384]{1,0:T(8,128)(2,1)S(1)}, bf16[256,384]{1,0:T(8,128)(2,1)S(1)}, u32[]{:S(2)}, u32[]{:S(2)}) collective-permute-start(bf16[256,384]{1,0:T(8,128)(2,1)S(1)} %collective-permute-done.10.refs_2_.refs_13_.refs_12_), channel_id=1, source_target_pairs={{0,2},{2,0},{4,6},{6,4},{8,10},{10,8},{12,14},{14,12},{16,18},{18,... | collective-permute-start | bytes 589832 | tf_op jit(solution)/shard_map/ppermute | solution.py:50
  36.7 6.6 %collective-permute-start.12 = (bf16[256,384]{1,0:T(8,128)(2,1)S(1)}, bf16[256,384]{1,0:T(8,128)(2,1)S(1)}, u32[]{:S(2)}, u32[]{:S(2)}) collective-permute-start(bf16[256,384]{1,0:T(8,128)(2,1)S(1)} %shard_map.116.refs_15_.refs_14_), channel_id=1, source_target_pairs={{0,2},{2,0},{4,6},{6,4},{8,10},{10,8},{12,14},{14,12},{16,18},{18,... | collective-permute-start | bytes 589832 | tf_op jit(solution)/shard_map/ppermute | solution.py:50
  41.8 1.5 %collective-permute-start.14 = (bf16[256,384]{1,0:T(8,128)(2,1)S(1)}, bf16[256,384]{1,0:T(8,128)(2,1)S(1)}, u32[]{:S(2)}, u32[]{:S(2)}) collective-permute-start(bf16[256,384]{1,0:T(8,128)(2,1)S(1)} %collective-permute-done.13.refs_17_.refs_16_), channel_id=1, source_target_pairs={{0,2},{2,0},{4,6},{6,4},{8,10},{10,8},{12,14},{14,12},{16,18},{18,... | collective-permute-start | bytes 589832 | tf_op jit(solution)/shard_map/ppermute | solution.py:50
  41.8 12.4 %collective-permute-start.16 = (bf16[112,1536]{1,0:T(8,128)(2,1)S(1)}, bf16[112,1536]{1,0:T(8,128)(2,1)S(1)}, u32[]{:S(2)}, u32[]{:S(2)}) collective-permute-start(bf16[112,1536]{1,0:T(8,128)(2,1)S(1)} %get-tuple-element.15.refs_2_), channel_id=1, source_target_pairs={{0,1},{1,0},{2,3},{3,2},{4,5},{5,4},{6,7},{7,6},{8,9},{9,8},{10,11... | collective-permute-start | bytes 1032200 | tf_op jit(solution)/shard_map/ppermute | solution.py:53
  47.4 6.8 %collective-permute-start.15 = (bf16[128,384]{1,0:T(8,128)(2,1)S(1)}, bf16[128,384]{1,0:T(8,128)(2,1)S(1)}, u32[]{:S(2)}, u32[]{:S(2)}) collective-permute-start(bf16[128,384]{1,0:T(8,128)(2,1)S(1)} %get-tuple-element.14.refs_0_), channel_id=1, source_target_pairs={{0,8},{2,10},{4,12},{6,14},{8,0},{10,2},{12,4},{14,6},{16,24},{18,... | collective-permute-start | bytes 294920 | tf_op jit(solution)/shard_map/ppermute | solution.py:47
  48.8 10.6 %collective-permute-start.17 = (bf16[128,384]{1,0:T(8,128)(2,1)S(1)}, bf16[128,384]{1,0:T(8,128)(2,1)S(1)}, u32[]{:S(2)}, u32[]{:S(2)}) collective-permute-start(bf16[128,384]{1,0:T(8,128)(2,1)S(1)} %get-tuple-element.16), channel_id=1, source_target_pairs={{0,16},{2,18},{4,20},{6,22},{8,24},{10,26},{12,28},{14,30},{16,0},... | collective-permute-start | bytes 294920 | tf_op jit(solution)/shard_map/ppermute | solution.py:47
  49.9 9.5 %collective-permute-start.18 = (bf16[128,384]{1,0:T(8,128)(2,1)S(1)}, bf16[128,384]{1,0:T(8,128)(2,1)S(1)}, u32[]{:S(2)}, u32[]{:S(2)}) collective-permute-start(bf16[128,384]{1,0:T(8,128)(2,1)S(1)} %get-tuple-element.17), channel_id=1, source_target_pairs={{0,24},{2,26},{4,28},{6,30},{8,16},{10,18},{12,20},{14,22},{16,8},... | collective-permute-start | bytes 294920 | tf_op jit(solution)/shard_map/ppermute | solution.py:47
  53.5 17.1 %copy-start.2 = (f32[64,128]{1,0:T(8,128)S(1)}, f32[64,128]{1,0:T(8,128)}, u32[]{:S(2)}) copy-start(f32[64,128]{1,0:T(8,128)} %refs_4_.1) | copy-start | bytes 98308
  53.5 17.1 %copy-start.4 = (s32[8]{0:T(128)S(1)}, s32[8]{0:T(128)}, u32[]{:S(2)}) copy-start(s32[8]{0:T(128)} %levels.1) | copy-start | bytes 100
  53.6 17.1 %copy-start.5 = (s32[9]{0:T(128)S(1)}, s32[9]{0:T(128)}, u32[]{:S(2)}) copy-start(s32[9]{0:T(128)} %timesteps.1) | copy-start | bytes 112
  61.1 9.5 %collective-permute-start.19 = (bf16[64,3072]{1,0:T(8,128)(2,1)S(1)}, bf16[64,3072]{1,0:T(8,128)(2,1)S(1)}, u32[]{:S(2)}, u32[]{:S(2)}) collective-permute-start(bf16[64,3072]{1,0:T(8,128)(2,1)S(1)} %get-tuple-element.19), channel_id=1, source_target_pairs={{0,1},{1,0},{2,3},{3,2},{4,5},{5,4},{6,7},{7,6},{8,9},{9,8},{10,11... | collective-permute-start | bytes 1179656 | tf_op jit(solution)/shard_map/ppermute | solution.py:53
  71.6 7.4 %collective-permute-start.21 = (f32[32,128]{1,0:T(8,128)S(1)}, f32[32,128]{1,0:T(8,128)S(1)}, u32[]{:S(2)}, u32[]{:S(2)}) collective-permute-start(f32[32,128]{1,0:T(8,128)S(1)} %get-tuple-element.20), channel_id=1, source_target_pairs={{0,5},{1,4},{2,7},{3,6},{4,9},{5,8},{6,11},{7,10},{8,13},{9,12},{1... | collective-permute-start | bytes 49160 | tf_op jit(solution)/shard_map/ppermute | solution.py:61
  73.9 6.4 %collective-permute-start.20 = (f32[32,128]{1,0:T(8,128)S(1)}, f32[32,128]{1,0:T(8,128)S(1)}, u32[]{:S(2)}, u32[]{:S(2)}) collective-permute-start(f32[32,128]{1,0:T(8,128)S(1)} %get-tuple-element.20), channel_id=1, source_target_pairs={{0,4},{1,5},{2,6},{3,7},{4,8},{5,9},{6,10},{7,11},{8,12},{9,13},{1... | collective-permute-start | bytes 49160 | tf_op jit(solution)/shard_map/ppermute | solution.py:61
  76.5 3.8 %collective-permute-start.22 = (f32[32,128]{1,0:T(8,128)S(1)}, f32[32,128]{1,0:T(8,128)S(1)}, u32[]{:S(2)}, u32[]{:S(2)}) collective-permute-start(f32[32,128]{1,0:T(8,128)S(1)} %get-tuple-element.21.refs_2_), channel_id=1, source_target_pairs={{0,1},{1,0},{2,3},{3,2},{4,5},{5,4},{6,7},{7,6},{8,9},{9,8},{10,11... | collective-permute-start | bytes 49160 | tf_op jit(solution)/shard_map/ppermute | solution.py:53

commit v3 on v2

--- a/solution.py
+++ b/solution.py
@@ -39,6 +39,10 @@
         self.per = 2 if self.span % 2 == 0 and self.members % 2 == 0 else 1
         self.blocks = self.sections // self.per
 
+    def row_starts(self):
+        tensor = lax.axis_index("tensor")
+        return [(tensor ^ step) * self.share for step in [*range(1, self.tensors), 0]]
+
     def part(self):
         return lax.axis_index("section") // self.members
 
@@ -123,106 +127,113 @@
     )(order, gain, head_weight, *after)
 
 
-def attend_kernel(plan, steps, waits, bias, *refs):
+def attend_kernel(plan, blocks, begun, last, bias, *refs):
     rows = plan.rows
-    refs = refs[waits:]
-    queries, refs = refs[: len(steps)], refs[len(steps) :]
-    pieces, refs = refs[: plan.sections], refs[plan.sections :]
-    outs, scores = refs[: len(steps)], refs[len(steps)]
+    before, refs = (refs[:3], refs[3:]) if begun else (None, refs)
+    queries, refs = refs[: plan.split], refs[plan.split :]
+    pieces, refs = refs[: len(blocks) * plan.per], refs[len(blocks) * plan.per :]
+    outs, scores = refs[:-1], refs[-1]
     factor = math.log2(math.e) / math.sqrt(HD)
-    many = len(steps) * rows
     width = plan.per * rows
 
     def hidden(j):
-        at = [step * plan.blocks + j for step in steps]
+        at = [step * plan.blocks + j for step in range(plan.split)]
         return jnp.concatenate([jnp.broadcast_to(bias[pl.ds(i, 1), :], (rows, HD)) for i in at], axis=0)
 
-    def block(j, which, lanes):
-        parts = pieces[j * plan.per : (j + 1) * plan.per]
+    def block(at, which, lanes):
+        parts = pieces[at * plan.per : (at + 1) * plan.per]
         return jnp.concatenate([ref[pl.ds(which * rows, rows), lanes] for ref in parts], axis=0)
 
     for h in range(plan.cols // HD):
         lanes = pl.ds(h * HD, HD)
-        q = [ref[pl.ds(ref.shape[0] - rows, rows), lanes] for ref in queries]
+        q = [
+            ref[pl.ds(pl.multiple_of(ref.shape[0] - rows + start, 16), plan.share), lanes]
+            for ref in queries
+            for start in plan.row_starts()
+        ]
         q = jnp.concatenate(q, axis=0)
-        top = None
-        for j in range(plan.blocks):
-            s = lax.dot_general(q, block(j, 0, lanes), (((1,), (1,)), ((), ())), preferred_element_type=jnp.float32)
-            scores[:, pl.ds(j * width, width)] = s
+        top = before[0][h] if begun else None
+        for at, j in enumerate(blocks):
+            s = lax.dot_general(q, block(at, 0, lanes), (((1,), (1,)), ((), ())), preferred_element_type=jnp.float32)
+            scores[:, pl.ds(at * width, width)] = s
             s = functools.reduce(jnp.maximum, [s[:, i : i + HD] for i in range(0, width, HD)])
             s = s + hidden(j)
             top = s if top is None else jnp.maximum(top, s)
         top = jnp.broadcast_to(jnp.max(top, axis=1, keepdims=True), top.shape)
-        total = jnp.zeros((many, HD), jnp.float32)
-        summed = jnp.zeros((many, HD), jnp.float32)
-        for j in range(plan.blocks):
+        if begun:
+            kept = jnp.exp2((before[0][h] - top) * factor)
+            total, summed = kept * before[1][h], kept * before[2][h]
+        else:
+            total = summed = jnp.zeros(top.shape, jnp.float32)
+        for at, j in enumerate(blocks):
             base = top - hidden(j)
-            w = [scores[:, pl.ds(j * width + i, HD)] for i in range(0, width, HD)]
+            w = [scores[:, pl.ds(at * width + i, HD)] for i in range(0, width, HD)]
             w = [jnp.exp2((s - base) * factor) for s in w]
             total += functools.reduce(jnp.add, w)
             w = jnp.concatenate(w, axis=1).astype(jnp.bfloat16)
-            summed += jnp.dot(w, block(j, 1, lanes), preferred_element_type=jnp.float32)
-        out = (summed / jnp.sum(total, axis=1, keepdims=True)).astype(jnp.bfloat16)
-        for i, ref in enumerate(outs):
-            ref[:, lanes] = out[i * rows : (i + 1) * rows]
-
-
-def attend(plan, steps, bias, queries, pieces, after=()):
-    keys = plan.sections * plan.rows
-    return pl.pallas_call(
-        functools.partial(attend_kernel, plan, steps, len(after)),
-        out_shape=[struct((plan.rows, plan.cols), jnp.bfloat16)] * len(steps),
-        in_specs=[VMEM] + [ANY] * len(after) + [VMEM] * (len(steps) + len(pieces)),
-        out_specs=[VMEM] * len(steps),
-        scratch_shapes=[pltpu.VMEM((len(steps) * plan.rows, keys), jnp.float32)],
+            summed += jnp.dot(w, block(at, 1, lanes), preferred_element_type=jnp.float32)
+        if last:
+            out = (summed / jnp.sum(total, axis=1, keepdims=True)).astype(jnp.bfloat16)
+            others = rows - plan.share
+            for i, (away, kept) in enumerate(zip(outs[: plan.split], outs[plan.split :])):
+                away[:, lanes] = out[i * rows : i * rows + others]
+                kept[:, lanes] = out[i * rows + others : (i + 1) * rows]
+        else:
+            outs[0][h], outs[1][h], outs[2][h] = top, total, summed
+
+
+def attend(plan, blocks, bias, queries, pieces, state=(), last=False):
+    many = plan.split * plan.rows
+    shapes = [struct((plan.cols // HD, many, HD), jnp.float32)] * 3
+    if last:
+        shapes = [struct((plan.rows - plan.share, plan.cols), jnp.bfloat16)] * plan.split
+        shapes += [struct((plan.share, plan.cols), jnp.bfloat16)] * plan.split
+    pieces = [p for j in blocks for p in pieces[j]]
+    out = pl.pallas_call(
+        functools.partial(attend_kernel, plan, blocks, bool(state), last),
+        out_shape=shapes,
+        in_specs=[VMEM] * (1 + len(state) + plan.split + len(pieces)),
+        out_specs=[VMEM] * len(shapes),
+        scratch_shapes=[pltpu.VMEM((many, len(pieces) * plan.rows), jnp.float32)],
         compiler_params=params(12),
         cost_estimate=pl.CostEstimate(
-            flops=4 * len(steps) * plan.rows * keys * plan.cols,
-            bytes_accessed=4 * keys * plan.cols,
-            transcendentals=len(steps) * plan.rows * keys * plan.cols // HD,
+            flops=16 * many * len(pieces) * plan.rows * plan.cols, bytes_accessed=0, transcendentals=0
         ),
-    )(bias, *after, *queries, *pieces)
+    )(bias, *state, *queries, *pieces)
+    return list(out)
 
 
 def project_kernel(plan, steps, begun, *refs):
-    parts, weight, refs = refs[: len(steps)], refs[len(steps)], refs[len(steps) + 1 :]
+    count = len(steps)
+    parts, weight, refs = refs[:count], refs[count], refs[count + 1 :]
     outs = refs[1:] if begun else refs
-    part, tensor = plan.part(), lax.axis_index("tensor")
     tile = 512
     for at in range(0, weight.shape[1], tile):
         cols = pl.ds(at, tile)
-        total = refs[0][:, cols] if begun else None
+        total = refs[0][:, cols] if begun else 0.0
         for step, ref in zip(steps, parts):
-            here = pl.ds(pl.multiple_of((part ^ step) * plan.cols, 128), plan.cols)
-            term = jnp.dot(ref[...], weight[here, cols], preferred_element_type=jnp.float32)
-            total = term if total is None else total + term
-        if not begun:
-            outs[0][:, cols] = total
-        else:
-            full = outs[-1]
-            full[...] = total
-            for step, out in enumerate(outs[:-1]):
-                here = pl.ds(pl.multiple_of((tensor ^ step) * plan.share, 8), plan.share)
-                out[:, cols] = full[here, :].astype(out.dtype)
-
-
-def project(plan, steps, parts, weight, begun=None):
-    width = weight.shape[1]
-    if begun is None:
-        shapes, scratch, extra = struct((plan.rows, width), jnp.float32), [], ()
-    else:
-        shapes = [struct((plan.share, width), jnp.float32)]
-        shapes += [struct((plan.share, width), jnp.bfloat16)] * (plan.tensors - 1)
-        scratch, extra = [pltpu.VMEM((plan.rows, 512), jnp.float32)], (begun,)
-    return pl.pallas_call(
-        functools.partial(project_kernel, plan, steps, begun is not None),
+            here = pl.ds(pl.multiple_of((plan.part() ^ step) * plan.cols, 128), plan.cols)
+            total += jnp.dot(ref[...], weight[here, cols], preferred_element_type=jnp.float32)
+        rows = total.shape[0] // len(outs)
+        for i, out in enumerate(outs):
+            out[:, cols] = total[i * rows : (i + 1) * rows].astype(out.dtype)
+
+
+def project(plan, steps, parts, weight, begun=None, split=False):
+    rows, width = parts[0].shape[0], weight.shape[1]
+    extra = () if begun is None else (begun,)
+    shapes = [struct((rows, width), jnp.float32)]
+    if split:
+        shapes = [struct((plan.share, width), jnp.bfloat16)] * (rows // plan.share)
+    out = pl.pallas_call(
+        functools.partial(project_kernel, plan, steps, bool(extra)),
         out_shape=shapes,
         in_specs=[VMEM] * (len(parts) + 1 + len(extra)),
-        out_specs=VMEM if begun is None else [VMEM] * plan.tensors,
-        scratch_shapes=scratch,
-        compiler_params=params(16),
-        cost_estimate=pl.CostEstimate(flops=1, bytes_accessed=1, transcendentals=0),
+        out_specs=[VMEM] * len(shapes),
+        compiler_params=params(8),
+        cost_estimate=pl.CostEstimate(flops=0, bytes_accessed=0, transcendentals=0),
     )(*parts, weight, *extra)
+    return list(out) if split else out[0]
 
 
 def head_kernel(plan, levels, timesteps, *refs):
@@ -306,34 +317,44 @@
     if split == 4 and plan.members == 4:
         two = plan.to_part(pack(plan, 2, keys, values, queries), 2)
         one = plan.to_part(pack(plan, 1, keys, values, queries), 1)
-        shared, bias = ready(plan, order, gain[None, :], head_weight.T, [one])
         own = plan.gather_members(own)
+        shared, bias = ready(plan, order, gain[None, :], head_weight.T, [own[2]])
+        shared = [shared] + [plan.to_tensor(shared, i) for i in range(1, tensors)]
         ones = plan.gather_members(one[: 2 * plan.rows])
-        three = pack(plan, 3, keys, values, queries)
-        gate = [two, own[2]]
-        three = plan.to_part(held([three], gate)[0] if gate else three, 3)
+        (three,) = held([pack(plan, 3, keys, values, queries)], [two, own[2], bias])
+        three = plan.to_part(three, 3)
         asked += [one, two, three]
-        twos = plan.gather_members(*held([two[: 2 * plan.rows]], [bias]))
-        threes = plan.gather_members(*held([three[: 2 * plan.rows]], [ones[2], twos[2]]))
-        pieces = own + ones + twos + threes
+        twos = plan.gather_members(*held([two[: 2 * plan.rows]], []))
+        threes = [*held([three[: 2 * plan.rows]], [ones[2], twos[2]])]
+        threes += [plan.to_member(threes[0], i) for i in (1, 2)]
+        pairs = [v[i : i + 2] for v in (own, ones, twos) for i in (0, 2)]
+        pairs.append(threes[:2])
+        state = attend(plan, [0, 2, 4, 6, 1, 3], bias, asked, pairs)
+        (last,) = held(threes[2:], [state[0]])
+        pairs.append([last, plan.to_member(last, 1)])
+        attended = attend(plan, [5, 7], bias, asked, pairs, state, True)
     else:
         shared, bias = ready(plan, order, gain[None, :], head_weight.T, [])
+        shared = [shared] + [plan.to_tensor(shared, i) for i in range(1, tensors)]
         sent = [own] + [plan.to_part(pack(plan, i, keys, values), i) for i in far]
         asked += [plan.to_part(pack(plan, i, queries), i) for i in far]
         pieces = [p for v in sent for p in plan.gather_members(v)]
-    shared = [shared] + [plan.to_tensor(shared, i) for i in range(1, tensors)]
-
-    attended = [None] * split
-    done = []
-    if far:
-        done = attend(plan, far, bias, [asked[i] for i in far], pieces)
-        attended[1:] = [plan.to_part(v, i) for i, v in zip(far, done)]
-    (attended[0],) = attend(plan, near, bias, asked[:1], pieces, done[:1])
-    sums = project(plan, near, attended[:1], out_weight)
-    if far:
-        attended[1:2] = held(attended[1:2], shared[1:])
-    sums = project(plan, far, attended[1:], out_weight, sums)
-    sums = [sums[0]] + [plan.to_tensor(sums[i], i) for i in range(1, tensors)]
+        pairs = [pieces[i : i + plan.per] for i in range(0, len(pieces), plan.per)]
+        blocks = list(range(plan.blocks))
+        own_blocks = blocks[:: plan.blocks // split]
+        state = attend(plan, own_blocks, bias, asked, pairs)
+        attended = attend(plan, [j for j in blocks if j not in own_blocks], bias, asked, pairs, state, True)
+
+    away, kept = attended[:split], attended[split:]
+    away = [plan.to_part(v, i) if i else v for i, v in enumerate(away)]
+    rest = far or near
+    begun = project(plan, near, away[:1], out_weight) if far else None
+    away[-1:] = held(away[-1:], shared[1:])
+    away = project(plan, rest, [away[i] for i in rest], out_weight, begun, True)
+    away = [plan.to_tensor(v, i + 1) for i, v in enumerate(away)]
+    kept = [plan.to_part(v, i) if i else v for i, v in enumerate(kept)]
+    begun = project(plan, near, kept[:1], out_weight) if far else None
+    sums = [project(plan, rest, [kept[i] for i in rest], out_weight, begun), *away]
     velocity, moved = head(plan, levels, timesteps, sums, shared, latents)
     advanced = [plan.to_next_group(moved, i) for i in range(tensors)]
     velocities = [velocity] + [plan.to_tensor(velocity, i) for i in range(1, tensors)]

time: 81.2 us -> 78 us (0.961)
  waiting for transfers between devices: 37.9 us -> 29.9 us
  starting transfers between devices: 26.6 us -> 30.8 us
  Pallas kernels: 10.2 us -> 11.4 us
    ppermute x12, waiting for transfers between devices: 14.2 us -> 7.89 us  [to_member(): lax.ppermute(value, 'section', [(s, s ^ step) for s in range(self.section...]
    ppermute x3, waiting for transfers between devices: 7.95 us -> 2.45 us  [to_tensor(): lax.ppermute(value, 'tensor', [(t, t ^ step) for t in range(self.tensors)])]
    ppermute x6 -> x9, starting transfers between devices: 12.7 us -> 18.1 us  [to_part(): return lax.ppermute(value, 'section', pairs)]
    ppermute x2, waiting for transfers between devices: 3.03 us -> 5.44 us  [to_next_group(): return lax.ppermute(value, ('section', 'tensor'), pairs)]
    ppermute x2, starting transfers between devices: 4.88 us -> 2.89 us  [to_next_group(): return lax.ppermute(value, ('section', 'tensor'), pairs)]
    ppermute x6 -> x9, waiting for transfers between devices: 12.7 us -> 14.1 us  [to_part(): return lax.ppermute(value, 'section', pairs)]
    pallas_call x4 -> x6, Pallas kernels: 8 us -> 9.14 us  [the longest x2 5.31 us: attend(): pl.pallas_call(functools.partial(attend_kernel, plan, blocks, bool(state)...]
    ppermute x12, starting transfers between devices: 5.28 us -> 6.31 us  [to_member(): lax.ppermute(value, 'section', [(s, s ^ step) for s in range(self.section...]
  transfers between devices with their start and end apart: 23 -> 26, of which waited for: 10 -> 12; matrix products, arithmetic and copies ran while one was open for 1% -> 1% of each run, Pallas kernels for 9% -> 11%
where the time goes in v3:
time: 78 us; the launch traced here: 77.8 us
  starting transfers between devices  30.8 us (39%)
  waiting for transfers between devices  29.9 us (38%)
  Pallas kernels  11.4 us (15%)
  local copies, waits for them, and re-layouts  4.78 us (6%)
  between operations  0.87 us (1%)
    ppermute x9, starting transfers between devices, to_part(): return lax.ppermute(value, 'section', pairs)  18.1 us
    ppermute x9, waiting for transfers between devices, to_part(): return lax.ppermute(value, 'section', pairs)  14.1 us
    ppermute x12, waiting for transfers between devices, to_member(): lax.ppermute(value, 'section', [(s, s ^ step) for s in range(self.section...  7.89 us
    ppermute x12, starting transfers between devices, to_member(): lax.ppermute(value, 'section', [(s, s ^ step) for s in range(self.section...  6.31 us
    ppermute x2, waiting for transfers between devices, to_next_group(): return lax.ppermute(value, ('section', 'tensor'), pairs)  5.44 us
    pallas_call x2, Pallas kernels, attend(): pl.pallas_call(functools.partial(attend_kernel, plan, blocks, bool(state)...  5.31 us
    pallas_call x4, Pallas kernels, project(): pl.pallas_call(functools.partial(project_kernel, plan, steps, bool(extra)...  3.83 us
    ppermute x3, starting transfers between devices, to_tensor(): lax.ppermute(value, 'tensor', [(t, t ^ step) for t in range(self.tensors)])  3.44 us
  transfers between devices with their start and end apart: 26, of which 12 were waited for; matrix products, arithmetic and copies ran while one was open for 1% of the time, Pallas kernels for 11%

profile of v3, /device:TPU:0, one launch (start us, length us, event | category | flops | bytes accessed | tf_op | source)
XLA Modules:
  0.0 77.8 jit_solution(5554768613246086991)
XLA Ops:
  0.7 1.1 %constant_dynamic-slice_fusion = (bf16[128,384]{1,0:T(8,128)(2,1)S(1)}, bf16[128,384]{1,0:T(8,128)(2,1)S(1)}, bf16[128,384]{1,0:T(8,128)(2,1)S(1)}, bf16[128,384]{1,0:T(8,128)(2,1)S(1)}) fusion(bf16[128,1536]{1,0:T(8,128)(2,1)} %param.10, s32[]{:T(128)S(6)} %select_n.33, s32[]{:T(128)S(6)} %select_n.31, s32[]{:T(128)S(6)} %select_n.30, s32[]{:T(128)S(6)} %select_n.32), kind=kLoop, calls=%fused_computation.4 | loop fusion | bytes 786448 | tf_op jit(solution)/shard_map/dynamic_slice | solution.py:78
  1.8 1.3 %constant_dynamic-slice_fusion.1 = (bf16[128,384]{1,0:T(8,128)(2,1)S(1)}, bf16[128,384]{1,0:T(8,128)(2,1)S(1)}, bf16[128,384]{1,0:T(8,128)(2,1)S(1)}, bf16[128,3...) fusion(bf16[128,1536]{1,0:T(8,128)(2,1)} %param.12, ...), kind=kLoop, calls=%fused_computation.5 | loop fusion | bytes 1572880 | tf_op jit(solution)/shard_map/dynamic_slice | solution.py:78
  3.1 4.1 %collective-permute-start.2 = (bf16[384,384]{1,0:T(8,128)(2,1)S(1)}, bf16[384,384]{1,0:T(8,128)(2,1)S(1)}, u32[]{:S(2)}, u32[]{:S(2)}) collective-permute-start(bf16[384,384]{1,0:T(8,128)(2,1)S(1)} %pad_maximum_fusion.1), channel_id=1, source_target_pairs={{0,16},{2,18},{4,20},{6,22},{8,24},{10,26},{12,28},{14,30},{16,0},... | collective-permute-start | bytes 884744 | tf_op jit(solution)/shard_map/ppermute | solution.py:51
  7.2 1.6 %collective-permute-start = (bf16[256,384]{1,0:T(8,128)(2,1)S(1)}, bf16[256,384]{1,0:T(8,128)(2,1)S(1)}, u32[]{:S(2)}, u32[]{:S(2)}) collective-permute-start(bf16[256,384]{1,0:T(8,128)(2,1)S(1)} %pad_maximum_fusion.3.refs_4_), channel_id=1, source_target_pairs={{0,4},{2,6},{4,0},{6,2},{8,12},{10,14},{12,8},{14,10},{16,20},{18,... | collective-permute-start | bytes 589832 | tf_op jit(solution)/shard_map/ppermute | solution.py:54
  8.9 1.6 %collective-permute-start.1 = (bf16[384,384]{1,0:T(8,128)(2,1)S(1)}, bf16[384,384]{1,0:T(8,128)(2,1)S(1)}, u32[]{:S(2)}, u32[]{:S(2)}) collective-permute-start(bf16[384,384]{1,0:T(8,128)(2,1)S(1)} %pad_maximum_fusion), channel_id=1, source_target_pairs={{0,8},{2,10},{4,12},{6,14},{8,0},{10,2},{12,4},{14,6},{16,24},{18,... | collective-permute-start | bytes 884744 | tf_op jit(solution)/shard_map/ppermute | solution.py:51
  10.5 0.7 broadcast_in_dim.3.gain
  11.2 2.4 %collective-permute-done.refs_0_.refs_2_.refs_12_ = bf16[256,384]{1,0:T(8,128)(2,1)S(1)} collective-permute-done((bf16[256,384]{1,0:T(8,128)(2,1)S(1)}, bf16[256,384]{1,0:T(8,128)(2,1)S(1)}, u32[]{:S(2)}, u32[]{:S(2)}) %collective-permute-start) | collective-permute-done | bytes 196640 | tf_op jit(solution)/shard_map/ppermute | solution.py:54
  13.7 0.9 %copy-done = bf16[1536,64]{0,1:T(8,128)(2,1)S(1)} copy-done((bf16[1536,64]{0,1:T(8,128)(2,1)S(1)}, bf16[1536,64]{0,1:T(8,128)(2,1)}, u32[]{:S(2)}) %copy-start) | copy-done | bytes 196632
  14.6 0.7 copy-done.2
  15.3 0.6 shard_map.113
  15.9 4.8 %collective-permute-done.2.refs_1_.refs_2_.refs_5_ = bf16[384,384]{1,0:T(8,128)(2,1)S(1)} collective-permute-done((bf16[384,384]{1,0:T(8,128)(2,1)S(1)}, bf16[384,384]{1,0:T(8,128)(2,1)S(1)}, u32[]{:S(2)}, u32[]{:S(2)}) %collective-permute-start.2) | collective-permute-done | bytes 294944 | tf_op jit(solution)/shard_map/ppermute | solution.py:51
  20.7 3.5 %collective-permute-start.3 = (bf16[384,384]{1,0:T(8,128)(2,1)S(1)}, bf16[384,384]{1,0:T(8,128)(2,1)S(1)}, u32[]{:S(2)}, u32[]{:S(2)}) collective-permute-start(bf16[384,384]{1,0:T(8,128)(2,1)S(1)} %shard_map.114), channel_id=1, source_target_pairs={{0,24},{2,26},{4,28},{6,30},{8,16},{10,18},{12,20},{14,22},{16,8},... | collective-permute-start | bytes 884744 | tf_op jit(solution)/shard_map/ppermute | solution.py:51
  24.2 1.5 %collective-permute-start.8 = (bf16[256,384]{1,0:T(8,128)(2,1)S(1)}, bf16[256,384]{1,0:T(8,128)(2,1)S(1)}, u32[]{:S(2)}, u32[]{:S(2)}) collective-permute-start(bf16[256,384]{1,0:T(8,128)(2,1)S(1)} %shard_map.115.refs_8_), channel_id=1, source_target_pairs={{0,4},{2,6},{4,0},{6,2},{8,12},{10,14},{12,8},{14,10},{16,20},{18,... | collective-permute-start | bytes 589832 | tf_op jit(solution)/shard_map/ppermute | solution.py:54
  25.7 0.0 collective-permute-done.1.refs_1_.refs_4_
  25.7 0.7 collective-permute-start.7
  26.4 0.0 collective-permute-start.4
  26.4 0.5 collective-permute-start.10
  26.9 4.5 %collective-permute-done.3.refs_3_.refs_6_ = bf16[384,384]{1,0:T(8,128)(2,1)S(1)} collective-permute-done((bf16[384,384]{1,0:T(8,128)(2,1)S(1)}, bf16[384,384]{1,0:T(8,128)(2,1)S(1)}, u32[]{:S(2)}, u32[]{:S(2)}) %collective-permute-start.3) | collective-permute-done | bytes 294944 | tf_op jit(solution)/shard_map/ppermute | solution.py:51
  31.4 0.0 collective-permute-start.6
  31.5 0.6 collective-permute-done.8.refs_2_.refs_7_
  32.1 0.0 collective-permute-start.5
  32.1 2.9 %collective-permute-done.7.refs_1_.refs_14_ = bf16[256,384]{1,0:T(8,128)(2,1)S(1)} collective-permute-done((bf16[256,384]{1,0:T(8,128)(2,1)S(1)}, bf16[256,384]{1,0:T(8,128)(2,1)S(1)}, u32[]{:S(2)}, u32[]{:S(2)}) %collective-permute-start.7) | collective-permute-done | bytes 196640 | tf_op jit(solution)/shard_map/ppermute | solution.py:54
  35.0 0.0 collective-permute-done.4.refs_5_
  35.0 0.5 collective-permute-start.9
  35.5 0.0 collective-permute-done.10.refs_13_
  35.5 0.1 collective-permute-start.12
  35.6 0.0 collective-permute-done.6.refs_9_
  35.6 1.5 %collective-permute-start.13 = (bf16[256,384]{1,0:T(8,128)(2,1)S(1)}, bf16[256,384]{1,0:T(8,128)(2,1)S(1)}, u32[]{:S(2)}, u32[]{:S(2)}) collective-permute-start(bf16[256,384]{1,0:T(8,128)(2,1)S(1)} %shard_map.116.refs_10_), channel_id=1, source_target_pairs={{0,4},{2,6},{4,0},{6,2},{8,12},{10,14},{12,8},{14,10},{16,20},{18,... | collective-permute-start | bytes 589832 | tf_op jit(solution)/shard_map/ppermute | solution.py:54
  37.1 0.0 collective-permute-done.5.refs_7_
  37.1 0.0 collective-permute-done.11.refs_15_
  37.1 0.0 collective-permute-done.9.refs_11_
  37.1 0.0 slice-start
  37.1 0.0 slice-start.1
  37.1 3.8 %shard_map.117 = (f32[3,512,128]{2,1,0:T(8,128)S(1)}, f32[3,512,128]{2,1,0:T(8,128)S(1)}, f32[3,512,128]{2,1,0:T(8,128)S(1)}) custom-call(f32[32,128]{1,0:T(8,128)S(1)} %get-tuple-element.19.refs_3_.bias, bf16[128,384]{1,0:T(8,128)(2,1)S(1)} %get-tuple-element.46.refs_0_.refs_3_, bf16[384,384]{1,0:T(8,128)(2,1)S(1)} %collective-permute-done.1.refs_1_.refs_4_, ...), custom_call_target="tpu_custom_call" | custom-call | flops 4831838208 | tf_op jit(solution)/shard_map/pallas_call | solution.py:192
  40.9 1.9 %collective-permute-done.13.refs_0_ = bf16[256,384]{1,0:T(8,128)(2,1)S(1)} collective-permute-done((bf16[256,384]{1,0:T(8,128)(2,1)S(1)}, bf16[256,384]{1,0:T(8,128)(2,1)S(1)}, u32[]{:S(2)}, u32[]{:S(2)}) %collective-permute-start.13) | collective-permute-done | bytes 196640 | tf_op jit(solution)/shard_map/ppermute | solution.py:54
  42.8 1.5 %collective-permute-start.21 = (bf16[112,1536]{1,0:T(8,128)(2,1)S(1)}, bf16[112,1536]{1,0:T(8,128)(2,1)S(1)}, u32[]{:S(2)}, u32[]{:S(2)}) collective-permute-start(bf16[112,1536]{1,0:T(8,128)(2,1)S(1)} %get-tuple-element.30.refs_2_), channel_id=1, source_target_pairs={{0,1},{1,0},{2,3},{3,2},{4,5},{5,4},{6,7},{7,6},{8,9},{9,8},{10,11... | collective-permute-start | bytes 1032200 | tf_op jit(solution)/shard_map/ppermute | solution.py:57
  44.3 0.0 collective-permute-done.12.refs_8_
  44.3 1.5 %shard_map.119 = (bf16[64,384]{1,0:T(8,128)(2,1)S(1)}, bf16[64,384]{1,0:T(8,128)(2,1)S(1)}, bf16[64,384]{1,0:T(8,128)(2,1)S(1)}, bf16[64,384]{1,0:T(8,128)(2,1)S...) custom-call(f32[32,128]{1,0:T(8,128)S(1)} %get-tuple-element.19.refs, ...), custom_call_target="tpu_custom_call" | custom-call | flops 1610612736 | tf_op jit(solution)/shard_map/pallas_call | solution.py:192
  45.8 0.7 collective-permute-start.20
  46.5 1.9 %collective-permute-start.18 = (bf16[64,384]{1,0:T(8,128)(2,1)S(1)}, bf16[64,384]{1,0:T(8,128)(2,1)S(1)}, u32[]{:S(2)}, u32[]{:S(2)}) collective-permute-start(bf16[64,384]{1,0:T(8,128)(2,1)S(1)} %get-tuple-element.27), channel_id=1, source_target_pairs={{0,8},{2,10},{4,12},{6,14},{8,0},{10,2},{12,4},{14,6},{16,24},{18,... | collective-permute-start | bytes 147464 | tf_op jit(solution)/shard_map/ppermute | solution.py:51
  48.4 1.9 %collective-permute-start.19 = (bf16[64,384]{1,0:T(8,128)(2,1)S(1)}, bf16[64,384]{1,0:T(8,128)(2,1)S(1)}, u32[]{:S(2)}, u32[]{:S(2)}) collective-permute-start(bf16[64,384]{1,0:T(8,128)(2,1)S(1)} %get-tuple-element.28), channel_id=1, source_target_pairs={{0,16},{2,18},{4,20},{6,22},{8,24},{10,26},{12,28},{14,30},{16,0},... | collective-permute-start | bytes 147464 | tf_op jit(solution)/shard_map/ppermute | solution.py:51
  50.3 0.6 shard_map.123.refs_4_
  50.9 2.4 %collective-permute-done.21.refs_1_.refs_3_ = bf16[112,1536]{1,0:T(8,128)(2,1)S(1)} collective-permute-done((bf16[112,1536]{1,0:T(8,128)(2,1)S(1)}, bf16[112,1536]{1,0:T(8,128)(2,1)S(1)}, u32[]{:S(2)}, u32[]{:S(2)}) %collective-permute-start.21) | collective-permute-done | bytes 344096 | tf_op jit(solution)/shard_map/ppermute | solution.py:57
  53.3 0.0 collective-permute-done.18.refs_0_
  53.3 1.3 %collective-permute-done.19.refs_1_ = bf16[64,384]{1,0:T(8,128)(2,1)S(1)} collective-permute-done((bf16[64,384]{1,0:T(8,128)(2,1)S(1)}, bf16[64,384]{1,0:T(8,128)(2,1)S(1)}, u32[]{:S(2)}, u32[]{:S(2)}) %collective-permute-start.19) | collective-permute-done | bytes 49184 | tf_op jit(solution)/shard_map/ppermute | solution.py:51
  54.6 1.4 %shard_map.124 = bf16[64,3072]{1,0:T(8,128)(2,1)S(1)} custom-call(bf16[64,384]{1,0:T(8,128)(2,1)S(1)} %collective-permute-done.18.refs_0_, bf16[64,384]{1,0:T(8,128)(2,1)S(1)} %collective-permute-done.19.refs_1_, bf16[64,384]{1,0:T(8,128)(2,1)S(1)} %shard_map.122.refs_2_, bf16[1536,3072]{1,0:T(8,128)(2,1)S(1)} %bitcast.2, f32[64,3072]{1,0:T(8,128)S(1)} %shard_map.123.refs_4_), custom_call_target="tpu_custom_call" | custom-call | tf_op jit(solution)/shard_map/pallas_call | solution.py:228
  56.0 1.4 %collective-permute-start.22 = (bf16[64,3072]{1,0:T(8,128)(2,1)S(1)}, bf16[64,3072]{1,0:T(8,128)(2,1)S(1)}, u32[]{:S(2)}, u32[]{:S(2)}) collective-permute-start(bf16[64,3072]{1,0:T(8,128)(2,1)S(1)} %shard_map.124), channel_id=1, source_target_pairs={{0,1},{1,0},{2,3},{3,2},{4,5},{5,4},{6,7},{7,6},{8,9},{9,8},{10,11... | collective-permute-start | bytes 1179656 | tf_op jit(solution)/shard_map/ppermute | solution.py:57
  57.4 1.1 %collective-permute-start.15 = (bf16[64,384]{1,0:T(8,128)(2,1)S(1)}, bf16[64,384]{1,0:T(8,128)(2,1)S(1)}, u32[]{:S(2)}, u32[]{:S(2)}) collective-permute-start(bf16[64,384]{1,0:T(8,128)(2,1)S(1)} %get-tuple-element.23), channel_id=1, source_target_pairs={{0,8},{2,10},{4,12},{6,14},{8,0},{10,2},{12,4},{14,6},{16,24},{18,... | collective-permute-start | bytes 147464 | tf_op jit(solution)/shard_map/ppermute | solution.py:51
  58.5 1.5 %collective-permute-start.16 = (bf16[64,384]{1,0:T(8,128)(2,1)S(1)}, bf16[64,384]{1,0:T(8,128)(2,1)S(1)}, u32[]{:S(2)}, u32[]{:S(2)}) collective-permute-start(bf16[64,384]{1,0:T(8,128)(2,1)S(1)} %get-tuple-element.24), channel_id=1, source_target_pairs={{0,16},{2,18},{4,20},{6,22},{8,24},{10,26},{12,28},{14,30},{16,0},... | collective-permute-start | bytes 147464 | tf_op jit(solution)/shard_map/ppermute | solution.py:51
  60.0 1.8 %collective-permute-start.17 = (bf16[64,384]{1,0:T(8,128)(2,1)S(1)}, bf16[64,384]{1,0:T(8,128)(2,1)S(1)}, u32[]{:S(2)}, u32[]{:S(2)}) collective-permute-start(bf16[64,384]{1,0:T(8,128)(2,1)S(1)} %get-tuple-element.25), channel_id=1, source_target_pairs={{0,24},{2,26},{4,28},{6,30},{8,16},{10,18},{12,20},{14,22},{16,8},... | collective-permute-start | bytes 147464 | tf_op jit(solution)/shard_map/ppermute | solution.py:51
  61.8 0.5 shard_map.120.refs_4_
  62.3 0.0 collective-permute-done.15.refs_0_
  62.3 2.0 %collective-permute-done.16.refs_1_ = bf16[64,384]{1,0:T(8,128)(2,1)S(1)} collective-permute-done((bf16[64,384]{1,0:T(8,128)(2,1)S(1)}, bf16[64,384]{1,0:T(8,128)(2,1)S(1)}, u32[]{:S(2)}, u32[]{:S(2)}) %collective-permute-start.16) | collective-permute-done | bytes 49184 | tf_op jit(solution)/shard_map/ppermute | solution.py:51
  64.3 1.6 %collective-permute-done.17.refs_2_ = bf16[64,384]{1,0:T(8,128)(2,1)S(1)} collective-permute-done((bf16[64,384]{1,0:T(8,128)(2,1)S(1)}, bf16[64,384]{1,0:T(8,128)(2,1)S(1)}, u32[]{:S(2)}, u32[]{:S(2)}) %collective-permute-start.17) | collective-permute-done | bytes 49184 | tf_op jit(solution)/shard_map/ppermute | solution.py:51
  65.9 1.4 %shard_map.121.refs_0_ = f32[64,3072]{1,0:T(8,128)S(1)} custom-call(bf16[64,384]{1,0:T(8,128)(2,1)S(1)} %collective-permute-done.15.refs_0_, bf16[64,384]{1,0:T(8,128)(2,1)S(1)} %collective-permute-done.16.refs_1_, bf16[64,384]{1,0:T(8,128)(2,1)S(1)} %collective-permute-done.17.refs_2_, bf16[1536,3072]{1,0:T(8,128)(2,1)S(1)} %bitcast.2, ...), custom_call_target="tpu_custom_call" | custom-call | tf_op jit(solution)/shard_map/pallas_call | solution.py:228
  67.3 0.0 collective-permute-done.22.refs_1_
  67.3 1.0 %shard_map.125 = (f32[32,128]{1,0:T(8,128)S(1)}, f32[32,128]{1,0:T(8,128)S(1)}) custom-call(s32[8]{0:T(128)S(1)} %copy-done.3, s32[9]{0:T(128)S(1)} %copy-done.4, f32[64,3072]{1,0:T(8,128)S(1)} %shard_map.121.refs_0_, bf16[64,3072]{1,0:T(8,128)(2,1)S(1)} %collective-permute-done.22.refs_1_, bf16[112,1536]{1,0:T(8,128)(2,1)S(1)} %get-tuple-element.30.refs_2_, ...), custom_call_target="tpu_custom_call" | custom-call | tf_op jit(solution)/shard_map/pallas_call | solution.py:278
  68.3 1.5 %collective-permute-start.23 = (f32[32,128]{1,0:T(8,128)S(1)}, f32[32,128]{1,0:T(8,128)S(1)}, u32[]{:S(2)}, u32[]{:S(2)}) collective-permute-start(f32[32,128]{1,0:T(8,128)S(1)} %get-tuple-element.32), channel_id=1, source_target_pairs={{0,4},{1,5},{2,6},{3,7},{4,8},{5,9},{6,10},{7,11},{8,12},{9,13},{1... | collective-permute-start | bytes 49160 | tf_op jit(solution)/shard_map/ppermute | solution.py:65
  69.8 1.4 %collective-permute-start.24 = (f32[32,128]{1,0:T(8,128)S(1)}, f32[32,128]{1,0:T(8,128)S(1)}, u32[]{:S(2)}, u32[]{:S(2)}) collective-permute-start(f32[32,128]{1,0:T(8,128)S(1)} %get-tuple-element.32), channel_id=1, source_target_pairs={{0,5},{1,4},{2,7},{3,6},{4,9},{5,8},{6,11},{7,10},{8,13},{9,12},{1... | collective-permute-start | bytes 49160 | tf_op jit(solution)/shard_map/ppermute | solution.py:65
  71.2 0.5 collective-permute-start.25
  71.7 3.1 %collective-permute-done.23.refs_0_ = f32[32,128]{1,0:T(8,128)S(1)} collective-permute-done((f32[32,128]{1,0:T(8,128)S(1)}, f32[32,128]{1,0:T(8,128)S(1)}, u32[]{:S(2)}, u32[]{:S(2)}) %collective-permute-start.23) | collective-permute-done | bytes 16416 | tf_op jit(solution)/shard_map/ppermute | solution.py:65
  74.8 2.4 %collective-permute-done.24.refs_1_ = f32[32,128]{1,0:T(8,128)S(1)} collective-permute-done((f32[32,128]{1,0:T(8,128)S(1)}, f32[32,128]{1,0:T(8,128)S(1)}, u32[]{:S(2)}, u32[]{:S(2)}) %collective-permute-start.24) | collective-permute-done | bytes 16416 | tf_op jit(solution)/shard_map/ppermute | solution.py:65
  77.1 0.0 collective-permute-done.25.refs_3_
  77.1 0.6 shard_map.126
  (29 shorter events, 0.2 us)
Async XLA Ops:
  3.1 17.5 %collective-permute-start.2 = (bf16[384,384]{1,0:T(8,128)(2,1)S(1)}, bf16[384,384]{1,0:T(8,128)(2,1)S(1)}, u32[]{:S(2)}, u32[]{:S(2)}) collective-permute-start(bf16[384,384]{1,0:T(8,128)(2,1)S(1)} %pad_maximum_fusion.1), channel_id=1, source_target_pairs={{0,16},{2,18},{4,20},{6,22},{8,24},{10,26},{12,28},{14,30},{16,0},... | collective-permute-start | bytes 884744 | tf_op jit(solution)/shard_map/ppermute | solution.py:51
  7.2 6.4 %collective-permute-start = (bf16[256,384]{1,0:T(8,128)(2,1)S(1)}, bf16[256,384]{1,0:T(8,128)(2,1)S(1)}, u32[]{:S(2)}, u32[]{:S(2)}) collective-permute-start(bf16[256,384]{1,0:T(8,128)(2,1)S(1)} %pad_maximum_fusion.3.refs_4_), channel_id=1, source_target_pairs={{0,4},{2,6},{4,0},{6,2},{8,12},{10,14},{12,8},{14,10},{16,20},{18,... | collective-permute-start | bytes 589832 | tf_op jit(solution)/shard_map/ppermute | solution.py:54
  8.9 16.8 %collective-permute-start.1 = (bf16[384,384]{1,0:T(8,128)(2,1)S(1)}, bf16[384,384]{1,0:T(8,128)(2,1)S(1)}, u32[]{:S(2)}, u32[]{:S(2)}) collective-permute-start(bf16[384,384]{1,0:T(8,128)(2,1)S(1)} %pad_maximum_fusion), channel_id=1, source_target_pairs={{0,8},{2,10},{4,12},{6,14},{8,0},{10,2},{12,4},{14,6},{16,24},{18,... | collective-permute-start | bytes 884744 | tf_op jit(solution)/shard_map/ppermute | solution.py:51
  13.7 0.9 %copy-start = (bf16[1536,64]{0,1:T(8,128)(2,1)S(1)}, bf16[1536,64]{0,1:T(8,128)(2,1)}, u32[]{:S(2)}) copy-start(bf16[1536,64]{0,1:T(8,128)(2,1)} %param.16) | copy-start | bytes 589828
  14.6 0.7 copy-start.2
  20.7 10.8 %collective-permute-start.3 = (bf16[384,384]{1,0:T(8,128)(2,1)S(1)}, bf16[384,384]{1,0:T(8,128)(2,1)S(1)}, u32[]{:S(2)}, u32[]{:S(2)}) collective-permute-start(bf16[384,384]{1,0:T(8,128)(2,1)S(1)} %shard_map.114), channel_id=1, source_target_pairs={{0,24},{2,26},{4,28},{6,30},{8,16},{10,18},{12,20},{14,22},{16,8},... | collective-permute-start | bytes 884744 | tf_op jit(solution)/shard_map/ppermute | solution.py:51
  24.2 7.9 %collective-permute-start.8 = (bf16[256,384]{1,0:T(8,128)(2,1)S(1)}, bf16[256,384]{1,0:T(8,128)(2,1)S(1)}, u32[]{:S(2)}, u32[]{:S(2)}) collective-permute-start(bf16[256,384]{1,0:T(8,128)(2,1)S(1)} %shard_map.115.refs_8_), channel_id=1, source_target_pairs={{0,4},{2,6},{4,0},{6,2},{8,12},{10,14},{12,8},{14,10},{16,20},{18,... | collective-permute-start | bytes 589832 | tf_op jit(solution)/shard_map/ppermute | solution.py:54
  25.7 9.3 %collective-permute-start.7 = (bf16[256,384]{1,0:T(8,128)(2,1)S(1)}, bf16[256,384]{1,0:T(8,128)(2,1)S(1)}, u32[]{:S(2)}, u32[]{:S(2)}) collective-permute-start(bf16[256,384]{1,0:T(8,128)(2,1)S(1)} %slice.12.refs_6_), channel_id=1, source_target_pairs={{0,4},{2,6},{4,0},{6,2},{8,12},{10,14},{12,8},{14,10},{16,20},{18,... | collective-permute-start | bytes 589832 | tf_op jit(solution)/shard_map/ppermute | solution.py:54
  26.4 8.6 %collective-permute-start.4 = (bf16[256,384]{1,0:T(8,128)(2,1)S(1)}, bf16[256,384]{1,0:T(8,128)(2,1)S(1)}, u32[]{:S(2)}, u32[]{:S(2)}) collective-permute-start(bf16[256,384]{1,0:T(8,128)(2,1)S(1)} %pad_maximum_fusion.3.refs_4_), channel_id=1, source_target_pairs={{0,2},{2,0},{4,6},{6,4},{8,10},{10,8},{12,14},{14,12},{16,18},{18,... | collective-permute-start | bytes 589832 | tf_op jit(solution)/shard_map/ppermute | solution.py:54
  26.4 9.1 %collective-permute-start.10 = (bf16[256,384]{1,0:T(8,128)(2,1)S(1)}, bf16[256,384]{1,0:T(8,128)(2,1)S(1)}, u32[]{:S(2)}, u32[]{:S(2)}) collective-permute-start(bf16[256,384]{1,0:T(8,128)(2,1)S(1)} %collective-permute-done.refs_0_.refs_2_.refs_12_), channel_id=1, source_target_pairs={{0,2},{2,0},{4,6},{6,4},{8,10},{10,8},{12,14},{14,12},{16,18},{18,... | collective-permute-start | bytes 589832 | tf_op jit(solution)/shard_map/ppermute | solution.py:54
  31.4 4.2 %collective-permute-start.6 = (bf16[256,384]{1,0:T(8,128)(2,1)S(1)}, bf16[256,384]{1,0:T(8,128)(2,1)S(1)}, u32[]{:S(2)}, u32[]{:S(2)}) collective-permute-start(bf16[256,384]{1,0:T(8,128)(2,1)S(1)} %shard_map.115.refs_8_), channel_id=1, source_target_pairs={{0,2},{2,0},{4,6},{6,4},{8,10},{10,8},{12,14},{14,12},{16,18},{18,... | collective-permute-start | bytes 589832 | tf_op jit(solution)/shard_map/ppermute | solution.py:54
  32.1 5.0 %collective-permute-start.5 = (bf16[256,384]{1,0:T(8,128)(2,1)S(1)}, bf16[256,384]{1,0:T(8,128)(2,1)S(1)}, u32[]{:S(2)}, u32[]{:S(2)}) collective-permute-start(bf16[256,384]{1,0:T(8,128)(2,1)S(1)} %slice.12.refs_6_), channel_id=1, source_target_pairs={{0,2},{2,0},{4,6},{6,4},{8,10},{10,8},{12,14},{14,12},{16,18},{18,... | collective-permute-start | bytes 589832 | tf_op jit(solution)/shard_map/ppermute | solution.py:54
  35.0 2.1 %collective-permute-start.11 = (bf16[256,384]{1,0:T(8,128)(2,1)S(1)}, bf16[256,384]{1,0:T(8,128)(2,1)S(1)}, u32[]{:S(2)}, u32[]{:S(2)}) collective-permute-start(bf16[256,384]{1,0:T(8,128)(2,1)S(1)} %collective-permute-done.7.refs_1_.refs_14_), channel_id=1, source_target_pairs={{0,2},{2,0},{4,6},{6,4},{8,10},{10,8},{12,14},{14,12},{16,18},{18,... | collective-permute-start | bytes 589832 | tf_op jit(solution)/shard_map/ppermute | solution.py:54
  35.0 2.1 %collective-permute-start.9 = (bf16[256,384]{1,0:T(8,128)(2,1)S(1)}, bf16[256,384]{1,0:T(8,128)(2,1)S(1)}, u32[]{:S(2)}, u32[]{:S(2)}) collective-permute-start(bf16[256,384]{1,0:T(8,128)(2,1)S(1)} %shard_map.116.refs_10_), channel_id=1, source_target_pairs={{0,2},{2,0},{4,6},{6,4},{8,10},{10,8},{12,14},{14,12},{16,18},{18,... | collective-permute-start | bytes 589832 | tf_op jit(solution)/shard_map/ppermute | solution.py:54
  35.5 8.8 %collective-permute-start.12 = (bf16[256,384]{1,0:T(8,128)(2,1)S(1)}, bf16[256,384]{1,0:T(8,128)(2,1)S(1)}, u32[]{:S(2)}, u32[]{:S(2)}) collective-permute-start(bf16[256,384]{1,0:T(8,128)(2,1)S(1)} %collective-permute-done.8.refs_2_.refs_7_), channel_id=1, source_target_pairs={{0,2},{2,0},{4,6},{6,4},{8,10},{10,8},{12,14},{14,12},{16,18},{18,... | collective-permute-start | bytes 589832 | tf_op jit(solution)/shard_map/ppermute | solution.py:54
  35.6 7.2 %collective-permute-start.13 = (bf16[256,384]{1,0:T(8,128)(2,1)S(1)}, bf16[256,384]{1,0:T(8,128)(2,1)S(1)}, u32[]{:S(2)}, u32[]{:S(2)}) collective-permute-start(bf16[256,384]{1,0:T(8,128)(2,1)S(1)} %shard_map.116.refs_10_), channel_id=1, source_target_pairs={{0,4},{2,6},{4,0},{6,2},{8,12},{10,14},{12,8},{14,10},{16,20},{18,... | collective-permute-start | bytes 589832 | tf_op jit(solution)/shard_map/ppermute | solution.py:54
  37.1 13.2 %slice-start = ((s8[9437184]{0:T(1024)(128)(4,1)}), s8[4194304]{0:T(1024)(128)(4,1)S(1)}, s32[]{:S(2)}) async-start(s8[9437184]{0:T(1024)(128)(4,1)} %bitcast.1), calls=%async_computation | async-start | bytes 8388608
  37.1 13.2 %slice-start.1 = ((s8[9437184]{0:T(1024)(128)(4,1)}), s8[4194304]{0:T(1024)(128)(4,1)S(1)}, s32[]{:S(2)}) async-start(s8[9437184]{0:T(1024)(128)(4,1)} %bitcast.1), calls=%async_computation.1 | async-start | bytes 8388608
  37.1 13.2 %slice-start.2 = ((s8[9437184]{0:T(1024)(128)(4,1)}), s8[1048576]{0:T(1024)(128)(4,1)S(1)}, s32[]{:S(2)}) async-start(s8[9437184]{0:T(1024)(128)(4,1)} %bitcast.1), calls=%async_computation.2 | async-start | bytes 2097152
  42.8 1.5 %collective-permute-start.14 = (bf16[256,384]{1,0:T(8,128)(2,1)S(1)}, bf16[256,384]{1,0:T(8,128)(2,1)S(1)}, u32[]{:S(2)}, u32[]{:S(2)}) collective-permute-start(bf16[256,384]{1,0:T(8,128)(2,1)S(1)} %shard_map.118.refs_9_), channel_id=1, source_target_pairs={{0,2},{2,0},{4,6},{6,4},{8,10},{10,8},{12,14},{14,12},{16,18},{18,... | collective-permute-start | bytes 589832 | tf_op jit(solution)/shard_map/ppermute | solution.py:54
  42.8 10.5 %collective-permute-start.21 = (bf16[112,1536]{1,0:T(8,128)(2,1)S(1)}, bf16[112,1536]{1,0:T(8,128)(2,1)S(1)}, u32[]{:S(2)}, u32[]{:S(2)}) collective-permute-start(bf16[112,1536]{1,0:T(8,128)(2,1)S(1)} %get-tuple-element.30.refs_2_), channel_id=1, source_target_pairs={{0,1},{1,0},{2,3},{3,2},{4,5},{5,4},{6,7},{7,6},{8,9},{9,8},{10,11... | collective-permute-start | bytes 1032200 | tf_op jit(solution)/shard_map/ppermute | solution.py:57
  45.8 7.5 %collective-permute-start.20 = (bf16[64,384]{1,0:T(8,128)(2,1)S(1)}, bf16[64,384]{1,0:T(8,128)(2,1)S(1)}, u32[]{:S(2)}, u32[]{:S(2)}) collective-permute-start(bf16[64,384]{1,0:T(8,128)(2,1)S(1)} %get-tuple-element.29), channel_id=1, source_target_pairs={{0,24},{2,26},{4,28},{6,30},{8,16},{10,18},{12,20},{14,22},{16,8},... | collective-permute-start | bytes 147464 | tf_op jit(solution)/shard_map/ppermute | solution.py:51
  46.5 6.8 %collective-permute-start.18 = (bf16[64,384]{1,0:T(8,128)(2,1)S(1)}, bf16[64,384]{1,0:T(8,128)(2,1)S(1)}, u32[]{:S(2)}, u32[]{:S(2)}) collective-permute-start(bf16[64,384]{1,0:T(8,128)(2,1)S(1)} %get-tuple-element.27), channel_id=1, source_target_pairs={{0,8},{2,10},{4,12},{6,14},{8,0},{10,2},{12,4},{14,6},{16,24},{18,... | collective-permute-start | bytes 147464 | tf_op jit(solution)/shard_map/ppermute | solution.py:51
  48.4 6.2 %collective-permute-start.19 = (bf16[64,384]{1,0:T(8,128)(2,1)S(1)}, bf16[64,384]{1,0:T(8,128)(2,1)S(1)}, u32[]{:S(2)}, u32[]{:S(2)}) collective-permute-start(bf16[64,384]{1,0:T(8,128)(2,1)S(1)} %get-tuple-element.28), channel_id=1, source_target_pairs={{0,16},{2,18},{4,20},{6,22},{8,24},{10,26},{12,28},{14,30},{16,0},... | collective-permute-start | bytes 147464 | tf_op jit(solution)/shard_map/ppermute | solution.py:51
  56.0 11.3 %collective-permute-start.22 = (bf16[64,3072]{1,0:T(8,128)(2,1)S(1)}, bf16[64,3072]{1,0:T(8,128)(2,1)S(1)}, u32[]{:S(2)}, u32[]{:S(2)}) collective-permute-start(bf16[64,3072]{1,0:T(8,128)(2,1)S(1)} %shard_map.124), channel_id=1, source_target_pairs={{0,1},{1,0},{2,3},{3,2},{4,5},{5,4},{6,7},{7,6},{8,9},{9,8},{10,11... | collective-permute-start | bytes 1179656 | tf_op jit(solution)/shard_map/ppermute | solution.py:57
  57.4 4.9 %collective-permute-start.15 = (bf16[64,384]{1,0:T(8,128)(2,1)S(1)}, bf16[64,384]{1,0:T(8,128)(2,1)S(1)}, u32[]{:S(2)}, u32[]{:S(2)}) collective-permute-start(bf16[64,384]{1,0:T(8,128)(2,1)S(1)} %get-tuple-element.23), channel_id=1, source_target_pairs={{0,8},{2,10},{4,12},{6,14},{8,0},{10,2},{12,4},{14,6},{16,24},{18,... | collective-permute-start | bytes 147464 | tf_op jit(solution)/shard_map/ppermute | solution.py:51
  58.5 5.8 %collective-permute-start.16 = (bf16[64,384]{1,0:T(8,128)(2,1)S(1)}, bf16[64,384]{1,0:T(8,128)(2,1)S(1)}, u32[]{:S(2)}, u32[]{:S(2)}) collective-permute-start(bf16[64,384]{1,0:T(8,128)(2,1)S(1)} %get-tuple-element.24), channel_id=1, source_target_pairs={{0,16},{2,18},{4,20},{6,22},{8,24},{10,26},{12,28},{14,30},{16,0},... | collective-permute-start | bytes 147464 | tf_op jit(solution)/shard_map/ppermute | solution.py:51
  60.0 5.9 %collective-permute-start.17 = (bf16[64,384]{1,0:T(8,128)(2,1)S(1)}, bf16[64,384]{1,0:T(8,128)(2,1)S(1)}, u32[]{:S(2)}, u32[]{:S(2)}) collective-permute-start(bf16[64,384]{1,0:T(8,128)(2,1)S(1)} %get-tuple-element.25), channel_id=1, source_target_pairs={{0,24},{2,26},{4,28},{6,30},{8,16},{10,18},{12,20},{14,22},{16,8},... | collective-permute-start | bytes 147464 | tf_op jit(solution)/shard_map/ppermute | solution.py:51
  61.7 5.5 %copy-start.1 = (f32[64,128]{1,0:T(8,128)S(1)}, f32[64,128]{1,0:T(8,128)}, u32[]{:S(2)}) copy-start(f32[64,128]{1,0:T(8,128)} %refs_4_.1) | copy-start | bytes 98308
  61.8 5.5 %copy-start.3 = (s32[8]{0:T(128)S(1)}, s32[8]{0:T(128)}, u32[]{:S(2)}) copy-start(s32[8]{0:T(128)} %levels.1) | copy-start | bytes 100
  61.8 5.5 %copy-start.4 = (s32[9]{0:T(128)S(1)}, s32[9]{0:T(128)}, u32[]{:S(2)}) copy-start(s32[9]{0:T(128)} %timesteps.1) | copy-start | bytes 112
  68.3 6.5 %collective-permute-start.23 = (f32[32,128]{1,0:T(8,128)S(1)}, f32[32,128]{1,0:T(8,128)S(1)}, u32[]{:S(2)}, u32[]{:S(2)}) collective-permute-start(f32[32,128]{1,0:T(8,128)S(1)} %get-tuple-element.32), channel_id=1, source_target_pairs={{0,4},{1,5},{2,6},{3,7},{4,8},{5,9},{6,10},{7,11},{8,12},{9,13},{1... | collective-permute-start | bytes 49160 | tf_op jit(solution)/shard_map/ppermute | solution.py:65
  69.8 7.3 %collective-permute-start.24 = (f32[32,128]{1,0:T(8,128)S(1)}, f32[32,128]{1,0:T(8,128)S(1)}, u32[]{:S(2)}, u32[]{:S(2)}) collective-permute-start(f32[32,128]{1,0:T(8,128)S(1)} %get-tuple-element.32), channel_id=1, source_target_pairs={{0,5},{1,4},{2,7},{3,6},{4,9},{5,8},{6,11},{7,10},{8,13},{9,12},{1... | collective-permute-start | bytes 49160 | tf_op jit(solution)/shard_map/ppermute | solution.py:65
  71.2 6.0 %collective-permute-start.25 = (f32[32,128]{1,0:T(8,128)S(1)}, f32[32,128]{1,0:T(8,128)S(1)}, u32[]{:S(2)}, u32[]{:S(2)}) collective-permute-start(f32[32,128]{1,0:T(8,128)S(1)} %get-tuple-element.33.refs_2_), channel_id=1, source_target_pairs={{0,1},{1,0},{2,3},{3,2},{4,5},{5,4},{6,7},{7,6},{8,9},{9,8},{10,11... | collective-permute-start | bytes 49160 | tf_op jit(solution)/shard_map/ppermute | solution.py:57

commit v4 on v3

--- a/solution.py
+++ b/solution.py
@@ -78,6 +78,25 @@
     return jnp.concatenate([lax.dynamic_slice_in_dim(a, at, plan.cols, 1) for a in arrays], axis=0)
 
 
+def pack_late_kernel(plan, steps, waits, *refs):
+    sources, refs = refs[:3], refs[3 + waits :]
+    for step, ref in zip(steps, refs):
+        here = pl.ds(pl.multiple_of((plan.part() ^ step) * plan.cols, 128), plan.cols)
+        rows = [source[:, here] for source in sources]
+        ref[...] = jnp.concatenate(rows, axis=0)[3 * plan.rows - ref.shape[0] :]
+
+
+def pack_late(plan, steps, arrays, after):
+    rows = [(3 if step else 1) * plan.rows for step in steps]
+    return pl.pallas_call(
+        functools.partial(pack_late_kernel, plan, steps, len(after)),
+        out_shape=[struct((n, plan.cols), arrays[0].dtype) for n in rows],
+        in_specs=[VMEM] * 3 + [ANY] * len(after),
+        out_specs=[VMEM] * len(steps),
+        compiler_params=params(4),
+    )(*arrays, *after)
+
+
 def held(values, after):
     def kernel(*refs):
         pass
@@ -92,8 +111,8 @@
     )(*values, *after)
 
 
-def ready_kernel(plan, waits, order, gain, head_weight, *refs):
-    shared, bias = refs[waits:]
+def ready_kernel(plan, waits, order, levels, timesteps, gain, head_weight, *refs):
+    shared, bias, delta = refs[waits:]
     count = head_weight.shape[0]
     shared[pl.ds(0, count), :] = head_weight[...]
     rest, rows = gain[...], []
@@ -103,6 +122,9 @@
     rows = [jnp.broadcast_to(row, (16, gain.shape[1])) for row in rows]
     shared[pl.ds(count, 48), :] = jnp.concatenate(rows, axis=0)
     me = lax.axis_index("section")
+    level = levels[me // plan.span]
+    change = (timesteps[level + 1] - timesteps[level]).astype(jnp.float32)
+    delta[...] = jnp.full(delta.shape, change, jnp.float32) / 1000.0
 
     def order_of(step, member):
         return order[(me ^ (step * plan.members + member)) // plan.span]
@@ -114,17 +136,18 @@
             bias[pl.ds(i * plan.blocks + j, 1), :] = jnp.full((1, HD), jnp.where(seen, 0.0, NEG))
 
 
-def ready(plan, order, gain, head_weight, after):
+def ready(plan, order, levels, timesteps, gain, head_weight, after):
     return pl.pallas_call(
         functools.partial(ready_kernel, plan, len(after)),
         out_shape=[
             struct((head_weight.shape[0] + 48, head_weight.shape[1]), jnp.bfloat16),
             struct((plan.split * plan.blocks, HD), jnp.float32),
+            struct((8, HD), jnp.float32),
         ],
-        in_specs=[SMEM, VMEM, VMEM] + [ANY] * len(after),
-        out_specs=[VMEM, VMEM],
+        in_specs=[SMEM] * 3 + [VMEM] * 2 + [ANY] * len(after),
+        out_specs=[VMEM] * 3,
         compiler_params=params(4),
-    )(order, gain, head_weight, *after)
+    )(order, levels, timesteps, gain, head_weight, *after)
 
 
 def attend_kernel(plan, blocks, begun, last, bias, *refs):
@@ -236,7 +259,7 @@
     return list(out) if split else out[0]
 
 
-def head_kernel(plan, levels, timesteps, *refs):
+def head_kernel(plan, delta, *refs):
     sums, refs = refs[: plan.tensors], refs[plan.tensors :]
     shared, refs = refs[: plan.tensors], refs[plan.tensors :]
     latents, velocity_ref, moved_ref, full, rows = refs
@@ -265,27 +288,24 @@
     velocity = jnp.concatenate(
         [rows[pl.ds(0, half, 2), :], rows[pl.ds(1, half, 2), :]], axis=1
     )
-    level = levels[lax.axis_index("section") // plan.span]
-    change = (timesteps[level + 1] - timesteps[level]).astype(jnp.float32)
-    delta = jnp.full(velocity.shape, change, jnp.float32) / 1000.0
     velocity_ref[...] = velocity
     here = pl.ds(pl.multiple_of(tensor * half, 8), half)
-    moved_ref[...] = latents[here, :] + delta * velocity
-
-
-def head(plan, levels, timesteps, sums, shared, latents):
+    moved_ref[...] = latents[here, :] + delta[pl.ds(0, 1), :] * velocity
+
+
+def head(plan, delta, sums, shared, latents):
     half = struct((plan.share // 2, latents.shape[1]), jnp.float32)
     return pl.pallas_call(
         functools.partial(head_kernel, plan),
         out_shape=[half, half],
-        in_specs=[SMEM, SMEM] + [VMEM] * (2 * plan.tensors + 1),
+        in_specs=[VMEM] * (2 * plan.tensors + 2),
         out_specs=[VMEM, VMEM],
         scratch_shapes=[
             pltpu.VMEM(sums[0].shape, jnp.float32),
             pltpu.VMEM((plan.share, latents.shape[1] // 2), jnp.float32),
         ],
         compiler_params=params(12),
-    )(levels, timesteps, *sums, *shared, latents)
+    )(delta, *sums, *shared, latents)
 
 
 def place_kernel(plan, *refs):
@@ -313,31 +333,32 @@
     split, tensors = plan.split, plan.tensors
 
     far, near = list(range(1, split)), [0]
-    own, asked = pack(plan, 0, keys, values), [pack(plan, 0, queries)]
+    own = pack(plan, 0, keys, values)
     if split == 4 and plan.members == 4:
         two = plan.to_part(pack(plan, 2, keys, values, queries), 2)
         one = plan.to_part(pack(plan, 1, keys, values, queries), 1)
         own = plan.gather_members(own)
-        shared, bias = ready(plan, order, gain[None, :], head_weight.T, [own[2]])
+        late, *asked = pack_late(plan, [3, 0], (keys, values, queries), [own[2]])
+        shared, bias, delta = ready(plan, order, levels, timesteps, gain[None, :], head_weight.T, [own[2], late])
         shared = [shared] + [plan.to_tensor(shared, i) for i in range(1, tensors)]
         ones = plan.gather_members(one[: 2 * plan.rows])
-        (three,) = held([pack(plan, 3, keys, values, queries)], [two, own[2], bias])
+        (three,) = held([late], [two, own[2], bias])
         three = plan.to_part(three, 3)
         asked += [one, two, three]
         twos = plan.gather_members(*held([two[: 2 * plan.rows]], []))
-        threes = [*held([three[: 2 * plan.rows]], [ones[2], twos[2]])]
+        threes = [*held([three[: 2 * plan.rows]], [ones[2], twos[2], *shared[1:]])]
         threes += [plan.to_member(threes[0], i) for i in (1, 2)]
         pairs = [v[i : i + 2] for v in (own, ones, twos) for i in (0, 2)]
         pairs.append(threes[:2])
-        state = attend(plan, [0, 2, 4, 6, 1, 3], bias, asked, pairs)
+        state = attend(plan, [0, 2, 4, 6, 1, 3, 5], bias, asked, pairs)
         (last,) = held(threes[2:], [state[0]])
         pairs.append([last, plan.to_member(last, 1)])
-        attended = attend(plan, [5, 7], bias, asked, pairs, state, True)
+        attended = attend(plan, [7], bias, asked, pairs, state, True)
     else:
-        shared, bias = ready(plan, order, gain[None, :], head_weight.T, [])
+        shared, bias, delta = ready(plan, order, levels, timesteps, gain[None, :], head_weight.T, [])
         shared = [shared] + [plan.to_tensor(shared, i) for i in range(1, tensors)]
         sent = [own] + [plan.to_part(pack(plan, i, keys, values), i) for i in far]
-        asked += [plan.to_part(pack(plan, i, queries), i) for i in far]
+        asked = [pack(plan, 0, queries)] + [plan.to_part(pack(plan, i, queries), i) for i in far]
         pieces = [p for v in sent for p in plan.gather_members(v)]
         pairs = [pieces[i : i + plan.per] for i in range(0, len(pieces), plan.per)]
         blocks = list(range(plan.blocks))
@@ -349,13 +370,12 @@
     away = [plan.to_part(v, i) if i else v for i, v in enumerate(away)]
     rest = far or near
     begun = project(plan, near, away[:1], out_weight) if far else None
-    away[-1:] = held(away[-1:], shared[1:])
     away = project(plan, rest, [away[i] for i in rest], out_weight, begun, True)
     away = [plan.to_tensor(v, i + 1) for i, v in enumerate(away)]
     kept = [plan.to_part(v, i) if i else v for i, v in enumerate(kept)]
     begun = project(plan, near, kept[:1], out_weight) if far else None
     sums = [project(plan, rest, [kept[i] for i in rest], out_weight, begun), *away]
-    velocity, moved = head(plan, levels, timesteps, sums, shared, latents)
+    velocity, moved = head(plan, delta, sums, shared, latents)
     advanced = [plan.to_next_group(moved, i) for i in range(tensors)]
     velocities = [velocity] + [plan.to_tensor(velocity, i) for i in range(1, tensors)]
     return place(plan, advanced, velocities)[::-1]

time: 78 us -> 77.2 us (0.990)
  waiting for transfers between devices: 29.9 us -> 25.1 us
  local copies, waits for them, and re-layouts: 4.78 us -> 8.83 us
    unnamed x16 -> x22, local copies, waits for them, and re-layouts: 1.61 us -> 5.89 us
    ppermute x9, waiting for transfers between devices: 14.1 us -> 10.5 us  [to_part(): return lax.ppermute(value, 'section', pairs)]
    ppermute x3, waiting for transfers between devices: 2.45 us -> 0.01 us  [to_tensor(): lax.ppermute(value, 'tensor', [(t, t ^ step) for t in range(self.tensors)])]
    ppermute x12, waiting for transfers between devices: 7.89 us -> 9.78 us  [to_member(): lax.ppermute(value, 'section', [(s, s ^ step) for s in range(self.section...]
  transfers between devices with their start and end apart: 26 -> 26, of which waited for: 12 -> 12; matrix products, arithmetic and copies ran while one was open for 1% -> 1% of each run, Pallas kernels for 11% -> 10%
where the time goes in v4:
time: 77.2 us; the launch traced here: 76.7 us
  starting transfers between devices  31.2 us (40%)
  waiting for transfers between devices  25.1 us (33%)
  Pallas kernels  10.7 us (14%)
  local copies, waits for them, and re-layouts  8.83 us (11%)
  between operations  0.87 us (1%)
    ppermute x9, starting transfers between devices, to_part(): return lax.ppermute(value, 'section', pairs)  18.1 us
    ppermute x9, waiting for transfers between devices, to_part(): return lax.ppermute(value, 'section', pairs)  10.5 us
    ppermute x12, waiting for transfers between devices, to_member(): lax.ppermute(value, 'section', [(s, s ^ step) for s in range(self.section...  9.78 us
    ppermute x12, starting transfers between devices, to_member(): lax.ppermute(value, 'section', [(s, s ^ step) for s in range(self.section...  6.25 us
    unnamed x22, local copies, waits for them, and re-layouts  5.89 us
    pallas_call x2, Pallas kernels, attend(): pl.pallas_call(functools.partial(attend_kernel, plan, blocks, bool(state)...  5.08 us
    ppermute x2, waiting for transfers between devices, to_next_group(): return lax.ppermute(value, ('section', 'tensor'), pairs)  4.79 us
    pallas_call x4, Pallas kernels, project(): pl.pallas_call(functools.partial(project_kernel, plan, steps, bool(extra)...  3.83 us
  transfers between devices with their start and end apart: 26, of which 12 were waited for; matrix products, arithmetic and copies ran while one was open for 1% of the time, Pallas kernels for 10%

profile of v4, /device:TPU:0, one launch (start us, length us, event | category | flops | bytes accessed | tf_op | source)
XLA Modules:
  0.0 76.7 jit_solution(636650035175494040)
XLA Ops:
  0.7 1.0 %constant_dynamic-slice_fusion.2 = (bf16[128,384]{1,0:T(8,128)(2,1)S(1)}, bf16[128,384]{1,0:T(8,128)(2,1)S(1)}, bf16[128,384]{1,0:T(8,128)(2,1)S(1)}) fusion(bf16[128,1536]{1,0:T(8,128)(2,1)} %refs_0_.1, s32[]{:T(128)S(6)} %select_n.24, s32[]{:T(128)S(6)} %select_n.22, s32[]{:T(128)S(6)} %select_n.23), kind=kLoop, calls=%fused_computation.5 | loop fusion | bytes 589836 | tf_op jit(solution)/shard_map/dynamic_slice | solution.py:78
  1.7 1.1 %constant_dynamic-slice_fusion = (bf16[128,384]{1,0:T(8,128)(2,1)S(1)}, bf16[128,384]{1,0:T(8,128)(2,1)S(1)}, bf16[128,384]{1,0:T(8,128)(2,1)S(1)}, bf16[128,384]{1,0:T(8,128)(2,1)S(1)}, bf16[128,384]{1,0:T(8,128)(2,1)S(1)}) fusion(bf16[128,1536]{1,0:T(8,128)(2,1)} %refs_2_.1, s32[]{:T(128)S(6)} %select_n.24, s32[]{:T(128)S(6)} %select_n.23, ...), kind=kLoop, calls=%fused_computation.3 | loop fusion | bytes 983052 | tf_op jit(solution)/shard_map/dynamic_slice | solution.py:78
  2.9 4.1 %collective-permute-start.2 = (bf16[384,384]{1,0:T(8,128)(2,1)S(1)}, bf16[384,384]{1,0:T(8,128)(2,1)S(1)}, u32[]{:S(2)}, u32[]{:S(2)}) collective-permute-start(bf16[384,384]{1,0:T(8,128)(2,1)S(1)} %pad_maximum_fusion.1), channel_id=1, source_target_pairs={{0,16},{2,18},{4,20},{6,22},{8,24},{10,26},{12,28},{14,30},{16,0},... | collective-permute-start | bytes 884744 | tf_op jit(solution)/shard_map/ppermute | solution.py:51
  7.0 1.6 %collective-permute-start = (bf16[256,384]{1,0:T(8,128)(2,1)S(1)}, bf16[256,384]{1,0:T(8,128)(2,1)S(1)}, u32[]{:S(2)}, u32[]{:S(2)}) collective-permute-start(bf16[256,384]{1,0:T(8,128)(2,1)S(1)} %pad_maximum_fusion.2.refs_4_), channel_id=1, source_target_pairs={{0,4},{2,6},{4,0},{6,2},{8,12},{10,14},{12,8},{14,10},{16,20},{18,... | collective-permute-start | bytes 589832 | tf_op jit(solution)/shard_map/ppermute | solution.py:54
  8.6 1.6 %collective-permute-start.1 = (bf16[384,384]{1,0:T(8,128)(2,1)S(1)}, bf16[384,384]{1,0:T(8,128)(2,1)S(1)}, u32[]{:S(2)}, u32[]{:S(2)}) collective-permute-start(bf16[384,384]{1,0:T(8,128)(2,1)S(1)} %pad_maximum_fusion), channel_id=1, source_target_pairs={{0,8},{2,10},{4,12},{6,14},{8,0},{10,2},{12,4},{14,6},{16,24},{18,... | collective-permute-start | bytes 884744 | tf_op jit(solution)/shard_map/ppermute | solution.py:51
  10.3 0.7 broadcast_in_dim.3.gain
  11.0 2.5 %collective-permute-done.refs_3_.refs_0_.refs_2_.refs_12_ = bf16[256,384]{1,0:T(8,128)(2,1)S(1)} collective-permute-done((bf16[256,384]{1,0:T(8,128)(2,1)S(1)}, bf16[256,384]{1,0:T(8,128)(2,1)S(1)}, u32[]{:S(2)}, u32[]{:S(2)}) %collective-permute-start) | collective-permute-done | bytes 196640 | tf_op jit(solution)/shard_map/ppermute | solution.py:54
  13.4 1.0 %copy-done = bf16[128,1536]{1,0:T(8,128)(2,1)S(1)} copy-done((bf16[128,1536]{1,0:T(8,128)(2,1)S(1)}, bf16[128,1536]{1,0:T(8,128)(2,1)}, u32[]{:S(2)}) %copy-start) | copy-done | bytes 393240
  14.4 1.0 %copy-done.1 = bf16[128,1536]{1,0:T(8,128)(2,1)S(1)} copy-done((bf16[128,1536]{1,0:T(8,128)(2,1)S(1)}, bf16[128,1536]{1,0:T(8,128)(2,1)}, u32[]{:S(2)}) %copy-start.1) | copy-done | bytes 393240
  15.4 1.0 %copy-done.2 = bf16[128,1536]{1,0:T(8,128)(2,1)S(1)} copy-done((bf16[128,1536]{1,0:T(8,128)(2,1)S(1)}, bf16[128,1536]{1,0:T(8,128)(2,1)}, u32[]{:S(2)}) %copy-start.2) | copy-done | bytes 393240
  16.5 0.0 copy-start.3
  16.5 0.9 %copy-done.3 = bf16[1536,64]{0,1:T(8,128)(2,1)S(1)} copy-done((bf16[1536,64]{0,1:T(8,128)(2,1)S(1)}, bf16[1536,64]{0,1:T(8,128)(2,1)}, u32[]{:S(2)}) %copy-start.3) | copy-done | bytes 196632
  17.4 0.7 copy-done.5
  18.1 0.7 copy-done.6
  18.7 0.7 copy-done.7
  19.4 0.7 shard_map.114
  20.0 0.4 collective-permute-done.2.refs_1_.refs_2_.refs_5_
  20.4 3.5 %collective-permute-start.3 = (bf16[384,384]{1,0:T(8,128)(2,1)S(1)}, bf16[384,384]{1,0:T(8,128)(2,1)S(1)}, u32[]{:S(2)}, u32[]{:S(2)}) collective-permute-start(bf16[384,384]{1,0:T(8,128)(2,1)S(1)} %shard_map.115), channel_id=1, source_target_pairs={{0,24},{2,26},{4,28},{6,30},{8,16},{10,18},{12,20},{14,22},{16,8},... | collective-permute-start | bytes 884744 | tf_op jit(solution)/shard_map/ppermute | solution.py:51
  24.0 1.5 %collective-permute-start.9 = (bf16[112,1536]{1,0:T(8,128)(2,1)S(1)}, bf16[112,1536]{1,0:T(8,128)(2,1)S(1)}, u32[]{:S(2)}, u32[]{:S(2)}) collective-permute-start(bf16[112,1536]{1,0:T(8,128)(2,1)S(1)} %get-tuple-element.26.refs_2_), channel_id=1, source_target_pairs={{0,1},{1,0},{2,3},{3,2},{4,5},{5,4},{6,7},{7,6},{8,9},{9,8},{10,11... | collective-permute-start | bytes 1032200 | tf_op jit(solution)/shard_map/ppermute | solution.py:57
  25.5 0.0 collective-permute-done.1.refs_1_.refs_4_
  25.5 1.5 %collective-permute-start.7 = (bf16[256,384]{1,0:T(8,128)(2,1)S(1)}, bf16[256,384]{1,0:T(8,128)(2,1)S(1)}, u32[]{:S(2)}, u32[]{:S(2)}) collective-permute-start(bf16[256,384]{1,0:T(8,128)(2,1)S(1)} %slice.12.refs_6_), channel_id=1, source_target_pairs={{0,4},{2,6},{4,0},{6,2},{8,12},{10,14},{12,8},{14,10},{16,20},{18,... | collective-permute-start | bytes 589832 | tf_op jit(solution)/shard_map/ppermute | solution.py:54
  27.0 0.7 collective-permute-start.8
  27.7 3.5 %collective-permute-done.3.refs_3_.refs_6_ = bf16[384,384]{1,0:T(8,128)(2,1)S(1)} collective-permute-done((bf16[384,384]{1,0:T(8,128)(2,1)S(1)}, bf16[384,384]{1,0:T(8,128)(2,1)S(1)}, u32[]{:S(2)}, u32[]{:S(2)}) %collective-permute-start.3) | collective-permute-done | bytes 294944 | tf_op jit(solution)/shard_map/ppermute | solution.py:51
  31.2 0.0 collective-permute-start.11
  31.2 2.2 %collective-permute-done.7.refs_1_.refs_14_ = bf16[256,384]{1,0:T(8,128)(2,1)S(1)} collective-permute-done((bf16[256,384]{1,0:T(8,128)(2,1)S(1)}, bf16[256,384]{1,0:T(8,128)(2,1)S(1)}, u32[]{:S(2)}, u32[]{:S(2)}) %collective-permute-start.7) | collective-permute-done | bytes 196640 | tf_op jit(solution)/shard_map/ppermute | solution.py:54
  33.4 0.0 collective-permute-start.5
  33.4 2.6 %collective-permute-done.8.refs_2_.refs_16_ = bf16[256,384]{1,0:T(8,128)(2,1)S(1)} collective-permute-done((bf16[256,384]{1,0:T(8,128)(2,1)S(1)}, bf16[256,384]{1,0:T(8,128)(2,1)S(1)}, u32[]{:S(2)}, u32[]{:S(2)}) %collective-permute-start.8) | collective-permute-done | bytes 196640 | tf_op jit(solution)/shard_map/ppermute | solution.py:54
  36.0 0.0 collective-permute-start.6
  36.0 0.0 collective-permute-done.9.refs_3_
  36.0 0.5 collective-permute-start.12
  36.5 0.1 collective-permute-start.13
  36.6 0.4 collective-permute-start.10
  37.0 1.5 %collective-permute-start.14 = (bf16[256,384]{1,0:T(8,128)(2,1)S(1)}, bf16[256,384]{1,0:T(8,128)(2,1)S(1)}, u32[]{:S(2)}, u32[]{:S(2)}) collective-permute-start(bf16[256,384]{1,0:T(8,128)(2,1)S(1)} %shard_map.117.refs_10_), channel_id=1, source_target_pairs={{0,4},{2,6},{4,0},{6,2},{8,12},{10,14},{12,8},{14,10},{16,20},{18,... | collective-permute-start | bytes 589832 | tf_op jit(solution)/shard_map/ppermute | solution.py:54
  38.5 0.0 collective-permute-done.13.refs_17_
  38.5 0.0 collective-permute-done.10.refs_11_
  38.5 0.0 slice-start
  38.5 0.0 slice-start.1
  38.5 0.0 slice-start.2
  38.5 4.2 %shard_map.118 = (f32[3,512,128]{2,1,0:T(8,128)S(1)}, f32[3,512,128]{2,1,0:T(8,128)S(1)}, f32[3,512,128]{2,1,0:T(8,128)S(1)}) custom-call(f32[32,128]{1,0:T(8,128)S(1)} %get-tuple-element.24.refs_3_.bias, bf16[128,384]{1,0:T(8,128)(2,1)S(1)} %get-tuple-element.25.refs_0_.refs_3_, bf16[384,384]{1,0:T(8,128)(2,1)S(1)} %collective-permute-done.1.refs_1_.refs_4_, ...), custom_call_target="tpu_custom_call" | custom-call | flops 5637144576 | tf_op jit(solution)/shard_map/pallas_call | solution.py:215
  42.8 1.1 %collective-permute-done.14.refs_0_ = bf16[256,384]{1,0:T(8,128)(2,1)S(1)} collective-permute-done((bf16[256,384]{1,0:T(8,128)(2,1)S(1)}, bf16[256,384]{1,0:T(8,128)(2,1)S(1)}, u32[]{:S(2)}, u32[]{:S(2)}) %collective-permute-start.14) | collective-permute-done | bytes 196640 | tf_op jit(solution)/shard_map/ppermute | solution.py:54
  43.9 1.4 %collective-permute-done.15.refs_8_ = bf16[256,384]{1,0:T(8,128)(2,1)S(1)} collective-permute-done((bf16[256,384]{1,0:T(8,128)(2,1)S(1)}, bf16[256,384]{1,0:T(8,128)(2,1)S(1)}, u32[]{:S(2)}, u32[]{:S(2)}) %collective-permute-start.15) | collective-permute-done | bytes 196640 | tf_op jit(solution)/shard_map/ppermute | solution.py:54
  45.3 0.9 %shard_map.120 = (bf16[64,384]{1,0:T(8,128)(2,1)S(1)}, bf16[64,384]{1,0:T(8,128)(2,1)S(1)}, bf16[64,384]{1,0:T(8,128)(2,1)S(1)}, bf16[64,384]{1,0:T(8,128)(2,1)S...) custom-call(f32[32,128]{1,0:T(8,128)S(1)} %get-tuple-element.24.refs, ...), custom_call_target="tpu_custom_call" | custom-call | flops 805306368 | tf_op jit(solution)/shard_map/pallas_call | solution.py:215
  46.2 1.4 %collective-permute-start.19 = (bf16[64,384]{1,0:T(8,128)(2,1)S(1)}, bf16[64,384]{1,0:T(8,128)(2,1)S(1)}, u32[]{:S(2)}, u32[]{:S(2)}) collective-permute-start(bf16[64,384]{1,0:T(8,128)(2,1)S(1)} %get-tuple-element.34), channel_id=1, source_target_pairs={{0,8},{2,10},{4,12},{6,14},{8,0},{10,2},{12,4},{14,6},{16,24},{18,... | collective-permute-start | bytes 147464 | tf_op jit(solution)/shard_map/ppermute | solution.py:51
  47.6 0.0 collective-permute-start.20
  47.6 3.1 %collective-permute-start.21 = (bf16[64,384]{1,0:T(8,128)(2,1)S(1)}, bf16[64,384]{1,0:T(8,128)(2,1)S(1)}, u32[]{:S(2)}, u32[]{:S(2)}) collective-permute-start(bf16[64,384]{1,0:T(8,128)(2,1)S(1)} %get-tuple-element.36), channel_id=1, source_target_pairs={{0,24},{2,26},{4,28},{6,30},{8,16},{10,18},{12,20},{14,22},{16,8},... | collective-permute-start | bytes 147464 | tf_op jit(solution)/shard_map/ppermute | solution.py:51
  50.7 0.6 shard_map.123.refs_4_
  51.2 0.0 collective-permute-done.19.refs_0_
  51.2 3.2 %collective-permute-done.20.refs_1_ = bf16[64,384]{1,0:T(8,128)(2,1)S(1)} collective-permute-done((bf16[64,384]{1,0:T(8,128)(2,1)S(1)}, bf16[64,384]{1,0:T(8,128)(2,1)S(1)}, u32[]{:S(2)}, u32[]{:S(2)}) %collective-permute-start.20) | collective-permute-done | bytes 49184 | tf_op jit(solution)/shard_map/ppermute | solution.py:51
  54.5 1.4 %shard_map.124 = bf16[64,3072]{1,0:T(8,128)(2,1)S(1)} custom-call(bf16[64,384]{1,0:T(8,128)(2,1)S(1)} %collective-permute-done.19.refs_0_, bf16[64,384]{1,0:T(8,128)(2,1)S(1)} %collective-permute-done.20.refs_1_, bf16[64,384]{1,0:T(8,128)(2,1)S(1)} %collective-permute-done.21.refs_2_, bf16[1536,3072]{1,0:T(8,128)(2,1)S(1)} %bitcast.2, ...), custom_call_target="tpu_custom_call" | custom-call | tf_op jit(solution)/shard_map/pallas_call | solution.py:251
  55.9 1.3 %collective-permute-start.22 = (bf16[64,3072]{1,0:T(8,128)(2,1)S(1)}, bf16[64,3072]{1,0:T(8,128)(2,1)S(1)}, u32[]{:S(2)}, u32[]{:S(2)}) collective-permute-start(bf16[64,3072]{1,0:T(8,128)(2,1)S(1)} %shard_map.124), channel_id=1, source_target_pairs={{0,1},{1,0},{2,3},{3,2},{4,5},{5,4},{6,7},{7,6},{8,9},{9,8},{10,11... | collective-permute-start | bytes 1179656 | tf_op jit(solution)/shard_map/ppermute | solution.py:57
  57.1 1.4 %collective-permute-start.16 = (bf16[64,384]{1,0:T(8,128)(2,1)S(1)}, bf16[64,384]{1,0:T(8,128)(2,1)S(1)}, u32[]{:S(2)}, u32[]{:S(2)}) collective-permute-start(bf16[64,384]{1,0:T(8,128)(2,1)S(1)} %get-tuple-element.30), channel_id=1, source_target_pairs={{0,8},{2,10},{4,12},{6,14},{8,0},{10,2},{12,4},{14,6},{16,24},{18,... | collective-permute-start | bytes 147464 | tf_op jit(solution)/shard_map/ppermute | solution.py:51
  58.5 1.0 %collective-permute-start.17 = (bf16[64,384]{1,0:T(8,128)(2,1)S(1)}, bf16[64,384]{1,0:T(8,128)(2,1)S(1)}, u32[]{:S(2)}, u32[]{:S(2)}) collective-permute-start(bf16[64,384]{1,0:T(8,128)(2,1)S(1)} %get-tuple-element.31), channel_id=1, source_target_pairs={{0,16},{2,18},{4,20},{6,22},{8,24},{10,26},{12,28},{14,30},{16,0},... | collective-permute-start | bytes 147464 | tf_op jit(solution)/shard_map/ppermute | solution.py:51
  59.5 2.0 %collective-permute-start.18 = (bf16[64,384]{1,0:T(8,128)(2,1)S(1)}, bf16[64,384]{1,0:T(8,128)(2,1)S(1)}, u32[]{:S(2)}, u32[]{:S(2)}) collective-permute-start(bf16[64,384]{1,0:T(8,128)(2,1)S(1)} %get-tuple-element.32), channel_id=1, source_target_pairs={{0,24},{2,26},{4,28},{6,30},{8,16},{10,18},{12,20},{14,22},{16,8},... | collective-permute-start | bytes 147464 | tf_op jit(solution)/shard_map/ppermute | solution.py:51
  61.5 0.5 shard_map.121.refs_4_
  62.1 2.2 %collective-permute-done.17.refs_1_ = bf16[64,384]{1,0:T(8,128)(2,1)S(1)} collective-permute-done((bf16[64,384]{1,0:T(8,128)(2,1)S(1)}, bf16[64,384]{1,0:T(8,128)(2,1)S(1)}, u32[]{:S(2)}, u32[]{:S(2)}) %collective-permute-start.17) | collective-permute-done | bytes 49184 | tf_op jit(solution)/shard_map/ppermute | solution.py:51
  64.3 1.1 %collective-permute-done.18.refs_2_ = bf16[64,384]{1,0:T(8,128)(2,1)S(1)} collective-permute-done((bf16[64,384]{1,0:T(8,128)(2,1)S(1)}, bf16[64,384]{1,0:T(8,128)(2,1)S(1)}, u32[]{:S(2)}, u32[]{:S(2)}) %collective-permute-start.18) | collective-permute-done | bytes 49184 | tf_op jit(solution)/shard_map/ppermute | solution.py:51
  65.4 1.4 %shard_map.122.refs_0_ = f32[64,3072]{1,0:T(8,128)S(1)} custom-call(bf16[64,384]{1,0:T(8,128)(2,1)S(1)} %collective-permute-done.16.refs_0_, bf16[64,384]{1,0:T(8,128)(2,1)S(1)} %collective-permute-done.17.refs_1_, bf16[64,384]{1,0:T(8,128)(2,1)S(1)} %collective-permute-done.18.refs_2_, bf16[1536,3072]{1,0:T(8,128)(2,1)S(1)} %bitcast.2, ...), custom_call_target="tpu_custom_call" | custom-call | tf_op jit(solution)/shard_map/pallas_call | solution.py:251
  66.8 0.4 shard_map.125
  67.2 1.5 %collective-permute-start.23 = (f32[32,128]{1,0:T(8,128)S(1)}, f32[32,128]{1,0:T(8,128)S(1)}, u32[]{:S(2)}, u32[]{:S(2)}) collective-permute-start(f32[32,128]{1,0:T(8,128)S(1)} %get-tuple-element.38), channel_id=1, source_target_pairs={{0,4},{1,5},{2,6},{3,7},{4,8},{5,9},{6,10},{7,11},{8,12},{9,13},{1... | collective-permute-start | bytes 49160 | tf_op jit(solution)/shard_map/ppermute | solution.py:65
  68.8 2.0 %collective-permute-start.24 = (f32[32,128]{1,0:T(8,128)S(1)}, f32[32,128]{1,0:T(8,128)S(1)}, u32[]{:S(2)}, u32[]{:S(2)}) collective-permute-start(f32[32,128]{1,0:T(8,128)S(1)} %get-tuple-element.38), channel_id=1, source_target_pairs={{0,5},{1,4},{2,7},{3,6},{4,9},{5,8},{6,11},{7,10},{8,13},{9,12},{1... | collective-permute-start | bytes 49160 | tf_op jit(solution)/shard_map/ppermute | solution.py:65
  70.8 0.5 collective-permute-start.25
  71.3 2.4 %collective-permute-done.23.refs_0_ = f32[32,128]{1,0:T(8,128)S(1)} collective-permute-done((f32[32,128]{1,0:T(8,128)S(1)}, f32[32,128]{1,0:T(8,128)S(1)}, u32[]{:S(2)}, u32[]{:S(2)}) %collective-permute-start.23) | collective-permute-done | bytes 16416 | tf_op jit(solution)/shard_map/ppermute | solution.py:65
  73.7 2.4 %collective-permute-done.24.refs_1_ = f32[32,128]{1,0:T(8,128)S(1)} collective-permute-done((f32[32,128]{1,0:T(8,128)S(1)}, f32[32,128]{1,0:T(8,128)S(1)}, u32[]{:S(2)}, u32[]{:S(2)}) %collective-permute-start.24) | collective-permute-done | bytes 16416 | tf_op jit(solution)/shard_map/ppermute | solution.py:65
  76.1 0.6 shard_map.126
  (34 shorter events, 0.2 us)
Async XLA Ops:
  2.9 17.5 %collective-permute-start.2 = (bf16[384,384]{1,0:T(8,128)(2,1)S(1)}, bf16[384,384]{1,0:T(8,128)(2,1)S(1)}, u32[]{:S(2)}, u32[]{:S(2)}) collective-permute-start(bf16[384,384]{1,0:T(8,128)(2,1)S(1)} %pad_maximum_fusion.1), channel_id=1, source_target_pairs={{0,16},{2,18},{4,20},{6,22},{8,24},{10,26},{12,28},{14,30},{16,0},... | collective-permute-start | bytes 884744 | tf_op jit(solution)/shard_map/ppermute | solution.py:51
  7.0 6.4 %collective-permute-start = (bf16[256,384]{1,0:T(8,128)(2,1)S(1)}, bf16[256,384]{1,0:T(8,128)(2,1)S(1)}, u32[]{:S(2)}, u32[]{:S(2)}) collective-permute-start(bf16[256,384]{1,0:T(8,128)(2,1)S(1)} %pad_maximum_fusion.2.refs_4_), channel_id=1, source_target_pairs={{0,4},{2,6},{4,0},{6,2},{8,12},{10,14},{12,8},{14,10},{16,20},{18,... | collective-permute-start | bytes 589832 | tf_op jit(solution)/shard_map/ppermute | solution.py:54
  8.6 16.8 %collective-permute-start.1 = (bf16[384,384]{1,0:T(8,128)(2,1)S(1)}, bf16[384,384]{1,0:T(8,128)(2,1)S(1)}, u32[]{:S(2)}, u32[]{:S(2)}) collective-permute-start(bf16[384,384]{1,0:T(8,128)(2,1)S(1)} %pad_maximum_fusion), channel_id=1, source_target_pairs={{0,8},{2,10},{4,12},{6,14},{8,0},{10,2},{12,4},{14,6},{16,24},{18,... | collective-permute-start | bytes 884744 | tf_op jit(solution)/shard_map/ppermute | solution.py:51
  13.4 1.0 %copy-start = (bf16[128,1536]{1,0:T(8,128)(2,1)S(1)}, bf16[128,1536]{1,0:T(8,128)(2,1)}, u32[]{:S(2)}) copy-start(bf16[128,1536]{1,0:T(8,128)(2,1)} %refs_1_.3) | copy-start | bytes 1179652
  14.4 1.0 %copy-start.1 = (bf16[128,1536]{1,0:T(8,128)(2,1)S(1)}, bf16[128,1536]{1,0:T(8,128)(2,1)}, u32[]{:S(2)}) copy-start(bf16[128,1536]{1,0:T(8,128)(2,1)} %refs_0_.1) | copy-start | bytes 1179652
  15.4 1.0 %copy-start.2 = (bf16[128,1536]{1,0:T(8,128)(2,1)S(1)}, bf16[128,1536]{1,0:T(8,128)(2,1)}, u32[]{:S(2)}) copy-start(bf16[128,1536]{1,0:T(8,128)(2,1)} %refs_2_.1) | copy-start | bytes 1179652
  16.5 0.9 %copy-start.3 = (bf16[1536,64]{0,1:T(8,128)(2,1)S(1)}, bf16[1536,64]{0,1:T(8,128)(2,1)}, u32[]{:S(2)}) copy-start(bf16[1536,64]{0,1:T(8,128)(2,1)} %param.16) | copy-start | bytes 589828
  17.4 0.7 copy-start.5
  18.1 0.7 copy-start.6
  18.7 0.7 copy-start.7
  20.4 10.8 %collective-permute-start.3 = (bf16[384,384]{1,0:T(8,128)(2,1)S(1)}, bf16[384,384]{1,0:T(8,128)(2,1)S(1)}, u32[]{:S(2)}, u32[]{:S(2)}) collective-permute-start(bf16[384,384]{1,0:T(8,128)(2,1)S(1)} %shard_map.115), channel_id=1, source_target_pairs={{0,24},{2,26},{4,28},{6,30},{8,16},{10,18},{12,20},{14,22},{16,8},... | collective-permute-start | bytes 884744 | tf_op jit(solution)/shard_map/ppermute | solution.py:51
  24.0 12.0 %collective-permute-start.9 = (bf16[112,1536]{1,0:T(8,128)(2,1)S(1)}, bf16[112,1536]{1,0:T(8,128)(2,1)S(1)}, u32[]{:S(2)}, u32[]{:S(2)}) collective-permute-start(bf16[112,1536]{1,0:T(8,128)(2,1)S(1)} %get-tuple-element.26.refs_2_), channel_id=1, source_target_pairs={{0,1},{1,0},{2,3},{3,2},{4,5},{5,4},{6,7},{7,6},{8,9},{9,8},{10,11... | collective-permute-start | bytes 1032200 | tf_op jit(solution)/shard_map/ppermute | solution.py:57
  25.5 7.9 %collective-permute-start.7 = (bf16[256,384]{1,0:T(8,128)(2,1)S(1)}, bf16[256,384]{1,0:T(8,128)(2,1)S(1)}, u32[]{:S(2)}, u32[]{:S(2)}) collective-permute-start(bf16[256,384]{1,0:T(8,128)(2,1)S(1)} %slice.12.refs_6_), channel_id=1, source_target_pairs={{0,4},{2,6},{4,0},{6,2},{8,12},{10,14},{12,8},{14,10},{16,20},{18,... | collective-permute-start | bytes 589832 | tf_op jit(solution)/shard_map/ppermute | solution.py:54
  27.0 9.0 %collective-permute-start.8 = (bf16[256,384]{1,0:T(8,128)(2,1)S(1)}, bf16[256,384]{1,0:T(8,128)(2,1)S(1)}, u32[]{:S(2)}, u32[]{:S(2)}) collective-permute-start(bf16[256,384]{1,0:T(8,128)(2,1)S(1)} %shard_map.116.refs_8_), channel_id=1, source_target_pairs={{0,4},{2,6},{4,0},{6,2},{8,12},{10,14},{12,8},{14,10},{16,20},{18,... | collective-permute-start | bytes 589832 | tf_op jit(solution)/shard_map/ppermute | solution.py:54
  27.7 8.8 %collective-permute-start.4 = (bf16[256,384]{1,0:T(8,128)(2,1)S(1)}, bf16[256,384]{1,0:T(8,128)(2,1)S(1)}, u32[]{:S(2)}, u32[]{:S(2)}) collective-permute-start(bf16[256,384]{1,0:T(8,128)(2,1)S(1)} %pad_maximum_fusion.2.refs_4_), channel_id=1, source_target_pairs={{0,2},{2,0},{4,6},{6,4},{8,10},{10,8},{12,14},{14,12},{16,18},{18,... | collective-permute-start | bytes 589832 | tf_op jit(solution)/shard_map/ppermute | solution.py:54
  31.2 5.4 %collective-permute-start.11 = (bf16[256,384]{1,0:T(8,128)(2,1)S(1)}, bf16[256,384]{1,0:T(8,128)(2,1)S(1)}, u32[]{:S(2)}, u32[]{:S(2)}) collective-permute-start(bf16[256,384]{1,0:T(8,128)(2,1)S(1)} %collective-permute-done.refs_3_.refs_0_.refs_2_.refs_12_), channel_id=1, source_target_pairs={{0,2},{2,0},{4,6},{6,4},{8,10},{10,8},{12,14},{14,12},{16,18},{18,... | collective-permute-start | bytes 589832 | tf_op jit(solution)/shard_map/ppermute | solution.py:54
  33.4 3.6 %collective-permute-start.5 = (bf16[256,384]{1,0:T(8,128)(2,1)S(1)}, bf16[256,384]{1,0:T(8,128)(2,1)S(1)}, u32[]{:S(2)}, u32[]{:S(2)}) collective-permute-start(bf16[256,384]{1,0:T(8,128)(2,1)S(1)} %slice.12.refs_6_), channel_id=1, source_target_pairs={{0,2},{2,0},{4,6},{6,4},{8,10},{10,8},{12,14},{14,12},{16,18},{18,... | collective-permute-start | bytes 589832 | tf_op jit(solution)/shard_map/ppermute | solution.py:54
  36.0 2.5 %collective-permute-start.6 = (bf16[256,384]{1,0:T(8,128)(2,1)S(1)}, bf16[256,384]{1,0:T(8,128)(2,1)S(1)}, u32[]{:S(2)}, u32[]{:S(2)}) collective-permute-start(bf16[256,384]{1,0:T(8,128)(2,1)S(1)} %shard_map.116.refs_8_), channel_id=1, source_target_pairs={{0,2},{2,0},{4,6},{6,4},{8,10},{10,8},{12,14},{14,12},{16,18},{18,... | collective-permute-start | bytes 589832 | tf_op jit(solution)/shard_map/ppermute | solution.py:54
  36.0 2.5 %collective-permute-start.12 = (bf16[256,384]{1,0:T(8,128)(2,1)S(1)}, bf16[256,384]{1,0:T(8,128)(2,1)S(1)}, u32[]{:S(2)}, u32[]{:S(2)}) collective-permute-start(bf16[256,384]{1,0:T(8,128)(2,1)S(1)} %collective-permute-done.7.refs_1_.refs_14_), channel_id=1, source_target_pairs={{0,2},{2,0},{4,6},{6,4},{8,10},{10,8},{12,14},{14,12},{16,18},{18,... | collective-permute-start | bytes 589832 | tf_op jit(solution)/shard_map/ppermute | solution.py:54
  36.5 2.0 %collective-permute-start.13 = (bf16[256,384]{1,0:T(8,128)(2,1)S(1)}, bf16[256,384]{1,0:T(8,128)(2,1)S(1)}, u32[]{:S(2)}, u32[]{:S(2)}) collective-permute-start(bf16[256,384]{1,0:T(8,128)(2,1)S(1)} %collective-permute-done.8.refs_2_.refs_16_), channel_id=1, source_target_pairs={{0,2},{2,0},{4,6},{6,4},{8,10},{10,8},{12,14},{14,12},{16,18},{18,... | collective-permute-start | bytes 589832 | tf_op jit(solution)/shard_map/ppermute | solution.py:54
  36.6 1.9 %collective-permute-start.10 = (bf16[256,384]{1,0:T(8,128)(2,1)S(1)}, bf16[256,384]{1,0:T(8,128)(2,1)S(1)}, u32[]{:S(2)}, u32[]{:S(2)}) collective-permute-start(bf16[256,384]{1,0:T(8,128)(2,1)S(1)} %shard_map.117.refs_10_), channel_id=1, source_target_pairs={{0,2},{2,0},{4,6},{6,4},{8,10},{10,8},{12,14},{14,12},{16,18},{18,... | collective-permute-start | bytes 589832 | tf_op jit(solution)/shard_map/ppermute | solution.py:54
  37.0 6.9 %collective-permute-start.14 = (bf16[256,384]{1,0:T(8,128)(2,1)S(1)}, bf16[256,384]{1,0:T(8,128)(2,1)S(1)}, u32[]{:S(2)}, u32[]{:S(2)}) collective-permute-start(bf16[256,384]{1,0:T(8,128)(2,1)S(1)} %shard_map.117.refs_10_), channel_id=1, source_target_pairs={{0,4},{2,6},{4,0},{6,2},{8,12},{10,14},{12,8},{14,10},{16,20},{18,... | collective-permute-start | bytes 589832 | tf_op jit(solution)/shard_map/ppermute | solution.py:54
  38.5 12.2 %slice-start = ((s8[9437184]{0:T(1024)(128)(4,1)}), s8[4194304]{0:T(1024)(128)(4,1)S(1)}, s32[]{:S(2)}) async-start(s8[9437184]{0:T(1024)(128)(4,1)} %bitcast.1), calls=%async_computation | async-start | bytes 8388608
  38.5 12.1 %slice-start.1 = ((s8[9437184]{0:T(1024)(128)(4,1)}), s8[4194304]{0:T(1024)(128)(4,1)S(1)}, s32[]{:S(2)}) async-start(s8[9437184]{0:T(1024)(128)(4,1)} %bitcast.1), calls=%async_computation.1 | async-start | bytes 8388608
  38.5 12.1 %slice-start.2 = ((s8[9437184]{0:T(1024)(128)(4,1)}), s8[1048576]{0:T(1024)(128)(4,1)S(1)}, s32[]{:S(2)}) async-start(s8[9437184]{0:T(1024)(128)(4,1)} %bitcast.1), calls=%async_computation.2 | async-start | bytes 2097152
  43.9 1.4 %collective-permute-start.15 = (bf16[256,384]{1,0:T(8,128)(2,1)S(1)}, bf16[256,384]{1,0:T(8,128)(2,1)S(1)}, u32[]{:S(2)}, u32[]{:S(2)}) collective-permute-start(bf16[256,384]{1,0:T(8,128)(2,1)S(1)} %shard_map.119.refs_7_), channel_id=1, source_target_pairs={{0,2},{2,0},{4,6},{6,4},{8,10},{10,8},{12,14},{14,12},{16,18},{18,... | collective-permute-start | bytes 589832 | tf_op jit(solution)/shard_map/ppermute | solution.py:54
  46.2 5.0 %collective-permute-start.19 = (bf16[64,384]{1,0:T(8,128)(2,1)S(1)}, bf16[64,384]{1,0:T(8,128)(2,1)S(1)}, u32[]{:S(2)}, u32[]{:S(2)}) collective-permute-start(bf16[64,384]{1,0:T(8,128)(2,1)S(1)} %get-tuple-element.34), channel_id=1, source_target_pairs={{0,8},{2,10},{4,12},{6,14},{8,0},{10,2},{12,4},{14,6},{16,24},{18,... | collective-permute-start | bytes 147464 | tf_op jit(solution)/shard_map/ppermute | solution.py:51
  47.6 6.9 %collective-permute-start.20 = (bf16[64,384]{1,0:T(8,128)(2,1)S(1)}, bf16[64,384]{1,0:T(8,128)(2,1)S(1)}, u32[]{:S(2)}, u32[]{:S(2)}) collective-permute-start(bf16[64,384]{1,0:T(8,128)(2,1)S(1)} %get-tuple-element.35), channel_id=1, source_target_pairs={{0,16},{2,18},{4,20},{6,22},{8,24},{10,26},{12,28},{14,30},{16,0},... | collective-permute-start | bytes 147464 | tf_op jit(solution)/shard_map/ppermute | solution.py:51
  47.6 6.9 %collective-permute-start.21 = (bf16[64,384]{1,0:T(8,128)(2,1)S(1)}, bf16[64,384]{1,0:T(8,128)(2,1)S(1)}, u32[]{:S(2)}, u32[]{:S(2)}) collective-permute-start(bf16[64,384]{1,0:T(8,128)(2,1)S(1)} %get-tuple-element.36), channel_id=1, source_target_pairs={{0,24},{2,26},{4,28},{6,30},{8,16},{10,18},{12,20},{14,22},{16,8},... | collective-permute-start | bytes 147464 | tf_op jit(solution)/shard_map/ppermute | solution.py:51
  55.9 10.9 %collective-permute-start.22 = (bf16[64,3072]{1,0:T(8,128)(2,1)S(1)}, bf16[64,3072]{1,0:T(8,128)(2,1)S(1)}, u32[]{:S(2)}, u32[]{:S(2)}) collective-permute-start(bf16[64,3072]{1,0:T(8,128)(2,1)S(1)} %shard_map.124), channel_id=1, source_target_pairs={{0,1},{1,0},{2,3},{3,2},{4,5},{5,4},{6,7},{7,6},{8,9},{9,8},{10,11... | collective-permute-start | bytes 1179656 | tf_op jit(solution)/shard_map/ppermute | solution.py:57
  57.1 4.9 %collective-permute-start.16 = (bf16[64,384]{1,0:T(8,128)(2,1)S(1)}, bf16[64,384]{1,0:T(8,128)(2,1)S(1)}, u32[]{:S(2)}, u32[]{:S(2)}) collective-permute-start(bf16[64,384]{1,0:T(8,128)(2,1)S(1)} %get-tuple-element.30), channel_id=1, source_target_pairs={{0,8},{2,10},{4,12},{6,14},{8,0},{10,2},{12,4},{14,6},{16,24},{18,... | collective-permute-start | bytes 147464 | tf_op jit(solution)/shard_map/ppermute | solution.py:51
  58.5 5.8 %collective-permute-start.17 = (bf16[64,384]{1,0:T(8,128)(2,1)S(1)}, bf16[64,384]{1,0:T(8,128)(2,1)S(1)}, u32[]{:S(2)}, u32[]{:S(2)}) collective-permute-start(bf16[64,384]{1,0:T(8,128)(2,1)S(1)} %get-tuple-element.31), channel_id=1, source_target_pairs={{0,16},{2,18},{4,20},{6,22},{8,24},{10,26},{12,28},{14,30},{16,0},... | collective-permute-start | bytes 147464 | tf_op jit(solution)/shard_map/ppermute | solution.py:51
  59.5 5.9 %collective-permute-start.18 = (bf16[64,384]{1,0:T(8,128)(2,1)S(1)}, bf16[64,384]{1,0:T(8,128)(2,1)S(1)}, u32[]{:S(2)}, u32[]{:S(2)}) collective-permute-start(bf16[64,384]{1,0:T(8,128)(2,1)S(1)} %get-tuple-element.32), channel_id=1, source_target_pairs={{0,24},{2,26},{4,28},{6,30},{8,16},{10,18},{12,20},{14,22},{16,8},... | collective-permute-start | bytes 147464 | tf_op jit(solution)/shard_map/ppermute | solution.py:51
  61.5 5.3 %copy-start.4 = (f32[64,128]{1,0:T(8,128)S(1)}, f32[64,128]{1,0:T(8,128)}, u32[]{:S(2)}) copy-start(f32[64,128]{1,0:T(8,128)} %refs_4_.1) | copy-start | bytes 98308
  67.2 6.5 %collective-permute-start.23 = (f32[32,128]{1,0:T(8,128)S(1)}, f32[32,128]{1,0:T(8,128)S(1)}, u32[]{:S(2)}, u32[]{:S(2)}) collective-permute-start(f32[32,128]{1,0:T(8,128)S(1)} %get-tuple-element.38), channel_id=1, source_target_pairs={{0,4},{1,5},{2,6},{3,7},{4,8},{5,9},{6,10},{7,11},{8,12},{9,13},{1... | collective-permute-start | bytes 49160 | tf_op jit(solution)/shard_map/ppermute | solution.py:65
  68.8 7.3 %collective-permute-start.24 = (f32[32,128]{1,0:T(8,128)S(1)}, f32[32,128]{1,0:T(8,128)S(1)}, u32[]{:S(2)}, u32[]{:S(2)}) collective-permute-start(f32[32,128]{1,0:T(8,128)S(1)} %get-tuple-element.38), channel_id=1, source_target_pairs={{0,5},{1,4},{2,7},{3,6},{4,9},{5,8},{6,11},{7,10},{8,13},{9,12},{1... | collective-permute-start | bytes 49160 | tf_op jit(solution)/shard_map/ppermute | solution.py:65
  70.8 5.3 %collective-permute-start.25 = (f32[32,128]{1,0:T(8,128)S(1)}, f32[32,128]{1,0:T(8,128)S(1)}, u32[]{:S(2)}, u32[]{:S(2)}) collective-permute-start(f32[32,128]{1,0:T(8,128)S(1)} %get-tuple-element.39.refs_2_), channel_id=1, source_target_pairs={{0,1},{1,0},{2,3},{3,2},{4,5},{5,4},{6,7},{7,6},{8,9},{9,8},{10,11... | collective-permute-start | bytes 49160 | tf_op jit(solution)/shard_map/ppermute | solution.py:57

commit v5 on v4

--- a/solution.py
+++ b/solution.py
@@ -332,7 +332,7 @@
     plan = Plan(queries)
     split, tensors = plan.split, plan.tensors
 
-    far, near = list(range(1, split)), [0]
+    far = list(range(1, split))
     own = pack(plan, 0, keys, values)
     if split == 4 and plan.members == 4:
         two = plan.to_part(pack(plan, 2, keys, values, queries), 2)
@@ -368,13 +368,13 @@
 
     away, kept = attended[:split], attended[split:]
     away = [plan.to_part(v, i) if i else v for i, v in enumerate(away)]
-    rest = far or near
-    begun = project(plan, near, away[:1], out_weight) if far else None
-    away = project(plan, rest, [away[i] for i in rest], out_weight, begun, True)
+    near, rest = list(range(split // 2)), list(range(split // 2, split))
+    begun = project(plan, near, away[: len(near)], out_weight) if near else None
+    away = project(plan, rest, away[len(near) :], out_weight, begun, True)
     away = [plan.to_tensor(v, i + 1) for i, v in enumerate(away)]
     kept = [plan.to_part(v, i) if i else v for i, v in enumerate(kept)]
-    begun = project(plan, near, kept[:1], out_weight) if far else None
-    sums = [project(plan, rest, [kept[i] for i in rest], out_weight, begun), *away]
+    begun = project(plan, near, kept[: len(near)], out_weight) if near else None
+    sums = [project(plan, rest, kept[len(near) :], out_weight, begun), *away]
     velocity, moved = head(plan, delta, sums, shared, latents)
     advanced = [plan.to_next_group(moved, i) for i in range(tensors)]
     velocities = [velocity] + [plan.to_tensor(velocity, i) for i in range(1, tensors)]

time: 77.2 us -> 76.3 us (0.988)
  waiting for transfers between devices: 25.1 us -> 23.8 us
    ppermute x9, waiting for transfers between devices: 10.5 us -> 9.67 us  [to_part(): return lax.ppermute(value, 'section', pairs)]
where the time goes in v5:
time: 76.3 us; the launch traced here: 75.9 us
  starting transfers between devices  31.6 us (41%)
  waiting for transfers between devices  23.8 us (31%)
  Pallas kernels  10.7 us (14%)
  local copies, waits for them, and re-layouts  8.83 us (12%)
  between operations  0.87 us (1%)
    ppermute x9, starting transfers between devices, to_part(): return lax.ppermute(value, 'section', pairs)  18.1 us
    ppermute x12, waiting for transfers between devices, to_member(): lax.ppermute(value, 'section', [(s, s ^ step) for s in range(self.section...  9.78 us
    ppermute x9, waiting for transfers between devices, to_part(): return lax.ppermute(value, 'section', pairs)  9.67 us
    ppermute x12, starting transfers between devices, to_member(): lax.ppermute(value, 'section', [(s, s ^ step) for s in range(self.section...  6.25 us
    unnamed x22, local copies, waits for them, and re-layouts  5.89 us
    pallas_call x2, Pallas kernels, attend(): pl.pallas_call(functools.partial(attend_kernel, plan, blocks, bool(state)...  5.08 us
    ppermute x2, waiting for transfers between devices, to_next_group(): return lax.ppermute(value, ('section', 'tensor'), pairs)  4.37 us
    ppermute x2, starting transfers between devices, to_next_group(): return lax.ppermute(value, ('section', 'tensor'), pairs)  3.95 us
  transfers between devices with their start and end apart: 26, of which 12 were waited for; matrix products, arithmetic and copies ran while one was open for 1% of the time, Pallas kernels for 10%

profile of v5, /device:TPU:0, one launch (start us, length us, event | category | flops | bytes accessed | tf_op | source)
XLA Modules:
  0.0 75.9 jit_solution(10411814986998631796)
XLA Ops:
  0.7 1.0 %constant_dynamic-slice_fusion.2 = (bf16[128,384]{1,0:T(8,128)(2,1)S(1)}, bf16[128,384]{1,0:T(8,128)(2,1)S(1)}, bf16[128,384]{1,0:T(8,128)(2,1)S(1)}) fusion(bf16[128,1536]{1,0:T(8,128)(2,1)} %refs_0_.1, s32[]{:T(128)S(6)} %select_n.24, s32[]{:T(128)S(6)} %select_n.22, s32[]{:T(128)S(6)} %select_n.23), kind=kLoop, calls=%fused_computation.5 | loop fusion | bytes 589836 | tf_op jit(solution)/shard_map/dynamic_slice | solution.py:78
  1.7 1.1 %constant_dynamic-slice_fusion = (bf16[128,384]{1,0:T(8,128)(2,1)S(1)}, bf16[128,384]{1,0:T(8,128)(2,1)S(1)}, bf16[128,384]{1,0:T(8,128)(2,1)S(1)}, bf16[128,384]{1,0:T(8,128)(2,1)S(1)}, bf16[128,384]{1,0:T(8,128)(2,1)S(1)}) fusion(bf16[128,1536]{1,0:T(8,128)(2,1)} %refs_2_.5, s32[]{:T(128)S(6)} %select_n.24, s32[]{:T(128)S(6)} %select_n.23, ...), kind=kLoop, calls=%fused_computation.3 | loop fusion | bytes 983052 | tf_op jit(solution)/shard_map/dynamic_slice | solution.py:78
  2.9 4.1 %collective-permute-start.2 = (bf16[384,384]{1,0:T(8,128)(2,1)S(1)}, bf16[384,384]{1,0:T(8,128)(2,1)S(1)}, u32[]{:S(2)}, u32[]{:S(2)}) collective-permute-start(bf16[384,384]{1,0:T(8,128)(2,1)S(1)} %pad_maximum_fusion.1), channel_id=1, source_target_pairs={{0,16},{2,18},{4,20},{6,22},{8,24},{10,26},{12,28},{14,30},{16,0},... | collective-permute-start | bytes 884744 | tf_op jit(solution)/shard_map/ppermute | solution.py:51
  7.0 1.6 %collective-permute-start = (bf16[256,384]{1,0:T(8,128)(2,1)S(1)}, bf16[256,384]{1,0:T(8,128)(2,1)S(1)}, u32[]{:S(2)}, u32[]{:S(2)}) collective-permute-start(bf16[256,384]{1,0:T(8,128)(2,1)S(1)} %pad_maximum_fusion.2.refs_4_), channel_id=1, source_target_pairs={{0,4},{2,6},{4,0},{6,2},{8,12},{10,14},{12,8},{14,10},{16,20},{18,... | collective-permute-start | bytes 589832 | tf_op jit(solution)/shard_map/ppermute | solution.py:54
  8.6 1.6 %collective-permute-start.1 = (bf16[384,384]{1,0:T(8,128)(2,1)S(1)}, bf16[384,384]{1,0:T(8,128)(2,1)S(1)}, u32[]{:S(2)}, u32[]{:S(2)}) collective-permute-start(bf16[384,384]{1,0:T(8,128)(2,1)S(1)} %pad_maximum_fusion), channel_id=1, source_target_pairs={{0,8},{2,10},{4,12},{6,14},{8,0},{10,2},{12,4},{14,6},{16,24},{18,... | collective-permute-start | bytes 884744 | tf_op jit(solution)/shard_map/ppermute | solution.py:51
  10.3 0.7 broadcast_in_dim.3.gain
  11.0 2.5 %collective-permute-done.refs_3_.refs_0_.refs_2_.refs_12_ = bf16[256,384]{1,0:T(8,128)(2,1)S(1)} collective-permute-done((bf16[256,384]{1,0:T(8,128)(2,1)S(1)}, bf16[256,384]{1,0:T(8,128)(2,1)S(1)}, u32[]{:S(2)}, u32[]{:S(2)}) %collective-permute-start) | collective-permute-done | bytes 196640 | tf_op jit(solution)/shard_map/ppermute | solution.py:54
  13.4 1.0 %copy-done = bf16[128,1536]{1,0:T(8,128)(2,1)S(1)} copy-done((bf16[128,1536]{1,0:T(8,128)(2,1)S(1)}, bf16[128,1536]{1,0:T(8,128)(2,1)}, u32[]{:S(2)}) %copy-start) | copy-done | bytes 393240
  14.4 1.0 %copy-done.1 = bf16[128,1536]{1,0:T(8,128)(2,1)S(1)} copy-done((bf16[128,1536]{1,0:T(8,128)(2,1)S(1)}, bf16[128,1536]{1,0:T(8,128)(2,1)}, u32[]{:S(2)}) %copy-start.1) | copy-done | bytes 393240
  15.4 1.0 %copy-done.2 = bf16[128,1536]{1,0:T(8,128)(2,1)S(1)} copy-done((bf16[128,1536]{1,0:T(8,128)(2,1)S(1)}, bf16[128,1536]{1,0:T(8,128)(2,1)}, u32[]{:S(2)}) %copy-start.2) | copy-done | bytes 393240
  16.5 0.0 copy-start.3
  16.5 0.9 %copy-done.3 = bf16[1536,64]{0,1:T(8,128)(2,1)S(1)} copy-done((bf16[1536,64]{0,1:T(8,128)(2,1)S(1)}, bf16[1536,64]{0,1:T(8,128)(2,1)}, u32[]{:S(2)}) %copy-start.3) | copy-done | bytes 196632
  17.4 0.7 copy-done.5
  18.1 0.7 copy-done.6
  18.7 0.7 copy-done.7
  19.4 0.7 shard_map.114
  20.0 0.4 collective-permute-done.2.refs_1_.refs_2_.refs_5_
  20.4 3.5 %collective-permute-start.3 = (bf16[384,384]{1,0:T(8,128)(2,1)S(1)}, bf16[384,384]{1,0:T(8,128)(2,1)S(1)}, u32[]{:S(2)}, u32[]{:S(2)}) collective-permute-start(bf16[384,384]{1,0:T(8,128)(2,1)S(1)} %shard_map.115), channel_id=1, source_target_pairs={{0,24},{2,26},{4,28},{6,30},{8,16},{10,18},{12,20},{14,22},{16,8},... | collective-permute-start | bytes 884744 | tf_op jit(solution)/shard_map/ppermute | solution.py:51
  24.0 1.5 %collective-permute-start.9 = (bf16[112,1536]{1,0:T(8,128)(2,1)S(1)}, bf16[112,1536]{1,0:T(8,128)(2,1)S(1)}, u32[]{:S(2)}, u32[]{:S(2)}) collective-permute-start(bf16[112,1536]{1,0:T(8,128)(2,1)S(1)} %get-tuple-element.26.refs_2_), channel_id=1, source_target_pairs={{0,1},{1,0},{2,3},{3,2},{4,5},{5,4},{6,7},{7,6},{8,9},{9,8},{10,11... | collective-permute-start | bytes 1032200 | tf_op jit(solution)/shard_map/ppermute | solution.py:57
  25.5 0.0 collective-permute-done.1.refs_1_.refs_4_
  25.5 1.5 %collective-permute-start.7 = (bf16[256,384]{1,0:T(8,128)(2,1)S(1)}, bf16[256,384]{1,0:T(8,128)(2,1)S(1)}, u32[]{:S(2)}, u32[]{:S(2)}) collective-permute-start(bf16[256,384]{1,0:T(8,128)(2,1)S(1)} %slice.12.refs_6_), channel_id=1, source_target_pairs={{0,4},{2,6},{4,0},{6,2},{8,12},{10,14},{12,8},{14,10},{16,20},{18,... | collective-permute-start | bytes 589832 | tf_op jit(solution)/shard_map/ppermute | solution.py:54
  27.0 0.7 collective-permute-start.8
  27.7 0.0 collective-permute-start.4
  27.7 3.5 %collective-permute-done.3.refs_3_.refs_6_ = bf16[384,384]{1,0:T(8,128)(2,1)S(1)} collective-permute-done((bf16[384,384]{1,0:T(8,128)(2,1)S(1)}, bf16[384,384]{1,0:T(8,128)(2,1)S(1)}, u32[]{:S(2)}, u32[]{:S(2)}) %collective-permute-start.3) | collective-permute-done | bytes 294944 | tf_op jit(solution)/shard_map/ppermute | solution.py:51
  31.2 0.0 collective-permute-start.11
  31.2 2.2 %collective-permute-done.7.refs_1_.refs_14_ = bf16[256,384]{1,0:T(8,128)(2,1)S(1)} collective-permute-done((bf16[256,384]{1,0:T(8,128)(2,1)S(1)}, bf16[256,384]{1,0:T(8,128)(2,1)S(1)}, u32[]{:S(2)}, u32[]{:S(2)}) %collective-permute-start.7) | collective-permute-done | bytes 196640 | tf_op jit(solution)/shard_map/ppermute | solution.py:54
  33.4 2.6 %collective-permute-done.8.refs_2_.refs_16_ = bf16[256,384]{1,0:T(8,128)(2,1)S(1)} collective-permute-done((bf16[256,384]{1,0:T(8,128)(2,1)S(1)}, bf16[256,384]{1,0:T(8,128)(2,1)S(1)}, u32[]{:S(2)}, u32[]{:S(2)}) %collective-permute-start.8) | collective-permute-done | bytes 196640 | tf_op jit(solution)/shard_map/ppermute | solution.py:54
  36.0 0.5 collective-permute-start.12
  36.5 0.0 collective-permute-done.4.refs_5_
  36.5 0.1 collective-permute-start.13
  36.6 0.0 collective-permute-done.11.refs_13_
  36.6 0.4 collective-permute-start.10
  37.0 0.0 collective-permute-done.5.refs_7_
  37.0 1.5 %collective-permute-start.14 = (bf16[256,384]{1,0:T(8,128)(2,1)S(1)}, bf16[256,384]{1,0:T(8,128)(2,1)S(1)}, u32[]{:S(2)}, u32[]{:S(2)}) collective-permute-start(bf16[256,384]{1,0:T(8,128)(2,1)S(1)} %shard_map.117.refs_10_), channel_id=1, source_target_pairs={{0,4},{2,6},{4,0},{6,2},{8,12},{10,14},{12,8},{14,10},{16,20},{18,... | collective-permute-start | bytes 589832 | tf_op jit(solution)/shard_map/ppermute | solution.py:54
  38.5 0.0 collective-permute-done.6.refs_9_
  38.5 0.0 collective-permute-done.12.refs_15_
  38.5 0.0 collective-permute-done.13.refs_17_
  38.5 0.0 slice-start
  38.5 0.0 slice-start.2
  38.5 4.2 %shard_map.118 = (f32[3,512,128]{2,1,0:T(8,128)S(1)}, f32[3,512,128]{2,1,0:T(8,128)S(1)}, f32[3,512,128]{2,1,0:T(8,128)S(1)}) custom-call(f32[32,128]{1,0:T(8,128)S(1)} %get-tuple-element.24.refs_3_.bias, bf16[128,384]{1,0:T(8,128)(2,1)S(1)} %get-tuple-element.25.refs_0_.refs_3_, bf16[384,384]{1,0:T(8,128)(2,1)S(1)} %collective-permute-done.1.refs_1_.refs_4_, ...), custom_call_target="tpu_custom_call" | custom-call | flops 5637144576 | tf_op jit(solution)/shard_map/pallas_call | solution.py:215
  42.8 1.1 %collective-permute-done.14.refs_0_ = bf16[256,384]{1,0:T(8,128)(2,1)S(1)} collective-permute-done((bf16[256,384]{1,0:T(8,128)(2,1)S(1)}, bf16[256,384]{1,0:T(8,128)(2,1)S(1)}, u32[]{:S(2)}, u32[]{:S(2)}) %collective-permute-start.14) | collective-permute-done | bytes 196640 | tf_op jit(solution)/shard_map/ppermute | solution.py:54
  43.9 0.0 collective-permute-start.15
  43.9 1.4 %collective-permute-done.15.refs_8_ = bf16[256,384]{1,0:T(8,128)(2,1)S(1)} collective-permute-done((bf16[256,384]{1,0:T(8,128)(2,1)S(1)}, bf16[256,384]{1,0:T(8,128)(2,1)S(1)}, u32[]{:S(2)}, u32[]{:S(2)}) %collective-permute-start.15) | collective-permute-done | bytes 196640 | tf_op jit(solution)/shard_map/ppermute | solution.py:54
  45.3 0.9 %shard_map.120 = (bf16[64,384]{1,0:T(8,128)(2,1)S(1)}, bf16[64,384]{1,0:T(8,128)(2,1)S(1)}, bf16[64,384]{1,0:T(8,128)(2,1)S(1)}, bf16[64,384]{1,0:T(8,128)(2,1)S...) custom-call(f32[32,128]{1,0:T(8,128)S(1)} %get-tuple-element.24.refs, ...), custom_call_target="tpu_custom_call" | custom-call | flops 805306368 | tf_op jit(solution)/shard_map/pallas_call | solution.py:215
  46.2 1.4 %collective-permute-start.21 = (bf16[64,384]{1,0:T(8,128)(2,1)S(1)}, bf16[64,384]{1,0:T(8,128)(2,1)S(1)}, u32[]{:S(2)}, u32[]{:S(2)}) collective-permute-start(bf16[64,384]{1,0:T(8,128)(2,1)S(1)} %get-tuple-element.37), channel_id=1, source_target_pairs={{0,8},{2,10},{4,12},{6,14},{8,0},{10,2},{12,4},{14,6},{16,24},{18,... | collective-permute-start | bytes 147464 | tf_op jit(solution)/shard_map/ppermute | solution.py:51
  47.6 3.1 %collective-permute-start.20 = (bf16[64,384]{1,0:T(8,128)(2,1)S(1)}, bf16[64,384]{1,0:T(8,128)(2,1)S(1)}, u32[]{:S(2)}, u32[]{:S(2)}) collective-permute-start(bf16[64,384]{1,0:T(8,128)(2,1)S(1)} %get-tuple-element.35), channel_id=1, source_target_pairs={{0,24},{2,26},{4,28},{6,30},{8,16},{10,18},{12,20},{14,22},{16,8},... | collective-permute-start | bytes 147464 | tf_op jit(solution)/shard_map/ppermute | solution.py:51
  50.7 1.0 %shard_map.123.refs_3_ = f32[64,3072]{1,0:T(8,128)S(1)} custom-call(bf16[64,384]{1,0:T(8,128)(2,1)S(1)} %get-tuple-element.36.refs_0_, bf16[64,384]{1,0:T(8,128)(2,1)S(1)} %collective-permute-done.21.refs_1_, bf16[1536,3072]{1,0:T(8,128)(2,1)S(1)} %bitcast.2), custom_call_target="tpu_custom_call" | custom-call | tf_op jit(solution)/shard_map/pallas_call | solution.py:251
  51.7 2.8 %collective-permute-done.19.refs_0_ = bf16[64,384]{1,0:T(8,128)(2,1)S(1)} collective-permute-done((bf16[64,384]{1,0:T(8,128)(2,1)S(1)}, bf16[64,384]{1,0:T(8,128)(2,1)S(1)}, u32[]{:S(2)}, u32[]{:S(2)}) %collective-permute-start.19) | collective-permute-done | bytes 49184 | tf_op jit(solution)/shard_map/ppermute | solution.py:51
  54.5 1.0 %shard_map.124 = bf16[64,3072]{1,0:T(8,128)(2,1)S(1)} custom-call(bf16[64,384]{1,0:T(8,128)(2,1)S(1)} %collective-permute-done.19.refs_0_, bf16[64,384]{1,0:T(8,128)(2,1)S(1)} %collective-permute-done.20.refs_1_, bf16[1536,3072]{1,0:T(8,128)(2,1)S(1)} %bitcast.2, f32[64,3072]{1,0:T(8,128)S(1)} %shard_map.123.refs_3_), custom_call_target="tpu_custom_call" | custom-call | tf_op jit(solution)/shard_map/pallas_call | solution.py:251
  55.4 1.3 %collective-permute-start.22 = (bf16[64,3072]{1,0:T(8,128)(2,1)S(1)}, bf16[64,3072]{1,0:T(8,128)(2,1)S(1)}, u32[]{:S(2)}, u32[]{:S(2)}) collective-permute-start(bf16[64,3072]{1,0:T(8,128)(2,1)S(1)} %shard_map.124), channel_id=1, source_target_pairs={{0,1},{1,0},{2,3},{3,2},{4,5},{5,4},{6,7},{7,6},{8,9},{9,8},{10,11... | collective-permute-start | bytes 1179656 | tf_op jit(solution)/shard_map/ppermute | solution.py:57
  56.7 1.4 %collective-permute-start.18 = (bf16[64,384]{1,0:T(8,128)(2,1)S(1)}, bf16[64,384]{1,0:T(8,128)(2,1)S(1)}, u32[]{:S(2)}, u32[]{:S(2)}) collective-permute-start(bf16[64,384]{1,0:T(8,128)(2,1)S(1)} %get-tuple-element.33), channel_id=1, source_target_pairs={{0,8},{2,10},{4,12},{6,14},{8,0},{10,2},{12,4},{14,6},{16,24},{18,... | collective-permute-start | bytes 147464 | tf_op jit(solution)/shard_map/ppermute | solution.py:51
  58.1 1.0 %collective-permute-start.16 = (bf16[64,384]{1,0:T(8,128)(2,1)S(1)}, bf16[64,384]{1,0:T(8,128)(2,1)S(1)}, u32[]{:S(2)}, u32[]{:S(2)}) collective-permute-start(bf16[64,384]{1,0:T(8,128)(2,1)S(1)} %get-tuple-element.30), channel_id=1, source_target_pairs={{0,16},{2,18},{4,20},{6,22},{8,24},{10,26},{12,28},{14,30},{16,0},... | collective-permute-start | bytes 147464 | tf_op jit(solution)/shard_map/ppermute | solution.py:51
  59.1 2.0 %collective-permute-start.17 = (bf16[64,384]{1,0:T(8,128)(2,1)S(1)}, bf16[64,384]{1,0:T(8,128)(2,1)S(1)}, u32[]{:S(2)}, u32[]{:S(2)}) collective-permute-start(bf16[64,384]{1,0:T(8,128)(2,1)S(1)} %get-tuple-element.31), channel_id=1, source_target_pairs={{0,24},{2,26},{4,28},{6,30},{8,16},{10,18},{12,20},{14,22},{16,8},... | collective-permute-start | bytes 147464 | tf_op jit(solution)/shard_map/ppermute | solution.py:51
  61.1 1.0 %shard_map.121.refs_3_ = f32[64,3072]{1,0:T(8,128)S(1)} custom-call(bf16[64,384]{1,0:T(8,128)(2,1)S(1)} %get-tuple-element.32.refs_0_, bf16[64,384]{1,0:T(8,128)(2,1)S(1)} %collective-permute-done.18.refs_1_, bf16[1536,3072]{1,0:T(8,128)(2,1)S(1)} %bitcast.2), custom_call_target="tpu_custom_call" | custom-call | tf_op jit(solution)/shard_map/pallas_call | solution.py:251
  62.1 1.8 %collective-permute-done.16.refs_0_ = bf16[64,384]{1,0:T(8,128)(2,1)S(1)} collective-permute-done((bf16[64,384]{1,0:T(8,128)(2,1)S(1)}, bf16[64,384]{1,0:T(8,128)(2,1)S(1)}, u32[]{:S(2)}, u32[]{:S(2)}) %collective-permute-start.16) | collective-permute-done | bytes 49184 | tf_op jit(solution)/shard_map/ppermute | solution.py:51
  63.9 1.1 %collective-permute-done.17.refs_1_ = bf16[64,384]{1,0:T(8,128)(2,1)S(1)} collective-permute-done((bf16[64,384]{1,0:T(8,128)(2,1)S(1)}, bf16[64,384]{1,0:T(8,128)(2,1)S(1)}, u32[]{:S(2)}, u32[]{:S(2)}) %collective-permute-start.17) | collective-permute-done | bytes 49184 | tf_op jit(solution)/shard_map/ppermute | solution.py:51
  65.0 1.0 %shard_map.122.refs_0_ = f32[64,3072]{1,0:T(8,128)S(1)} custom-call(bf16[64,384]{1,0:T(8,128)(2,1)S(1)} %collective-permute-done.16.refs_0_, bf16[64,384]{1,0:T(8,128)(2,1)S(1)} %collective-permute-done.17.refs_1_, bf16[1536,3072]{1,0:T(8,128)(2,1)S(1)} %bitcast.2, f32[64,3072]{1,0:T(8,128)S(1)} %shard_map.121.refs_3_), custom_call_target="tpu_custom_call" | custom-call | tf_op jit(solution)/shard_map/pallas_call | solution.py:251
  66.0 0.4 shard_map.125
  66.4 1.5 %collective-permute-start.23 = (f32[32,128]{1,0:T(8,128)S(1)}, f32[32,128]{1,0:T(8,128)S(1)}, u32[]{:S(2)}, u32[]{:S(2)}) collective-permute-start(f32[32,128]{1,0:T(8,128)S(1)} %get-tuple-element.38), channel_id=1, source_target_pairs={{0,4},{1,5},{2,6},{3,7},{4,8},{5,9},{6,10},{7,11},{8,12},{9,13},{1... | collective-permute-start | bytes 49160 | tf_op jit(solution)/shard_map/ppermute | solution.py:65
  67.9 2.4 %collective-permute-start.24 = (f32[32,128]{1,0:T(8,128)S(1)}, f32[32,128]{1,0:T(8,128)S(1)}, u32[]{:S(2)}, u32[]{:S(2)}) collective-permute-start(f32[32,128]{1,0:T(8,128)S(1)} %get-tuple-element.38), channel_id=1, source_target_pairs={{0,5},{1,4},{2,7},{3,6},{4,9},{5,8},{6,11},{7,10},{8,13},{9,12},{1... | collective-permute-start | bytes 49160 | tf_op jit(solution)/shard_map/ppermute | solution.py:65
  70.4 0.5 collective-permute-start.25
  70.9 2.0 %collective-permute-done.23.refs_0_ = f32[32,128]{1,0:T(8,128)S(1)} collective-permute-done((f32[32,128]{1,0:T(8,128)S(1)}, f32[32,128]{1,0:T(8,128)S(1)}, u32[]{:S(2)}, u32[]{:S(2)}) %collective-permute-start.23) | collective-permute-done | bytes 16416 | tf_op jit(solution)/shard_map/ppermute | solution.py:65
  72.9 2.4 %collective-permute-done.24.refs_1_ = f32[32,128]{1,0:T(8,128)S(1)} collective-permute-done((f32[32,128]{1,0:T(8,128)S(1)}, f32[32,128]{1,0:T(8,128)S(1)}, u32[]{:S(2)}, u32[]{:S(2)}) %collective-permute-start.24) | collective-permute-done | bytes 16416 | tf_op jit(solution)/shard_map/ppermute | solution.py:65
  75.3 0.6 shard_map.126
  (34 shorter events, 0.2 us)
Async XLA Ops:
  2.9 17.5 %collective-permute-start.2 = (bf16[384,384]{1,0:T(8,128)(2,1)S(1)}, bf16[384,384]{1,0:T(8,128)(2,1)S(1)}, u32[]{:S(2)}, u32[]{:S(2)}) collective-permute-start(bf16[384,384]{1,0:T(8,128)(2,1)S(1)} %pad_maximum_fusion.1), channel_id=1, source_target_pairs={{0,16},{2,18},{4,20},{6,22},{8,24},{10,26},{12,28},{14,30},{16,0},... | collective-permute-start | bytes 884744 | tf_op jit(solution)/shard_map/ppermute | solution.py:51
  7.0 6.4 %collective-permute-start = (bf16[256,384]{1,0:T(8,128)(2,1)S(1)}, bf16[256,384]{1,0:T(8,128)(2,1)S(1)}, u32[]{:S(2)}, u32[]{:S(2)}) collective-permute-start(bf16[256,384]{1,0:T(8,128)(2,1)S(1)} %pad_maximum_fusion.2.refs_4_), channel_id=1, source_target_pairs={{0,4},{2,6},{4,0},{6,2},{8,12},{10,14},{12,8},{14,10},{16,20},{18,... | collective-permute-start | bytes 589832 | tf_op jit(solution)/shard_map/ppermute | solution.py:54
  8.6 16.8 %collective-permute-start.1 = (bf16[384,384]{1,0:T(8,128)(2,1)S(1)}, bf16[384,384]{1,0:T(8,128)(2,1)S(1)}, u32[]{:S(2)}, u32[]{:S(2)}) collective-permute-start(bf16[384,384]{1,0:T(8,128)(2,1)S(1)} %pad_maximum_fusion), channel_id=1, source_target_pairs={{0,8},{2,10},{4,12},{6,14},{8,0},{10,2},{12,4},{14,6},{16,24},{18,... | collective-permute-start | bytes 884744 | tf_op jit(solution)/shard_map/ppermute | solution.py:51
  13.4 1.0 %copy-start = (bf16[128,1536]{1,0:T(8,128)(2,1)S(1)}, bf16[128,1536]{1,0:T(8,128)(2,1)}, u32[]{:S(2)}) copy-start(bf16[128,1536]{1,0:T(8,128)(2,1)} %refs_1_.1) | copy-start | bytes 1179652
  14.4 1.0 %copy-start.1 = (bf16[128,1536]{1,0:T(8,128)(2,1)S(1)}, bf16[128,1536]{1,0:T(8,128)(2,1)}, u32[]{:S(2)}) copy-start(bf16[128,1536]{1,0:T(8,128)(2,1)} %refs_0_.1) | copy-start | bytes 1179652
  15.4 1.0 %copy-start.2 = (bf16[128,1536]{1,0:T(8,128)(2,1)S(1)}, bf16[128,1536]{1,0:T(8,128)(2,1)}, u32[]{:S(2)}) copy-start(bf16[128,1536]{1,0:T(8,128)(2,1)} %refs_2_.5) | copy-start | bytes 1179652
  16.5 0.9 %copy-start.3 = (bf16[1536,64]{0,1:T(8,128)(2,1)S(1)}, bf16[1536,64]{0,1:T(8,128)(2,1)}, u32[]{:S(2)}) copy-start(bf16[1536,64]{0,1:T(8,128)(2,1)} %param.16) | copy-start | bytes 589828
  17.4 0.7 copy-start.5
  18.1 0.7 copy-start.6
  18.7 0.7 copy-start.7
  20.4 10.8 %collective-permute-start.3 = (bf16[384,384]{1,0:T(8,128)(2,1)S(1)}, bf16[384,384]{1,0:T(8,128)(2,1)S(1)}, u32[]{:S(2)}, u32[]{:S(2)}) collective-permute-start(bf16[384,384]{1,0:T(8,128)(2,1)S(1)} %shard_map.115), channel_id=1, source_target_pairs={{0,24},{2,26},{4,28},{6,30},{8,16},{10,18},{12,20},{14,22},{16,8},... | collective-permute-start | bytes 884744 | tf_op jit(solution)/shard_map/ppermute | solution.py:51
  24.0 12.0 %collective-permute-start.9 = (bf16[112,1536]{1,0:T(8,128)(2,1)S(1)}, bf16[112,1536]{1,0:T(8,128)(2,1)S(1)}, u32[]{:S(2)}, u32[]{:S(2)}) collective-permute-start(bf16[112,1536]{1,0:T(8,128)(2,1)S(1)} %get-tuple-element.26.refs_2_), channel_id=1, source_target_pairs={{0,1},{1,0},{2,3},{3,2},{4,5},{5,4},{6,7},{7,6},{8,9},{9,8},{10,11... | collective-permute-start | bytes 1032200 | tf_op jit(solution)/shard_map/ppermute | solution.py:57
  25.5 7.9 %collective-permute-start.7 = (bf16[256,384]{1,0:T(8,128)(2,1)S(1)}, bf16[256,384]{1,0:T(8,128)(2,1)S(1)}, u32[]{:S(2)}, u32[]{:S(2)}) collective-permute-start(bf16[256,384]{1,0:T(8,128)(2,1)S(1)} %slice.12.refs_6_), channel_id=1, source_target_pairs={{0,4},{2,6},{4,0},{6,2},{8,12},{10,14},{12,8},{14,10},{16,20},{18,... | collective-permute-start | bytes 589832 | tf_op jit(solution)/shard_map/ppermute | solution.py:54
  27.0 9.0 %collective-permute-start.8 = (bf16[256,384]{1,0:T(8,128)(2,1)S(1)}, bf16[256,384]{1,0:T(8,128)(2,1)S(1)}, u32[]{:S(2)}, u32[]{:S(2)}) collective-permute-start(bf16[256,384]{1,0:T(8,128)(2,1)S(1)} %shard_map.116.refs_8_), channel_id=1, source_target_pairs={{0,4},{2,6},{4,0},{6,2},{8,12},{10,14},{12,8},{14,10},{16,20},{18,... | collective-permute-start | bytes 589832 | tf_op jit(solution)/shard_map/ppermute | solution.py:54
  27.7 8.8 %collective-permute-start.4 = (bf16[256,384]{1,0:T(8,128)(2,1)S(1)}, bf16[256,384]{1,0:T(8,128)(2,1)S(1)}, u32[]{:S(2)}, u32[]{:S(2)}) collective-permute-start(bf16[256,384]{1,0:T(8,128)(2,1)S(1)} %pad_maximum_fusion.2.refs_4_), channel_id=1, source_target_pairs={{0,2},{2,0},{4,6},{6,4},{8,10},{10,8},{12,14},{14,12},{16,18},{18,... | collective-permute-start | bytes 589832 | tf_op jit(solution)/shard_map/ppermute | solution.py:54
  31.2 5.4 %collective-permute-start.11 = (bf16[256,384]{1,0:T(8,128)(2,1)S(1)}, bf16[256,384]{1,0:T(8,128)(2,1)S(1)}, u32[]{:S(2)}, u32[]{:S(2)}) collective-permute-start(bf16[256,384]{1,0:T(8,128)(2,1)S(1)} %collective-permute-done.refs_3_.refs_0_.refs_2_.refs_12_), channel_id=1, source_target_pairs={{0,2},{2,0},{4,6},{6,4},{8,10},{10,8},{12,14},{14,12},{16,18},{18,... | collective-permute-start | bytes 589832 | tf_op jit(solution)/shard_map/ppermute | solution.py:54
  33.4 3.6 %collective-permute-start.5 = (bf16[256,384]{1,0:T(8,128)(2,1)S(1)}, bf16[256,384]{1,0:T(8,128)(2,1)S(1)}, u32[]{:S(2)}, u32[]{:S(2)}) collective-permute-start(bf16[256,384]{1,0:T(8,128)(2,1)S(1)} %slice.12.refs_6_), channel_id=1, source_target_pairs={{0,2},{2,0},{4,6},{6,4},{8,10},{10,8},{12,14},{14,12},{16,18},{18,... | collective-permute-start | bytes 589832 | tf_op jit(solution)/shard_map/ppermute | solution.py:54
  36.0 2.5 %collective-permute-start.6 = (bf16[256,384]{1,0:T(8,128)(2,1)S(1)}, bf16[256,384]{1,0:T(8,128)(2,1)S(1)}, u32[]{:S(2)}, u32[]{:S(2)}) collective-permute-start(bf16[256,384]{1,0:T(8,128)(2,1)S(1)} %shard_map.116.refs_8_), channel_id=1, source_target_pairs={{0,2},{2,0},{4,6},{6,4},{8,10},{10,8},{12,14},{14,12},{16,18},{18,... | collective-permute-start | bytes 589832 | tf_op jit(solution)/shard_map/ppermute | solution.py:54
  36.0 2.5 %collective-permute-start.12 = (bf16[256,384]{1,0:T(8,128)(2,1)S(1)}, bf16[256,384]{1,0:T(8,128)(2,1)S(1)}, u32[]{:S(2)}, u32[]{:S(2)}) collective-permute-start(bf16[256,384]{1,0:T(8,128)(2,1)S(1)} %collective-permute-done.7.refs_1_.refs_14_), channel_id=1, source_target_pairs={{0,2},{2,0},{4,6},{6,4},{8,10},{10,8},{12,14},{14,12},{16,18},{18,... | collective-permute-start | bytes 589832 | tf_op jit(solution)/shard_map/ppermute | solution.py:54
  36.5 2.0 %collective-permute-start.13 = (bf16[256,384]{1,0:T(8,128)(2,1)S(1)}, bf16[256,384]{1,0:T(8,128)(2,1)S(1)}, u32[]{:S(2)}, u32[]{:S(2)}) collective-permute-start(bf16[256,384]{1,0:T(8,128)(2,1)S(1)} %collective-permute-done.8.refs_2_.refs_16_), channel_id=1, source_target_pairs={{0,2},{2,0},{4,6},{6,4},{8,10},{10,8},{12,14},{14,12},{16,18},{18,... | collective-permute-start | bytes 589832 | tf_op jit(solution)/shard_map/ppermute | solution.py:54
  36.6 1.9 %collective-permute-start.10 = (bf16[256,384]{1,0:T(8,128)(2,1)S(1)}, bf16[256,384]{1,0:T(8,128)(2,1)S(1)}, u32[]{:S(2)}, u32[]{:S(2)}) collective-permute-start(bf16[256,384]{1,0:T(8,128)(2,1)S(1)} %shard_map.117.refs_10_), channel_id=1, source_target_pairs={{0,2},{2,0},{4,6},{6,4},{8,10},{10,8},{12,14},{14,12},{16,18},{18,... | collective-permute-start | bytes 589832 | tf_op jit(solution)/shard_map/ppermute | solution.py:54
  37.0 6.9 %collective-permute-start.14 = (bf16[256,384]{1,0:T(8,128)(2,1)S(1)}, bf16[256,384]{1,0:T(8,128)(2,1)S(1)}, u32[]{:S(2)}, u32[]{:S(2)}) collective-permute-start(bf16[256,384]{1,0:T(8,128)(2,1)S(1)} %shard_map.117.refs_10_), channel_id=1, source_target_pairs={{0,4},{2,6},{4,0},{6,2},{8,12},{10,14},{12,8},{14,10},{16,20},{18,... | collective-permute-start | bytes 589832 | tf_op jit(solution)/shard_map/ppermute | solution.py:54
  38.5 12.2 %slice-start = ((s8[9437184]{0:T(1024)(128)(4,1)}), s8[4194304]{0:T(1024)(128)(4,1)S(1)}, s32[]{:S(2)}) async-start(s8[9437184]{0:T(1024)(128)(4,1)} %bitcast.1), calls=%async_computation | async-start | bytes 8388608
  38.5 12.1 %slice-start.1 = ((s8[9437184]{0:T(1024)(128)(4,1)}), s8[4194304]{0:T(1024)(128)(4,1)S(1)}, s32[]{:S(2)}) async-start(s8[9437184]{0:T(1024)(128)(4,1)} %bitcast.1), calls=%async_computation.1 | async-start | bytes 8388608
  38.5 12.1 %slice-start.2 = ((s8[9437184]{0:T(1024)(128)(4,1)}), s8[1048576]{0:T(1024)(128)(4,1)S(1)}, s32[]{:S(2)}) async-start(s8[9437184]{0:T(1024)(128)(4,1)} %bitcast.1), calls=%async_computation.2 | async-start | bytes 2097152
  43.9 1.4 %collective-permute-start.15 = (bf16[256,384]{1,0:T(8,128)(2,1)S(1)}, bf16[256,384]{1,0:T(8,128)(2,1)S(1)}, u32[]{:S(2)}, u32[]{:S(2)}) collective-permute-start(bf16[256,384]{1,0:T(8,128)(2,1)S(1)} %shard_map.119.refs_7_), channel_id=1, source_target_pairs={{0,2},{2,0},{4,6},{6,4},{8,10},{10,8},{12,14},{14,12},{16,18},{18,... | collective-permute-start | bytes 589832 | tf_op jit(solution)/shard_map/ppermute | solution.py:54
  46.2 4.5 %collective-permute-start.21 = (bf16[64,384]{1,0:T(8,128)(2,1)S(1)}, bf16[64,384]{1,0:T(8,128)(2,1)S(1)}, u32[]{:S(2)}, u32[]{:S(2)}) collective-permute-start(bf16[64,384]{1,0:T(8,128)(2,1)S(1)} %get-tuple-element.37), channel_id=1, source_target_pairs={{0,8},{2,10},{4,12},{6,14},{8,0},{10,2},{12,4},{14,6},{16,24},{18,... | collective-permute-start | bytes 147464 | tf_op jit(solution)/shard_map/ppermute | solution.py:51
  47.6 6.9 %collective-permute-start.19 = (bf16[64,384]{1,0:T(8,128)(2,1)S(1)}, bf16[64,384]{1,0:T(8,128)(2,1)S(1)}, u32[]{:S(2)}, u32[]{:S(2)}) collective-permute-start(bf16[64,384]{1,0:T(8,128)(2,1)S(1)} %get-tuple-element.34), channel_id=1, source_target_pairs={{0,16},{2,18},{4,20},{6,22},{8,24},{10,26},{12,28},{14,30},{16,0},... | collective-permute-start | bytes 147464 | tf_op jit(solution)/shard_map/ppermute | solution.py:51
  47.6 6.9 %collective-permute-start.20 = (bf16[64,384]{1,0:T(8,128)(2,1)S(1)}, bf16[64,384]{1,0:T(8,128)(2,1)S(1)}, u32[]{:S(2)}, u32[]{:S(2)}) collective-permute-start(bf16[64,384]{1,0:T(8,128)(2,1)S(1)} %get-tuple-element.35), channel_id=1, source_target_pairs={{0,24},{2,26},{4,28},{6,30},{8,16},{10,18},{12,20},{14,22},{16,8},... | collective-permute-start | bytes 147464 | tf_op jit(solution)/shard_map/ppermute | solution.py:51
  55.4 10.5 %collective-permute-start.22 = (bf16[64,3072]{1,0:T(8,128)(2,1)S(1)}, bf16[64,3072]{1,0:T(8,128)(2,1)S(1)}, u32[]{:S(2)}, u32[]{:S(2)}) collective-permute-start(bf16[64,3072]{1,0:T(8,128)(2,1)S(1)} %shard_map.124), channel_id=1, source_target_pairs={{0,1},{1,0},{2,3},{3,2},{4,5},{5,4},{6,7},{7,6},{8,9},{9,8},{10,11... | collective-permute-start | bytes 1179656 | tf_op jit(solution)/shard_map/ppermute | solution.py:57
  56.7 4.4 %collective-permute-start.18 = (bf16[64,384]{1,0:T(8,128)(2,1)S(1)}, bf16[64,384]{1,0:T(8,128)(2,1)S(1)}, u32[]{:S(2)}, u32[]{:S(2)}) collective-permute-start(bf16[64,384]{1,0:T(8,128)(2,1)S(1)} %get-tuple-element.33), channel_id=1, source_target_pairs={{0,8},{2,10},{4,12},{6,14},{8,0},{10,2},{12,4},{14,6},{16,24},{18,... | collective-permute-start | bytes 147464 | tf_op jit(solution)/shard_map/ppermute | solution.py:51
  58.1 5.8 %collective-permute-start.16 = (bf16[64,384]{1,0:T(8,128)(2,1)S(1)}, bf16[64,384]{1,0:T(8,128)(2,1)S(1)}, u32[]{:S(2)}, u32[]{:S(2)}) collective-permute-start(bf16[64,384]{1,0:T(8,128)(2,1)S(1)} %get-tuple-element.30), channel_id=1, source_target_pairs={{0,16},{2,18},{4,20},{6,22},{8,24},{10,26},{12,28},{14,30},{16,0},... | collective-permute-start | bytes 147464 | tf_op jit(solution)/shard_map/ppermute | solution.py:51
  59.1 5.9 %collective-permute-start.17 = (bf16[64,384]{1,0:T(8,128)(2,1)S(1)}, bf16[64,384]{1,0:T(8,128)(2,1)S(1)}, u32[]{:S(2)}, u32[]{:S(2)}) collective-permute-start(bf16[64,384]{1,0:T(8,128)(2,1)S(1)} %get-tuple-element.31), channel_id=1, source_target_pairs={{0,24},{2,26},{4,28},{6,30},{8,16},{10,18},{12,20},{14,22},{16,8},... | collective-permute-start | bytes 147464 | tf_op jit(solution)/shard_map/ppermute | solution.py:51
  61.1 4.9 %copy-start.4 = (f32[64,128]{1,0:T(8,128)S(1)}, f32[64,128]{1,0:T(8,128)}, u32[]{:S(2)}) copy-start(f32[64,128]{1,0:T(8,128)} %refs_4_.1) | copy-start | bytes 98308
  66.4 6.5 %collective-permute-start.23 = (f32[32,128]{1,0:T(8,128)S(1)}, f32[32,128]{1,0:T(8,128)S(1)}, u32[]{:S(2)}, u32[]{:S(2)}) collective-permute-start(f32[32,128]{1,0:T(8,128)S(1)} %get-tuple-element.38), channel_id=1, source_target_pairs={{0,4},{1,5},{2,6},{3,7},{4,8},{5,9},{6,10},{7,11},{8,12},{9,13},{1... | collective-permute-start | bytes 49160 | tf_op jit(solution)/shard_map/ppermute | solution.py:65
  67.9 7.3 %collective-permute-start.24 = (f32[32,128]{1,0:T(8,128)S(1)}, f32[32,128]{1,0:T(8,128)S(1)}, u32[]{:S(2)}, u32[]{:S(2)}) collective-permute-start(f32[32,128]{1,0:T(8,128)S(1)} %get-tuple-element.38), channel_id=1, source_target_pairs={{0,5},{1,4},{2,7},{3,6},{4,9},{5,8},{6,11},{7,10},{8,13},{9,12},{1... | collective-permute-start | bytes 49160 | tf_op jit(solution)/shard_map/ppermute | solution.py:65
  70.4 4.9 %collective-permute-start.25 = (f32[32,128]{1,0:T(8,128)S(1)}, f32[32,128]{1,0:T(8,128)S(1)}, u32[]{:S(2)}, u32[]{:S(2)}) collective-permute-start(f32[32,128]{1,0:T(8,128)S(1)} %get-tuple-element.39.refs_2_), channel_id=1, source_target_pairs={{0,1},{1,0},{2,3},{3,2},{4,5},{5,4},{6,7},{7,6},{8,9},{9,8},{10,11... | collective-permute-start | bytes 49160 | tf_op jit(solution)/shard_map/ppermute | solution.py:57
